TPU v7x, 32 devices: a whole 2x2x4 slice. The times are simulated.
32 devices in a mesh: dp: 8 (over z, y), tensor: 4 (over x, core).
Axes of the slice: x: 2, y: 2, z: 4, core: 2. Of those that a mesh axis runs over, the one named last changes fastest.
Arguments:
- hidden_in: float32 [16384, 1024], P('dp'), may hold values from -6 to 6
- seg_ids: int32 [8, 2048], P('dp'), may hold values from 0 to 3, never falling along the last dimension, each value on 1 to 1024 neighbouring positions
- token_mask: int32 [8, 2048], P('dp'), may hold values 0 or 1
- out_grad: float32 [16384, 1024], P('dp'), may hold values from -6 to 6
- proj_qkv: float32 [1024, 4096], P('dp', 'tensor'), may hold values from -0.1875 to 0.1875
- proj_out: float32 [2048, 1024], P('tensor', 'dp'), may hold values from -0.5 to 0.5
- proj_gate_up: float32 [1024, 6144], P('dp', 'tensor'), may hold values from -0.1875 to 0.1875
- proj_down: float32 [3072, 1024], P('tensor', 'dp'), may hold values from -0.109375 to 0.109375
- gains: float32 [2304], replicated, may hold values from 0.5 to 1.5
- moment_qkv: float32 [1024, 4096], P('dp', 'tensor'), may hold values from -28 to 28
- moment_out: float32 [2048, 1024], P('tensor', 'dp'), may hold values from -28 to 28
- moment_gate_up: float32 [1024, 6144], P('dp', 'tensor'), may hold values from -28 to 28
- moment_down: float32 [3072, 1024], P('tensor', 'dp'), may hold values from -28 to 28
- error_qkv: float32 [8, 1024, 4096], P('dp', None, 'tensor'), may hold values from -80 to 80
- error_out: float32 [8, 2048, 1024], P('dp', 'tensor'), may hold values from -80 to 80
- error_gate_up: float32 [8, 1024, 6144], P('dp', None, 'tensor'), may hold values from -80 to 80
- error_down: float32 [8, 3072, 1024], P('dp', 'tensor'), may hold values from -80 to 80
- factor_qkv: float32 [4096, 8], P('tensor'), may hold values from -6 to 6
- factor_out: float32 [2048, 8], P('tensor'), may hold values from -6 to 6
- factor_gate_up: float32 [6144, 8], P('tensor'), may hold values from -6 to 6
- factor_down: float32 [3072, 8], P('tensor'), may hold values from -6 to 6
- gain_moment: float32 [2304], replicated, may hold values from -48 to 48
Outputs:
- layer_out: float32 [16384, 1024], P('dp')
- input_grad: float32 [16384, 1024], P('dp')
- new_proj_qkv: float32 [1024, 4096], P('dp', 'tensor')
- new_proj_out: float32 [2048, 1024], P('tensor', 'dp')
- new_proj_gate_up: float32 [1024, 6144], P('dp', 'tensor')
- new_proj_down: float32 [3072, 1024], P('tensor', 'dp')
- new_moment_qkv: float32 [1024, 4096], P('dp', 'tensor')
- new_moment_out: float32 [2048, 1024], P('tensor', 'dp')
- new_moment_gate_up: float32 [1024, 6144], P('dp', 'tensor')
- new_moment_down: float32 [3072, 1024], P('tensor', 'dp')
- new_error_qkv: float32 [8, 1024, 4096], P('dp', None, 'tensor')
- new_error_out: float32 [8, 2048, 1024], P('dp', 'tensor')
- new_error_gate_up: float32 [8, 1024, 6144], P('dp', None, 'tensor')
- new_error_down: float32 [8, 3072, 1024], P('dp', 'tensor')
- new_factor_qkv: float32 [4096, 8], P('tensor')
- new_factor_out: float32 [2048, 8], P('tensor')
- new_factor_gate_up: float32 [6144, 8], P('tensor')
- new_factor_down: float32 [3072, 8], P('tensor')
- new_gains: float32 [2304], replicated
- new_gain_moment: float32 [2304], replicated
Inputs may be any that keep to these rules, and one draw needn't show every extreme that they name: `seg_ids`: segment numbers never fall along a sequence; a document has at most 1024 tokens.
All inputs are finite; a program needn't handle non-finite values. No bound on the sum of `token_mask` on one device may be relied on, other than what follows from the above.
Results may differ from a plain program's by a relative error of at most 0.018.
The roundings to bfloat16 on the way count: a program that leaves them out, or rounds other values in their place, can miss the bound.
Values may be sent and summed in bfloat16 or wider, within the bound.
No kernel may reach another device: no remote copies, remote signals or barrier semaphores. Data moves between devices by JAX's collectives and lax.ppermute only.
A program may use at most 256 MiB of HBM per device.

v0:
```python
import math

import jax
import jax.numpy as jnp
from jax import lax
from jax.sharding import PartitionSpec as P

D = 1024
QUERY_HEADS = 16
KEY_VALUE_HEADS = 8
HEAD_SIZE = 128
FF = 3072


EPSILON = 1e-06
ROPE_THETA = 1000000.0
MASKED = -1000000000.0
MOMENTUM = 0.5
STEP_RATE = 0.003
GAIN_RATE = 0.02
EXACT_PRECISION = lax.Precision.HIGHEST


def rms_parts(values, gain_vec):
    factor = lax.rsqrt(jnp.mean(values * values, axis=-1, keepdims=True) + EPSILON)
    normal = values * factor
    return (normal * gain_vec, normal, factor)


def norm_back(grad_in, normal, factor, gain_vec):
    scaled = grad_in * gain_vec
    return factor * (scaled - normal * jnp.mean(scaled * normal, axis=-1, keepdims=True))


def rope_tables(sequence_length):
    position = jnp.arange(sequence_length, dtype=jnp.float32)
    inverse = ROPE_THETA ** (-(jnp.arange(HEAD_SIZE // 2, dtype=jnp.float32) * 2.0 / HEAD_SIZE))
    angles = position[:, None] * inverse[None, :]
    return (jnp.cos(angles)[:, None, :], jnp.sin(angles)[:, None, :])


def apply_rotary(values, cosine_table, sine_table):
    half_dim = values.shape[-1] // 2
    first_half = values[..., :half_dim]
    second_half = values[..., half_dim:]
    return jnp.concatenate(
        [
            first_half * cosine_table - second_half * sine_table,
            second_half * cosine_table + first_half * sine_table,
        ],
        axis=-1,
    )


def rotate_back(values, cosine_table, sine_table):
    half_dim = values.shape[-1] // 2
    first_half = values[..., :half_dim]
    second_half = values[..., half_dim:]
    return jnp.concatenate(
        [
            first_half * cosine_table + second_half * sine_table,
            second_half * cosine_table - first_half * sine_table,
        ],
        axis=-1,
    )


def allowed_block(seg_row, keep_row, begin_row, count_rows):
    row_ids = begin_row + jnp.arange(count_rows)
    col_ids = jnp.arange(seg_row.shape[0])
    seg_rows = lax.dynamic_slice_in_dim(seg_row, begin_row, count_rows)
    same_doc = seg_row[None, :] == seg_rows[:, None]
    causal = col_ids[None, :] <= row_ids[:, None]
    visible = (keep_row[None, :] == 1) | (col_ids[None, :] == row_ids[:, None])
    return same_doc & causal & visible


def block_scores(query_block, key_head_rows, seg_row, keep_row, begin_row, attention_scale):
    attention_scores = (
        jnp.einsum("cwbn,zwn->wbcz", query_block, key_head_rows, preferred_element_type=jnp.float32)
        * attention_scale
    )
    return jnp.where(
        allowed_block(seg_row, keep_row, begin_row, query_block.shape[0]), attention_scores, MASKED
    )


def attention_forward(
    query_rows, key_head_rows, value_head_rows, seg_row, keep_row, attention_scale, block_rows
):
    sequence_length = query_rows.shape[0]

    def block_forward(block_id):
        begin_row = block_id * block_rows
        query_block = lax.dynamic_slice_in_dim(query_rows, begin_row, block_rows, 0)
        attention_scores = block_scores(
            query_block, key_head_rows, seg_row, keep_row, begin_row, attention_scale
        )
        row_max = jnp.max(attention_scores, axis=-1, keepdims=True)
        expo_vals = jnp.exp(attention_scores - row_max)
        row_total = jnp.sum(expo_vals, axis=-1, keepdims=True)
        probabilities = expo_vals / row_total
        attention_output = jnp.einsum(
            "ynel,lyf->eynf",
            probabilities.astype(jnp.bfloat16),
            value_head_rows,
            preferred_element_type=jnp.float32,
        )
        return (attention_output, row_max + jnp.log(row_total))

    attention_output, log_total = lax.map(block_forward, jnp.arange(sequence_length // block_rows))
    return (attention_output.reshape(sequence_length, -1), log_total)


def attention_backward(
    query_rows,
    key_head_rows,
    value_head_rows,
    d_att,
    log_total,
    seg_row,
    keep_row,
    attention_scale,
    block_rows,
):
    sequence_length = query_rows.shape[0]

    def block_backward(running, block_id):
        key_acc, value_acc = running
        begin_row = block_id * block_rows
        query_block = lax.dynamic_slice_in_dim(query_rows, begin_row, block_rows, 0)
        gradient_block = lax.dynamic_slice_in_dim(d_att, begin_row, block_rows, 0)
        attention_scores = block_scores(
            query_block, key_head_rows, seg_row, keep_row, begin_row, attention_scale
        )
        probabilities = jnp.exp(attention_scores - log_total[block_id])
        d_probs = jnp.einsum(
            "cwbn,zwn->wbcz", gradient_block, value_head_rows, preferred_element_type=jnp.float32
        )
        score_gradient = (
            probabilities * (d_probs - jnp.sum(probabilities * d_probs, axis=-1, keepdims=True))
        ).astype(jnp.bfloat16)
        d_query = (
            jnp.einsum(
                "ynel,lyf->eynf", score_gradient, key_head_rows, preferred_element_type=jnp.float32
            )
            * attention_scale
        )
        key_acc = (
            key_acc
            + jnp.einsum(
                "vnyc,yvnp->cvp", score_gradient, query_block, preferred_element_type=jnp.float32
            )
            * attention_scale
        )
        value_acc = value_acc + jnp.einsum(
            "vnyc,yvnp->cvp",
            probabilities.astype(jnp.bfloat16),
            gradient_block,
            preferred_element_type=jnp.float32,
        )
        return ((key_acc, value_acc), d_query)

    zero_heads = jnp.zeros(key_head_rows.shape, jnp.float32)
    (d_keys, d_values), d_query = lax.scan(
        block_backward, (zero_heads, zero_heads), jnp.arange(sequence_length // block_rows)
    )
    return (d_query.reshape(query_rows.shape), d_keys, d_values)


def orthonormal(block):
    columns = []
    for column_id in range(block.shape[-1]):
        column = block[..., column_id]
        for finished in columns:
            column = column - jnp.sum(column * finished, axis=-1, keepdims=True) * finished
        column = column * lax.rsqrt(jnp.sum(column * column, axis=-1, keepdims=True) + 1e-12)
        columns.append(column)
    return jnp.stack(columns, axis=-1)


def compress(grad_in, error_in, factor_in, moment_in, weight_in, flipped):
    workers = lax.axis_size("dp")
    merged = grad_in + error_in[0]
    if flipped:
        p_local = jnp.einsum(
            "cd,cr->dr",
            merged,
            factor_in,
            precision=EXACT_PRECISION,
            preferred_element_type=jnp.float32,
        )
    else:
        p_local = jnp.dot(
            merged, factor_in, precision=EXACT_PRECISION, preferred_element_type=jnp.float32
        )
    p_hat = orthonormal(lax.psum(p_local, "dp") / workers)
    if flipped:
        q_local = jnp.dot(
            merged, p_hat, precision=EXACT_PRECISION, preferred_element_type=jnp.float32
        )
    else:
        q_local = jnp.einsum(
            "dc,dr->cr",
            merged,
            p_hat,
            precision=EXACT_PRECISION,
            preferred_element_type=jnp.float32,
        )
    q_new = lax.psum(q_local, "dp") / workers
    own_count = D // workers
    p_own = lax.dynamic_slice_in_dim(p_hat, lax.axis_index("dp") * own_count, own_count, 0)
    if flipped:
        approx = jnp.einsum(
            "cr,dr->cd", q_new, p_hat, precision=EXACT_PRECISION, preferred_element_type=jnp.float32
        )
        approx_own = jnp.einsum(
            "cr,dr->cd", q_new, p_own, precision=EXACT_PRECISION, preferred_element_type=jnp.float32
        )
    else:
        approx = jnp.einsum(
            "dr,cr->dc", p_hat, q_new, precision=EXACT_PRECISION, preferred_element_type=jnp.float32
        )
        approx_own = jnp.einsum(
            "dr,cr->dc", p_own, q_new, precision=EXACT_PRECISION, preferred_element_type=jnp.float32
        )
    new_moment = MOMENTUM * moment_in + approx_own
    new_weight = weight_in - STEP_RATE * new_moment
    return (new_weight, new_moment, (merged - approx)[None], q_new)


def tensor_total(partial_sum):
    return lax.psum(partial_sum, "tensor")


def local(
    hidden_in,
    seg_ids,
    token_mask,
    out_grad,
    proj_qkv,
    proj_out,
    proj_gate_up,
    proj_down,
    gains,
    moment_qkv,
    moment_out,
    moment_gate_up,
    moment_down,
    error_qkv,
    error_out,
    error_gate_up,
    error_down,
    factor_qkv,
    factor_out,
    factor_gate_up,
    factor_down,
    gain_moment,
):
    half_type = jnp.bfloat16
    tensor_worker_count = lax.axis_size("tensor")
    workers = lax.axis_size("dp")
    sequence_length = hidden_in.shape[0]
    q_heads = QUERY_HEADS // tensor_worker_count
    key_value_heads = KEY_VALUE_HEADS // tensor_worker_count
    heads_per_group = QUERY_HEADS // KEY_VALUE_HEADS
    query_columns = q_heads * HEAD_SIZE
    key_value_columns = key_value_heads * HEAD_SIZE
    ff_cols = FF // tensor_worker_count
    block_rows = min(sequence_length, 512)
    attention_scale = 1.0 / math.sqrt(HEAD_SIZE)
    qkv_b, gu_b, out_b, down_b = (
        lax.all_gather(proj_qkv.astype(half_type), "dp", axis=0, tiled=True),
        lax.all_gather(proj_gate_up.astype(half_type), "dp", axis=0, tiled=True),
        lax.all_gather(proj_out.astype(half_type), "dp", axis=1, tiled=True),
        lax.all_gather(proj_down.astype(half_type), "dp", axis=1, tiled=True),
    )
    seg_row = seg_ids[0]
    keep_row = token_mask[0]
    g_att = gains[:D]
    g_mlp = gains[D : 2 * D]
    query_gradient = gains[2 * D : 2 * D + HEAD_SIZE]
    g_key = gains[2 * D + HEAD_SIZE :]
    cosine_table, sine_table = rope_tables(sequence_length)
    h_att_f, unit_att, inv_att = rms_parts(hidden_in, g_att)
    h_att = h_att_f.astype(half_type)
    unrotated_projection = jnp.dot(h_att, qkv_b, preferred_element_type=jnp.float32)
    query_n, query_unit, query_inv = rms_parts(
        unrotated_projection[:, :query_columns].reshape(sequence_length, q_heads, HEAD_SIZE),
        query_gradient,
    )
    key_n, key_unit, key_inv = rms_parts(
        unrotated_projection[:, query_columns : query_columns + key_value_columns].reshape(
            sequence_length, key_value_heads, HEAD_SIZE
        ),
        g_key,
    )
    query_rows = (
        apply_rotary(query_n, cosine_table, sine_table)
        .astype(half_type)
        .reshape(sequence_length, key_value_heads, heads_per_group, HEAD_SIZE)
    )
    key_head_rows = apply_rotary(key_n, cosine_table, sine_table).astype(half_type)
    value_head_rows = (
        unrotated_projection[:, query_columns + key_value_columns :]
        .reshape(sequence_length, key_value_heads, HEAD_SIZE)
        .astype(half_type)
    )
    attended_f, log_total = attention_forward(
        query_rows, key_head_rows, value_head_rows, seg_row, keep_row, attention_scale, block_rows
    )
    attention_output = attended_f.astype(half_type)
    att_part = jnp.dot(attention_output, out_b, preferred_element_type=jnp.float32)
    resid_mid = hidden_in + tensor_total(att_part)
    h_mlp_f, unit_mlp, inv_mlp = rms_parts(resid_mid, g_mlp)
    h_mlp = h_mlp_f.astype(half_type)
    gate_up = jnp.dot(h_mlp, gu_b, preferred_element_type=jnp.float32)
    gate_in = gate_up[:, :ff_cols]
    up_in = gate_up[:, ff_cols:]
    gate_sig = jax.nn.sigmoid(gate_in)
    gate_silu = gate_in * gate_sig
    activ = (gate_silu * up_in).astype(half_type)
    mlp_part = jnp.dot(activ, down_b, preferred_element_type=jnp.float32)
    d_mlp = out_grad.astype(half_type)
    grad_down = jnp.dot(activ.T, d_mlp, preferred_element_type=jnp.float32)
    d_activ = jnp.dot(d_mlp, down_b.T, preferred_element_type=jnp.float32)
    d_gate = d_activ * up_in * gate_sig * (1.0 + gate_in * (1.0 - gate_sig))
    d_up = d_activ * gate_silu
    d_gate_up = jnp.concatenate([d_gate, d_up], axis=1).astype(half_type)
    grad_gate_up = jnp.dot(h_mlp.T, d_gate_up, preferred_element_type=jnp.float32)
    d_h_mlp_part = jnp.dot(d_gate_up, gu_b.T, preferred_element_type=jnp.float32)
    out_rows = resid_mid + tensor_total(mlp_part)
    term_mlp = jnp.sum(d_h_mlp_part * unit_mlp, axis=0)
    d_h_mlp = tensor_total(d_h_mlp_part)
    d_mid = out_grad + norm_back(d_h_mlp, unit_mlp, inv_mlp, g_mlp)
    d_branch = d_mid.astype(half_type)
    grad_out = jnp.dot(attention_output.T, d_branch, preferred_element_type=jnp.float32)
    d_att = (
        jnp.dot(d_branch, out_b.T, preferred_element_type=jnp.float32)
        .astype(half_type)
        .reshape(sequence_length, key_value_heads, heads_per_group, HEAD_SIZE)
    )
    d_query, d_keys, d_values = attention_backward(
        query_rows,
        key_head_rows,
        value_head_rows,
        d_att,
        log_total,
        seg_row,
        keep_row,
        attention_scale,
        block_rows,
    )
    d_query_n = rotate_back(
        d_query.reshape(sequence_length, q_heads, HEAD_SIZE), cosine_table, sine_table
    )
    d_key_n = rotate_back(d_keys, cosine_table, sine_table)
    term_query = jnp.sum(d_query_n * query_unit, axis=(0, 1))
    term_key = jnp.sum(d_key_n * key_unit, axis=(0, 1))
    d_query_raw = norm_back(d_query_n, query_unit, query_inv, query_gradient)
    d_key_raw = norm_back(d_key_n, key_unit, key_inv, g_key)
    d_raw = jnp.concatenate(
        [
            d_query_raw.reshape(sequence_length, query_columns),
            d_key_raw.reshape(sequence_length, key_value_columns),
            d_values.reshape(sequence_length, key_value_columns),
        ],
        axis=1,
    ).astype(half_type)
    grad_qkv = jnp.dot(h_att.T, d_raw, preferred_element_type=jnp.float32)
    d_h_att_part = jnp.dot(d_raw, qkv_b.T, preferred_element_type=jnp.float32)
    term_att = jnp.sum(d_h_att_part * unit_att, axis=0)
    d_h_att = tensor_total(d_h_att_part)
    input_grad = d_mid + norm_back(d_h_att, unit_att, inv_att, g_att)
    gain_terms = jnp.concatenate([term_att, term_mlp, term_query, term_key])
    gain_grad = lax.psum(gain_terms, ("dp", "tensor")) / workers
    new_gain_moment = MOMENTUM * gain_moment + gain_grad
    new_gains = gains - GAIN_RATE * new_gain_moment
    res_down = compress(grad_down, error_down, factor_down, moment_down, proj_down, True)
    res_gu = compress(
        grad_gate_up, error_gate_up, factor_gate_up, moment_gate_up, proj_gate_up, False
    )
    res_out = compress(grad_out, error_out, factor_out, moment_out, proj_out, True)
    res_qkv = compress(grad_qkv, error_qkv, factor_qkv, moment_qkv, proj_qkv, False)
    return (
        out_rows,
        input_grad,
        res_qkv[0],
        res_out[0],
        res_gu[0],
        res_down[0],
        res_qkv[1],
        res_out[1],
        res_gu[1],
        res_down[1],
        res_qkv[2],
        res_out[2],
        res_gu[2],
        res_down[2],
        res_qkv[3],
        res_out[3],
        res_gu[3],
        res_down[3],
        new_gains,
        new_gain_moment,
    )


def solution(mesh):
    in_specs = (
        P("dp", None),
        P("dp", None),
        P("dp", None),
        P("dp", None),
        P("dp", "tensor"),
        P("tensor", "dp"),
        P("dp", "tensor"),
        P("tensor", "dp"),
        P(),
        P("dp", "tensor"),
        P("tensor", "dp"),
        P("dp", "tensor"),
        P("tensor", "dp"),
        P("dp", None, "tensor"),
        P("dp", "tensor", None),
        P("dp", None, "tensor"),
        P("dp", "tensor", None),
        P("tensor", None),
        P("tensor", None),
        P("tensor", None),
        P("tensor", None),
        P(),
    )
    out_specs = (
        P("dp", None),
        P("dp", None),
        P("dp", "tensor"),
        P("tensor", "dp"),
        P("dp", "tensor"),
        P("tensor", "dp"),
        P("dp", "tensor"),
        P("tensor", "dp"),
        P("dp", "tensor"),
        P("tensor", "dp"),
        P("dp", None, "tensor"),
        P("dp", "tensor", None),
        P("dp", None, "tensor"),
        P("dp", "tensor", None),
        P("tensor", None),
        P("tensor", None),
        P("tensor", None),
        P("tensor", None),
        P(),
        P(),
    )
    return jax.shard_map(local, mesh=mesh, in_specs=in_specs, out_specs=out_specs, check_vma=False)
```

profile of v0, /device:TPU:0, one launch (start us, length us, event | category | flops | bytes accessed | tf_op | source)
XLA Modules:
  0.0 1749.5 jit_solution(11674688688044509170)
XLA Ops:
  21.5 41.5 %all-gather.5.cloned.1.call-done = bf16[1024,1024]{1,0:T(8,128)(2,1)} async-done(((bf16[128,1024]{1,0:T(8,128)(2,1)}), bf16[1024,1024]{1,0:T(8,128)(2,1)}) %all-gather.5.cloned.1.call-update) | async-done | bytes 2097168 | tf_op jit(solution)/shard_map/all_gather | solution.py:273
  62.9 8.6 fusion.86
  80.7 5.4 copy.67
  99.0 82.6 %while.27 = (s32[]{:T(128)}, bf16[4,512,2,2,128]{4,1,3,2,0:T(8,128)(2,1)}, f32[4,2,2,512,1]{3,2,1,4,0:T(2,128)S(1)}, s32[1,2048]{1,0:T(1,128)S(1)}, s32[4]{0:T(1...) while((s32[]{:T(128)}, ...), condition=%wide.region_6.7_spmd, body=%wide.region_3.6_spmd.sunk | while | flops 2204107264 | bytes 58292940 | solution.py:111
  113.2 6.5 fusion.168
  133.8 6.5 fusion.168
  154.4 6.5 fusion.168
  175.0 6.5 fusion.168
  181.6 5.8 copy.72
  191.5 7.6 fusion.94
  202.3 148.3 %all-reduce.9.cloned.1.call-done = f32[2048,1024]{1,0:T(8,128)} async-done(((f32[2048,1024]{1,0:T(8,128)}), f32[2048,1024]{1,0:T(8,128)}) %all-reduce.9.cloned.1.call-update) | async-done | bytes 8388624 | tf_op jit(solution)/shard_map/psum | solution.py:233
  350.6 10.1 multiply_reduce_fusion.4
  360.7 53.2 %all-gather.9.cloned.1.call-done = bf16[1024,1536]{1,0:T(8,128)(2,1)} async-done(((bf16[128,1536]{1,0:T(8,128)(2,1)}), bf16[1024,1536]{1,0:T(8,128)(2,1)}) %all-gather.9.cloned.1.call-update) | async-done | bytes 3145744 | tf_op jit(solution)/shard_map/all_gather | solution.py:274
  413.9 13.0 fusion.87
  426.9 33.4 %all-gather.11.cloned.1.call-done = bf16[768,1024]{1,0:T(8,128)(2,1)} async-done(((bf16[768,128]{1,0:T(8,128)(2,1)}), bf16[768,1024]{1,0:T(8,128)(2,1)}) %all-gather.11.cloned.1.call-update) | async-done | bytes 1572880 | tf_op jit(solution)/shard_map/all_gather | solution.py:276
  460.3 12.6 multiply_convert_fusion.3
  475.7 9.2 fusion.56
  486.7 9.5 bitcast_add_fusion.2
  500.2 14.3 bitcast_add_fusion
  514.5 8.0 fusion.100
  522.5 113.6 %all-reduce.11.cloned.1.call-done = f32[2048,1024]{1,0:T(8,128)} async-done(((f32[2048,1024]{1,0:T(8,128)}), f32[2048,1024]{1,0:T(8,128)}) %all-reduce.11.cloned.1.call-update) | async-done | bytes 8388624 | tf_op jit(solution)/shard_map/psum | solution.py:233
  636.1 10.6 multiply_reduce_fusion
  646.7 6.9 multiply_add_fusion.1
  657.6 266.6 %while.28 = (s32[]{:T(128)}, f32[2048,2,128]{0,2,1:T(8,128)S(1)}, f32[2048,2,128]{0,2,1:T(8,128)}, f32[4,512,2,2,128]{4,1,0,3,2:T(8,128)}, s32[4]{0:T(128)S(1)},...) while((s32[]{:T(128)}, f32[2048,2,128]{0,2,1:T(8,128)S(1)}, ...), condition=%wide.region_14.15_spmd.clone, body=%wide.region_12.14_spmd.clone.sunk | while | flops 5440799232 | bytes 182541152 | solution.py:165
  663.0 9.5 fusion.177
  674.5 13.2 fusion.179
  687.7 12.2 fusion.180
  712.0 12.1 fusion.182
  729.1 9.5 fusion.177
  740.5 13.3 fusion.179
  753.8 12.2 fusion.180
  778.0 12.7 fusion.182
  795.7 9.5 fusion.177
  807.2 13.3 fusion.179
  820.4 12.2 fusion.180
  839.3 5.4 fusion.181
  844.7 12.7 fusion.182
  862.4 9.5 fusion.177
  873.8 13.3 fusion.179
  887.1 12.2 fusion.180
  911.3 12.7 fusion.182
  934.2 5.4 copy.78
  945.3 6.0 bitcast_add_fusion.3
  955.6 8.2 bitcast_add_fusion.1
  972.2 9.2 fusion.95
  981.4 61.4 %all-reduce.15.cloned.1.call-done = (f32[1024,8]{0,1:T(8,128)}, f32[1024,8]{0,1:T(8,128)}, f32[1024,8]{0,1:T(8,128)}, f32[1024,8]{0,1:T(8,128)}) async-done(((f32[1024,8]{0,1:T(8,128)}, f32[1024,8]{0,1:T(8,128)}, f32[1024,8]{0,1:T(8,128)}, f32[1024,8]{0,1:T(8,128)}), (f32[1024,8]{0,1:T(8,128)}, f32[1024,8]{0,1:T(8,128)}, f32[1024,8]{0,1:T(8,128)}, f32[1024,8]{0,1:T(8,128)})) %all-reduce.15.cloned.1.call-update) | async-done | bytes 131088 | tf_op jit(solution)/shard_map/psum | solution.py:197
  1057.1 6.5 multiply_reduce_fusion.15
  1086.7 17.9 %subtract_multiply_fusion = (f32[1024,1]{0,1:T(1,128)S(1)}, f32[1024,1]{0,1:T(1,128)S(1)}, f32[1024,1]{0,1:T(1,128)S(1)}, f32[1024,1]{0,1:T(1,128)S(1)}, f32[102...) fusion(f32[1024,1]{0,1:T(1,128)S(1)} %get-tuple-element.562, f32[]{:T(128)S(6)} %rsqrt.195, ...), kind=kLoop, calls=%fused_computation.166 | loop fusion | flops 64512 | bytes 61580 | tf_op jit(solution)/shard_map/mul | solution.py:177
  1123.3 6.4 multiply_reduce_fusion.51
  1152.6 18.0 %subtract_multiply_fusion.7 = (f32[1024,1]{0,1:T(1,128)S(1)}, f32[1024,1]{0,1:T(1,128)S(1)}, f32[1024,1]{0,1:T(1,128)S(1)}, f32[1024,1]{0,1:T(1,128)S(1)}, f32[1...) fusion(f32[1024,1]{0,1:T(1,128)S(1)} %get-tuple-element.570, f32[]{:T(128)S(6)} %rsqrt.187, ...), kind=kLoop, calls=%fused_computation.237 | loop fusion | flops 64512 | bytes 61580 | tf_op jit(solution)/shard_map/mul | solution.py:177
  1170.6 6.4 fusion.101
  1190.6 6.5 multiply_reduce_fusion.87
  1220.2 17.9 %subtract_multiply_fusion.14 = (f32[1024,1]{0,1:T(1,128)S(1)}, f32[1024,1]{0,1:T(1,128)S(1)}, f32[1024,1]{0,1:T(1,128)S(1)}, f32[1024,1]{0,1:T(1,128)S(1)}, f32[...) fusion(f32[1024,1]{0,1:T(1,128)S(1)} %get-tuple-element.578, f32[]{:T(128)S(6)} %rsqrt.179, ...), kind=kLoop, calls=%fused_computation.308 | loop fusion | flops 64512 | bytes 61580 | tf_op jit(solution)/shard_map/mul | solution.py:177
  1254.3 6.5 multiply_reduce_fusion.123
  1284.0 17.9 %subtract_multiply_fusion.21 = (f32[1024,1]{0,1:T(1,128)S(1)}, f32[1024,1]{0,1:T(1,128)S(1)}, f32[1024,1]{0,1:T(1,128)S(1)}, f32[1024,1]{0,1:T(1,128)S(1)}, f32[...) fusion(f32[1024,1]{0,1:T(1,128)S(1)} %get-tuple-element.586, f32[]{:T(128)S(6)} %rsqrt.171, ...), kind=kLoop, calls=%fused_computation.379 | loop fusion | flops 64512 | bytes 61580 | tf_op jit(solution)/shard_map/mul | solution.py:177
  1307.2 10.3 fusion.67
  1317.6 58.6 %all-reduce.13.cloned.1.call-done = (f32[1024,8]{0,1:T(8,128)}, f32[512,8]{0,1:T(8,128)}, f32[1536,8]{0,1:T(8,128)}, f32[768,8]{0,1:T(8,128)}) async-done(((f32[1024,8]{0,1:T(8,128)}, f32[512,8]{0,1:T(8,128)}, f32[1536,8]{0,1:T(8,128)}, f32[768,8]{0,1:T(8,128)}), (f32[1024,8]{0,1:T(8,128)}, f32[512,8]{0,1:T(8,128)}, f32[1536,8]{0,1:T(8,128)}, f32[768,8]{0,1:T(8,128)})) %all-reduce.13.cloned.1.call-update) | async-done | bytes 122896 | tf_op jit(solution)/shard_map/psum | solution.py:210
  1387.9 5.4 subtract_bitcast_fusion.1
  1397.1 7.3 subtract_bitcast_fusion
  1404.5 263.8 %all-reduce.17.cloned.1.call-done = (f32[2048,1024]{1,0:T(8,128)}, f32[2048,1024]{1,0:T(8,128)}) async-done(((f32[2048,1024]{1,0:T(8,128)}, f32[2048,1024]{1,0:T(8,128)}), (f32[2048,1024]{1,0:T(8,128)}, f32[2048,1024]{1,0:T(8,128)})) %all-reduce.17.cloned.1.call-update) | async-done | bytes 16777232 | tf_op jit(solution)/shard_map/psum | solution.py:233
  1668.3 9.3 multiply_reduce_fusion.1
  1677.7 39.5 %psum.103 = f32[2304]{0:T(1024)S(1)} all-reduce(f32[2304]{0:T(1024)S(1)} %pad_maximum_fusion.10), channel_id=1, replica_groups=mesh['dp'=8,'tensor'=4] {'dp','tensor'}, use_global_device_ids=true, to_apply=%region_177.178 | all-reduce | flops 2304 | bytes 18432 | tf_op jit(solution)/shard_map/psum | solution.py:376
  1717.2 12.7 multiply_add_fusion
  1729.9 12.2 add.324
  (388 shorter events, 352.4 us)
Async XLA Ops:
  7.2 507.3 %copy-start = (f32[1536,8]{0,1:T(8,128)S(1)}, f32[1536,8]{0,1:T(8,128)}, u32[]{:S(2)}) copy-start(f32[1536,8]{0,1:T(8,128)} %param.45) | copy-start | bytes 147460
  7.2 55.7 %all-gather.5.cloned.1.call-start = ((), (), s32[]{:S(2)}) async-start(), calls=%async_computation | async-start | bytes 2359296 | tf_op jit(solution)/shard_map/all_gather | solution.py:273
  9.1 182.4 %all-gather.7.cloned.1.call-start = ((), (), s32[]{:S(2)}) async-start(), calls=%async_computation.1 | async-start | bytes 1179648 | tf_op jit(solution)/shard_map/all_gather | solution.py:275
  10.8 339.9 %all-reduce.9.cloned.1.call-start = ((), (), s32[]{:S(2)}) async-start(), calls=%async_computation.2 | async-start | bytes 16777216 | tf_op jit(solution)/shard_map/psum | solution.py:233
  12.1 50.8 %copy-start.47 = (f32[1024]{0:T(1024)}, f32[1024]{0:T(1024)S(1)}, u32[]{:S(2)}) copy-start(f32[1024]{0:T(1024)S(1)} %get-tuple-element.594) | copy-start | bytes 12292
  12.9 63.7 %copy-start.63 = (f32[128]{0:T(128)}, f32[128]{0:T(128)S(1)}, u32[]{:S(2)}) copy-start(f32[128]{0:T(128)S(1)} %get-tuple-element.595) | copy-start | bytes 1540
  12.9 73.2 %copy-start.59 = (f32[128]{0:T(128)}, f32[128]{0:T(128)S(1)}, u32[]{:S(2)}) copy-start(f32[128]{0:T(128)S(1)} %get-tuple-element.596) | copy-start | bytes 1540
  16.9 54.6 %copy-start.43 = (f32[2048]{0:T(1024)}, f32[2048]{0:T(1024)S(1)}, u32[]{:S(2)}) copy-start(f32[2048]{0:T(1024)S(1)} %add_rsqrt_fusion.3) | copy-start | bytes 24580
  20.8 68.9 %copy-start.14 = (f32[2048,64]{1,0:T(8,128)}, f32[2048,64]{1,0:T(8,128)S(1)}, u32[]{:S(2)}) copy-start(f32[2048,64]{1,0:T(8,128)S(1)} %get-tuple-element.597) | copy-start | bytes 1572868
  20.8 68.9 %copy-start.15 = (f32[2048,64]{1,0:T(8,128)}, f32[2048,64]{1,0:T(8,128)S(1)}, u32[]{:S(2)}) copy-start(f32[2048,64]{1,0:T(8,128)S(1)} %get-tuple-element.598) | copy-start | bytes 1572868
  21.1 56.4 %copy-start.18 = (f32[2048,64]{0,1:T(8,128)}, f32[2048,64]{0,1:T(8,128)S(1)}, u32[]{:S(2)}) copy-start(f32[2048,64]{0,1:T(8,128)S(1)} %copy.68) | copy-start | bytes 1572868
  21.5 56.1 %copy-start.20 = (f32[2048,64]{0,1:T(8,128)}, f32[2048,64]{0,1:T(8,128)S(1)}, u32[]{:S(2)}) copy-start(f32[2048,64]{0,1:T(8,128)S(1)} %copy.69) | copy-start | bytes 1572868
  80.7 5.4 copy-start.32
  92.6 6.4 copy-start.28
  92.6 6.4 copy-start.30
  181.6 9.9 copy-start.5
  181.6 9.9 copy-start.9
  199.1 214.7 %all-gather.9.cloned.1.call-start = ((), (), s32[]{:S(2)}) async-start(), calls=%async_computation.3 | async-start | bytes 3538944 | tf_op jit(solution)/shard_map/all_gather | solution.py:274
  201.0 259.3 %all-gather.11.cloned.1.call-start = ((), (), s32[]{:S(2)}) async-start(), calls=%async_computation.4 | async-start | bytes 1769472 | tf_op jit(solution)/shard_map/all_gather | solution.py:276
  201.8 212.1 %copy-start.49 = (f32[1024]{0:T(1024)S(1)}, f32[1024]{0:T(1024)}, u32[]{:S(2)}) copy-start(f32[1024]{0:T(1024)} %get-tuple-element.593) | copy-start | bytes 12292
  201.8 434.3 %all-reduce.11.cloned.1.call-start = ((), (), s32[]{:S(2)}) async-start(), calls=%async_computation.5 | async-start | bytes 16777216 | tf_op jit(solution)/shard_map/psum | solution.py:233
  460.3 15.4 copy-start.67
  484.9 557.9 %all-reduce.15.cloned.1.call-start = ((), (), s32[]{:S(2)}) async-start(), calls=%async_computation.7 | async-start | bytes 262144 | tf_op jit(solution)/shard_map/psum | solution.py:197
  486.7 11.2 copy-start.54
  486.7 13.5 copy-start.70
  636.1 10.6 copy-start.11
  646.7 6.9 copy-start.68
  687.7 15.6 copy-start.10
  753.8 15.6 copy-start.10
  820.4 15.6 copy-start.10
  887.1 15.6 copy-start.10
  924.2 5.3 copy-start.6
  924.2 5.3 copy-start.33
  924.2 5.3 copy-start.61
  934.2 5.5 copy-start.19
  934.2 5.5 copy-start.21
  940.4 10.9 slice-start.2
  945.2 6.0 slice-start.3
  945.3 6.0 copy-start.16
  945.3 6.0 copy-start.62
  945.3 10.3 slice-start
  955.6 10.2 copy-start.50
  972.1 404.1 %all-reduce.13.cloned.1.call-start = ((), (), s32[]{:S(2)}) async-start(), calls=%async_computation.6 | async-start | bytes 245760 | tf_op jit(solution)/shard_map/psum | solution.py:210
  1109.9 67.1 %copy-start.52 = (f32[1024,8]{0,1:T(8,128)S(1)}, f32[1024,8]{0,1:T(8,128)}, u32[]{:S(2)}) copy-start(f32[1024,8]{0,1:T(8,128)} %get-tuple-element.420) | copy-start | bytes 98308
  1109.9 67.1 %copy-start.53 = (f32[1024,8]{0,1:T(8,128)S(1)}, f32[1024,8]{0,1:T(8,128)}, u32[]{:S(2)}) copy-start(f32[1024,8]{0,1:T(8,128)} %get-tuple-element.421) | copy-start | bytes 98308
  1307.0 361.3 %all-reduce.17.cloned.1.call-start = ((), (), s32[]{:S(2)}) async-start(), calls=%async_computation.8 | async-start | bytes 33554432 | tf_op jit(solution)/shard_map/psum | solution.py:233
  1377.1 7.7 copy-start.42
  1380.3 5.9 copy-start.27
  1380.3 5.9 copy-start.36
  1380.3 7.6 copy-start.41
  1380.4 12.9 copy-start.37
  1380.4 7.5 copy-start.8
  1386.2 10.9 slice-start.4
  1387.9 5.4 copy-start.25
  1387.9 5.4 copy-start.34
  1387.9 7.1 copy-start.45
  1387.9 7.1 copy-start.23
  1387.9 7.1 copy-start.31
  1387.9 9.2 slice-start.5
  1395.0 9.4 copy-start.35
  1668.3 9.3 copy-start.57
  1729.9 12.2 copy-start.46
  1729.9 12.2 copy-start.58
  1729.9 12.8 copy-start.1
  (29 other events, 83.3 us)
Sparse Core Ops, SparseCore 0:
  10.7 52.1 all-gather.4
  65.6 38.6 all-gather.6
  199.3 151.3 all-reduce.8
  353.2 60.5 all-gather.8
  416.3 43.9 all-gather.10
  485.0 151.0 all-reduce.10
  972.2 70.5 all-reduce.14
  1307.1 69.0 all-reduce.12
  1379.5 288.7 all-reduce.16
where the time goes:
time: 1760 us; the launch traced here: 1750 us
  waiting for transfers between devices  774 us (44%)
  other arithmetic  428 us (24%)
  matrix products  395 us (22%)
  local copies, waits for them, and re-layouts  60.4 us (3%)
  blocking collectives  39.5 us (2%)
  between operations  36.8 us (2%)
    psum x3, waiting for transfers between devices, tensor_total(): return lax.psum(partial_sum, 'tensor')  526 us
    reduce_sum x36, other arithmetic, orthonormal(): jnp.sum(column * finished, axis=-1, keepdims=True) * finished  113 us
    mul x4, other arithmetic, orthonormal(): column * lax.rsqrt(jnp.sum(column * column, axis=-1, keepdims=True) + 1e-12)  71.7 us
    psum x1, waiting for transfers between devices, compress(): p_hat = orthonormal(lax.psum(p_local, 'dp') / workers)  61.4 us
    psum x1, waiting for transfers between devices, compress(): q_new = lax.psum(q_local, 'dp') / workers  58.6 us
    dot_general x8, matrix products, block_scores(): jnp.einsum('cwbn,zwn->wbcz', query_block, key_head_rows, preferred_elemen...  56 us
    all_gather x1, waiting for transfers between devices, local(): lax.all_gather(proj_gate_up.astype(half_type), 'dp', axis=0, tiled=True)  53.2 us
    dot_general x4, matrix products, block_backward(): jnp.einsum('cwbn,zwn->wbcz', gradient_block, value_head_rows, preferred_e...  53 us
  transfers between devices with their start and end apart: 9, of which 8 were waited for; matrix products, arithmetic and copies ran while one was open for 14% of the time, Pallas kernels for 0%

commit v1 on v0

v1 whole, which is shorter than its diff:
```python
import functools
import math

import jax
import jax.numpy as jnp
from jax import lax
from jax.experimental import pallas as pl
from jax.experimental.pallas import tpu as pltpu
from jax.sharding import PartitionSpec as P

D = 1024
QUERY_HEADS = 16
KEY_VALUE_HEADS = 8
HEAD_SIZE = 128
FF = 3072
RANK = 8


EPSILON = 1e-06
ROPE_THETA = 1000000.0
MOMENTUM = 0.5
STEP_RATE = 0.003
GAIN_RATE = 0.02
CHUNKS = 2
BLOCK = 256
ROWS = 256
SCALE = 1.0 / math.sqrt(HEAD_SIZE)
SCALE_2 = SCALE / math.log(2.0)
MIB = 1024 * 1024

HALF = jnp.bfloat16
FULL = jnp.float32
NN = (((1,), (0,)), ((), ()))
NT = (((1,), (1,)), ((), ()))
TN = (((0,), (0,)), ((), ()))


def mul(left, right, dims=NN):
    return lax.dot_general(left, right, dims, preferred_element_type=FULL)


def shape_of(dims, dtype):
    return jax.ShapeDtypeStruct(dims, dtype)


def far(array):
    return pltpu.with_memory_space_constraint(array, pltpu.HBM)


def near(array):
    return pltpu.with_memory_space_constraint(array, pltpu.VMEM)


def near_shape(dims, dtype):
    return pltpu.VMEM(dims, dtype)


def far_shape(dims, dtype):
    return pltpu.HBM(dims, dtype)


def whole(*dims):
    return pl.BlockSpec(dims, lambda *_: (0,) * len(dims), pipeline_mode=pl.Buffered(1))


def made(*dims):
    return pl.BlockSpec(dims, lambda *_: (0,) * len(dims))


def block_bytes(spec, array):
    if spec.block_shape is None:
        return 0
    size = array.dtype.itemsize
    *lead, height, width = spec.block_shape
    height = -(-height // (32 // size)) * (32 // size)
    count = 2 if spec.pipeline_mode is None else spec.pipeline_mode.buffer_count
    return math.prod(lead) * height * (-(-width // 128) * 128) * size * count


def call(kernel, grid, in_specs, out_specs, out_shape, args, scratch=(), table=None, flops=0, aliases=None, after=(), room=6):
    moved = sum(math.prod(a.shape) * a.dtype.itemsize for a in list(args) + list(out_shape))
    prefetch = () if table is None else (table,)
    first = len(prefetch) + len(args)
    need = sum(block_bytes(*pair) for pair in zip(list(in_specs) + list(out_specs), list(args) + list(out_shape)))
    need += sum(math.prod(item.shape) * jnp.dtype(item.dtype).itemsize for item in scratch) + room * MIB

    def body(*refs):
        kernel(*refs[:first], *refs[first + len(after) :])

    return pl.pallas_call(
        body,
        grid_spec=pltpu.PrefetchScalarGridSpec(
            num_scalar_prefetch=len(prefetch),
            grid=grid,
            in_specs=list(in_specs) + [pl.BlockSpec(memory_space=pl.ANY)] * len(after),
            out_specs=out_specs,
            scratch_shapes=list(scratch),
        ),
        out_shape=out_shape,
        input_output_aliases=aliases or {},
        compiler_params=pltpu.CompilerParams(vmem_limit_bytes=need),
        cost_estimate=pl.CostEstimate(
            flops=int(flops), bytes_accessed=int(moved), transcendentals=0
        ),
    )(*prefetch, *args, *after)


def rms_parts(values, gain_vec):
    factor = lax.rsqrt(jnp.mean(values * values, axis=-1, keepdims=True) + EPSILON)
    normal = values * factor
    return (normal * gain_vec, normal, factor)


def norm_back(grad_in, normal, factor, gain_vec):
    scaled = grad_in * gain_vec
    return factor * (scaled - normal * jnp.mean(scaled * normal, axis=-1, keepdims=True))


def rope_tables(sequence_length):
    position = jnp.arange(sequence_length, dtype=FULL)
    inverse = ROPE_THETA ** (-(jnp.arange(HEAD_SIZE // 2, dtype=FULL) * 2.0 / HEAD_SIZE))
    angles = position[:, None] * inverse[None, :]
    cosine, sine = jnp.cos(angles), jnp.sin(angles)
    return jnp.concatenate([cosine, cosine], 1), jnp.concatenate([-sine, sine], 1)


def ring_of(count):
    return list(range(0, count, 2)) + list(range(1, count, 2))[::-1]


def ring_step(pair, count, cut=None):
    ring = ring_of(count)
    ahead = [(ring[i], ring[(i + 1) % count]) for i in range(count)]
    back = [(target, source) for source, target in ahead]
    from_left, from_right = pair
    if cut is not None:
        from_left, from_right = from_left[:cut], from_right[cut:]
    return lax.ppermute(from_left, "dp", ahead), lax.ppermute(from_right, "dp", back)


def ring_gather(own, count):
    steps, pair = [], (own, own)
    for _ in range(count // 2 - 1):
        pair = ring_step(pair, count)
        steps.append(pair)
    steps.append(ring_step(pair, count, own.shape[0] // 2))
    return [own] + [piece for step in steps for piece in step], steps


def ring_places(count, shard):
    index = lax.axis_index("dp")
    here = jnp.where(index % 2 == 0, index // 2, count - 1 - index // 2)
    shifts = [0]
    for shift in range(1, count // 2):
        shifts += [count - shift, shift]
    shifts = jnp.array(shifts + [count // 2] * 2, jnp.int32)
    at = (here + shifts) % count
    owner = jnp.where(at < count // 2, 2 * at, 2 * (count - 1 - at) + 1)
    late = (jnp.arange(shifts.shape[0]) == shifts.shape[0] - 1).astype(jnp.int32)
    return (owner * shard + late * (shard // 2)).astype(jnp.int32)


def assemble(tab_ref, first, pieces, target):
    for number, piece in enumerate(pieces):
        rows = piece.shape[0]
        target[pl.ds(pl.multiple_of(tab_ref[first + number], rows), rows), :] = piece[...]


def stage_kernel(in_ref, out_ref):
    out_ref[...] = in_ref[...]


def stage(values, after):
    spec = whole(*values.shape)
    return call(stage_kernel, (1,), [spec], [made(*values.shape)], [shape_of(values.shape, values.dtype)], (values,), after=after)[0]


def input_kernel(x_ref, g_ref, h_ref):
    h_ref[...] = rms_parts(x_ref[...], g_ref[...])[0].astype(HALF)


def input_norm(hidden_in, g_att):
    rows = hidden_in.shape[0]
    by_row = pl.BlockSpec((BLOCK, D), lambda i: (i, 0))
    return call(
        input_kernel, (rows // BLOCK,), [by_row, whole(1, D)], [by_row], [shape_of((rows, D), HALF)],
        (far(hidden_in), g_att[None]),
    )[0]


def turn_kernel(h_ref, ht_ref):
    ht_ref[...] = h_ref[...].T


def turned(h_att, after):
    rows = h_att.shape[0]
    return call(
        turn_kernel,
        (rows // BLOCK,),
        [pl.BlockSpec((BLOCK, D), lambda i: (i, 0))],
        [pl.BlockSpec((D, BLOCK), lambda i: (0, i))],
        [far_shape((D, rows), HALF)],
        (h_att,),
        after=after,
    )[0]


def qkv_kernel(q_heads, kv_heads, count, tab_ref, h_ref, gq_ref, gk_ref, cos_ref, sin_ref, *refs):
    pieces, (w_ref, q_ref, k_ref, v_ref, kt_ref, rq_ref, rk_ref) = refs[:count], refs[count:]

    @pl.when(pl.program_id(0) == 0)
    def _():
        assemble(tab_ref, 0, pieces, w_ref)

    h_att = h_ref[...]
    cosine, sine = cos_ref[...], sin_ref[...]
    ones = jnp.ones((h_att.shape[0], HEAD_SIZE), HALF)
    for pair in range((q_heads + 2 * kv_heads) // 2):
        both = mul(h_att, w_ref[:, 2 * pair * HEAD_SIZE : 2 * (pair + 1) * HEAD_SIZE])
        for part in range(2):
            head = 2 * pair + part
            raw = both[:, heads_of(part)]
            if head >= q_heads + kv_heads:
                at = 2 * (head - q_heads - kv_heads) * HEAD_SIZE
                v_ref[:, at : at + HEAD_SIZE] = raw.astype(HALF)
                v_ref[:, at + HEAD_SIZE : at + 2 * HEAD_SIZE] = ones
                continue
            normed = rms_parts(raw, gq_ref[...] if head < q_heads else gk_ref[...])[0]
            rotated = normed * cosine + pltpu.roll(normed, HEAD_SIZE // 2, 1) * sine
            if head < q_heads:
                rq_ref[:, heads_of(head)] = raw
                q_ref[:, heads_of(head)] = rotated.astype(HALF)
            else:
                rk_ref[:, heads_of(head - q_heads)] = raw
                k_ref[:, heads_of(head - q_heads)] = rotated.astype(HALF)
                kt_ref[heads_of(head - q_heads), :] = rotated.T.astype(HALF)


def make_qkv(table, h_att, pieces, g_query, g_key, cosine, sine, q_heads, kv_heads, after):
    rows = h_att.shape[0]
    q_cols, k_cols = q_heads * HEAD_SIZE, kv_heads * HEAD_SIZE
    cols = q_cols + 2 * k_cols
    w_cols = pieces[0].shape[1]
    by_row = lambda width: pl.BlockSpec((BLOCK, width), lambda i, _: (i, 0))
    by_col = lambda height: pl.BlockSpec((height, BLOCK), lambda i, _: (0, i))
    return call(
        functools.partial(qkv_kernel, q_heads, kv_heads, len(pieces)),
        (rows // BLOCK,),
        [by_row(D), whole(1, HEAD_SIZE), whole(1, HEAD_SIZE), by_row(HEAD_SIZE), by_row(HEAD_SIZE)]
        + [whole(*piece.shape) for piece in pieces],
        [made(D, w_cols), by_row(q_cols), by_row(k_cols), by_row(2 * k_cols), by_col(k_cols),
         by_row(q_cols), by_row(k_cols)],
        [near_shape((D, w_cols), HALF), near_shape((rows, q_cols), HALF),
         near_shape((rows, k_cols), HALF), near_shape((rows, 2 * k_cols), HALF), far_shape((k_cols, rows), HALF),
         far_shape((rows, q_cols), FULL), far_shape((rows, k_cols), FULL)],
        (h_att, g_query[None], g_key[None], far(cosine), far(sine)) + tuple(far(piece) for piece in pieces),
        table=table,
        flops=2 * rows * D * cols,
        after=after,
    )


def picked(*dims):
    return pl.BlockSpec(dims, lambda i, tab: (tab[i], 0))


def picked_col(*dims):
    return pl.BlockSpec(dims, lambda i, tab: (0, tab[i]))


def stepped(*dims):
    return pl.BlockSpec(dims, lambda i, *_: (i, 0))


def stepped_col(*dims):
    return pl.BlockSpec(dims, lambda i, *_: (0, i))


def halves_of(steps, *dims):
    half = steps // 2
    return [
        pl.BlockSpec(dims, lambda i, *_: (jnp.minimum(i, half - 1), 0)),
        pl.BlockSpec(dims, lambda i, *_: (jnp.maximum(i - half, 0), 0)),
    ]


def half_shapes(rows):
    return [shape_of((rows // 2, D), HALF), shape_of((rows // 2, D), FULL)]


def put_halves(step, steps, part, send_ref, keep_ref):
    @pl.when(step < steps // 2)
    def _():
        send_ref[...] = part.astype(HALF)

    @pl.when(step >= steps // 2)
    def _():
        keep_ref[...] = part


def take_halves(step, steps, theirs, mine, target):
    @pl.when(step < steps // 2)
    def _():
        target[...] = theirs[...]

    @pl.when(step >= steps // 2)
    def _():
        target[...] = mine[...]


def mask_of(seg_keys, seg_queries, key_at, query_at, diagonal, key_axis):
    same = seg_keys == seg_queries
    if not diagonal:
        return same
    key_pos = key_at + lax.broadcasted_iota(jnp.int32, same.shape, key_axis)
    query_pos = query_at + lax.broadcasted_iota(jnp.int32, same.shape, 1 - key_axis)
    return (same & (key_pos < query_pos)) | (key_pos == query_pos)


def over_keys(tab_ref, steps, visit):
    step = pl.program_id(0)
    last = tab_ref[step]
    query_at = last * BLOCK
    visit(pl.multiple_of(query_at, BLOCK), query_at, True)

    def body(key_block, carry):
        visit(pl.multiple_of(key_block * BLOCK, BLOCK), query_at, False)
        return carry

    lax.fori_loop(tab_ref[steps + step], last, body, 0)


def heads_of(index):
    return slice(index * HEAD_SIZE, (index + 1) * HEAD_SIZE)


def attend_kernel(steps, q_heads, group, tab_ref, q_ref, k_ref, v_ref, segq_ref, segk_ref,
                  att_ref, att_t_ref, log_ref, q_scr, out_scr):
    shared_heads = q_heads // group
    high = group * BLOCK
    for head in range(q_heads):
        q_scr[head * BLOCK : (head + 1) * BLOCK, :] = q_ref[:, heads_of(head)]
    out_scr[...] = jnp.zeros(out_scr.shape, FULL)

    def visit(key_at, query_at, diagonal):
        keys = pl.ds(key_at, BLOCK)
        mask = mask_of(segk_ref[:, keys], segq_ref[...], key_at, query_at, diagonal, 1)
        mask = jnp.concatenate([mask] * group, axis=0)
        for shared in range(shared_heads):
            at = slice(shared * high, (shared + 1) * high)
            scores = mul(q_scr[at, :], k_ref[keys, heads_of(shared)], NT)
            expo = jnp.where(mask, jnp.exp2(scores * SCALE_2), 0.0).astype(HALF)
            out_scr[at, :] += mul(expo, v_ref[keys, 2 * shared * HEAD_SIZE : 2 * (shared + 1) * HEAD_SIZE])

    over_keys(tab_ref, steps, visit)
    for head in range(q_heads):
        at = slice(head * BLOCK, (head + 1) * BLOCK)
        total = out_scr[at, HEAD_SIZE:]
        attended = (out_scr[at, :HEAD_SIZE] / total).astype(HALF)
        att_ref[:, heads_of(head)] = attended
        att_t_ref[heads_of(head), :] = attended.T
        log_ref[head : head + 1, :] = jnp.log2(total).T[:1, :]


def attend(chunk, table, queries, keys, values, seg_col, key_row, group, after):
    rows, q_cols = queries.shape
    k_cols = keys.shape[1]
    q_heads = q_cols // HEAD_SIZE
    size = rows // CHUNKS
    steps = size // BLOCK
    extent = size * (chunk + 1)
    return call(
        functools.partial(attend_kernel, steps, q_heads, group),
        (steps,),
        [picked(BLOCK, q_cols), whole(extent, k_cols), whole(extent, 2 * k_cols), picked(BLOCK, 1),
         whole(1, extent)],
        [stepped(BLOCK, q_cols), stepped_col(q_cols, BLOCK), stepped_col(q_heads, BLOCK)],
        [shape_of((size, q_cols), HALF), far_shape((q_cols, size), HALF), shape_of((q_heads, size), FULL)],
        (near(queries), near(keys), near(values), far(seg_col), key_row),
        scratch=[pltpu.VMEM((q_heads * BLOCK, HEAD_SIZE), HALF), pltpu.VMEM((q_heads * BLOCK, 2 * HEAD_SIZE), FULL)],
        table=table,
        flops=6 * size * q_cols * 1024,
        room=8,
        after=after,
    )


def attend_back_kernel(steps, q_heads, group, first, tab_ref, q_ref, k_ref, v_ref, kt_ref, segq_ref, segk_ref,
                       wo_ref, att_ref, log_ref, rq_ref, gq_ref, cos_ref, sin_ref, theirs_ref, mine_ref, *refs):
    if not first:
        dk_in, dv_in, refs = refs[0], refs[1], refs[2:]
    raw_ref, term_ref, dk_ref, dv_ref, branch_scr, q_scr, datt_scr, log_scr, delta_scr, dq_scr = refs
    step = pl.program_id(0)
    shared_heads = q_heads // group
    wide = group * BLOCK

    @pl.when(step == 0)
    def _():
        term_ref[...] = jnp.zeros(term_ref.shape, FULL)
        if first:
            dk_ref[...] = jnp.zeros(dk_ref.shape, FULL)
            dv_ref[...] = jnp.zeros(dv_ref.shape, FULL)
        else:
            dk_ref[...] = dk_in[...]
            dv_ref[...] = dv_in[...]

    take_halves(step, steps, theirs_ref, mine_ref, branch_scr)
    d_att = mul(branch_scr[...], wo_ref[...]).astype(HALF)
    product = (d_att.astype(FULL) * att_ref[...].astype(FULL)).T
    for head in range(q_heads):
        at = slice(head * BLOCK, (head + 1) * BLOCK)
        q_scr[at, :] = q_ref[:, heads_of(head)]
        datt_scr[at, :] = d_att[:, heads_of(head)]
        log_scr[:, at] = log_ref[head : head + 1, :]
        delta_scr[:, at] = jnp.sum(product[heads_of(head), :], axis=0, keepdims=True)
    dq_scr[...] = jnp.zeros(dq_scr.shape, FULL)

    def visit(key_at, query_at, diagonal):
        keys = pl.ds(key_at, BLOCK)
        mask = mask_of(segk_ref[keys, :], segq_ref[...], key_at, query_at, diagonal, 0)
        mask = jnp.concatenate([mask] * group, axis=1)
        for shared in range(shared_heads):
            at = slice(shared * wide, (shared + 1) * wide)
            own = heads_of(shared)
            scores = mul(k_ref[keys, own], q_scr[at, :], NT)
            probs = jnp.where(mask, jnp.exp2(scores * SCALE_2 - log_scr[:, at]), 0.0)
            value_cols = slice(2 * shared * HEAD_SIZE, (2 * shared + 1) * HEAD_SIZE)
            d_probs = mul(v_ref[keys, value_cols], datt_scr[at, :], NT)
            d_scores = (probs * (d_probs - delta_scr[:, at])).astype(HALF)
            dv_ref[keys, own] += mul(probs.astype(HALF), datt_scr[at, :])
            dk_ref[keys, own] += mul(d_scores, q_scr[at, :])
            dq_scr[:, at] += mul(kt_ref[own, keys], d_scores)

    over_keys(tab_ref, steps, visit)
    cosine, sine = cos_ref[...], sin_ref[...]
    gain = gq_ref[...]
    for head in range(q_heads):
        turned = dq_scr[:, head * BLOCK : (head + 1) * BLOCK].T * SCALE
        d_normed = turned * cosine - pltpu.roll(turned, HEAD_SIZE // 2, 1) * sine
        _, unit, factor = rms_parts(rq_ref[:, heads_of(head)], gain)
        term_ref[...] += jnp.sum(d_normed * unit, axis=0, keepdims=True)
        raw_ref[:, heads_of(head)] = norm_back(d_normed, unit, factor, gain).astype(HALF)


def attend_back(chunk, table, queries, keys, values, keys_t, seg_row, key_col, first_b, att, log_total,
                raw_q, g_query, cosine, sine, pieces, later, group, after):
    rows, q_cols = queries.shape
    k_cols = keys.shape[1]
    q_heads = q_cols // HEAD_SIZE
    size = rows // CHUNKS
    steps = size // BLOCK
    extent = size * (chunk + 1)
    return call(
        functools.partial(attend_back_kernel, steps, q_heads, group, not later),
        (steps,),
        [picked(BLOCK, q_cols), whole(extent, k_cols), whole(extent, 2 * k_cols), whole(k_cols, extent),
         picked_col(1, BLOCK), whole(extent, 1), pl.BlockSpec((D, q_cols), lambda *_: (0, 2)),
         stepped(BLOCK, q_cols), stepped_col(q_heads, BLOCK), picked(BLOCK, q_cols), whole(1, HEAD_SIZE),
         picked(BLOCK, HEAD_SIZE), picked(BLOCK, HEAD_SIZE)]
        + halves_of(steps, BLOCK, D)
        + [whole(extent, k_cols)] * len(later),
        [stepped(BLOCK, q_cols), made(1, HEAD_SIZE), made(extent, k_cols), made(extent, k_cols)],
        [shape_of((size, q_cols), HALF), shape_of((1, HEAD_SIZE), FULL),
         shape_of((extent, k_cols), FULL), shape_of((extent, k_cols), FULL)],
        (near(queries), near(keys), near(values), far(keys_t), seg_row, far(key_col), near(first_b), att, log_total,
         far(raw_q), g_query[None], far(cosine), far(sine)) + tuple(pieces) + tuple(later),
        scratch=[pltpu.VMEM((BLOCK, D), HALF), pltpu.VMEM((q_heads * BLOCK, HEAD_SIZE), HALF),
                 pltpu.VMEM((q_heads * BLOCK, HEAD_SIZE), HALF), pltpu.VMEM((1, q_heads * BLOCK), FULL),
                 pltpu.VMEM((1, q_heads * BLOCK), FULL), pltpu.VMEM((HEAD_SIZE, q_heads * BLOCK), FULL)],
        table=table,
        flops=10 * size * q_cols * 1024 + 2 * size * q_cols * D,
        room=10,
        after=after,
    )


def raw_back_kernel(steps, kv_heads, tab_ref, rawq_ref, dk_ref, dv_ref, rk_ref, gk_ref, cos_ref, sin_ref,
                    w_ref, f_ref, raw_ref, thin_ref, term_ref, send_ref, keep_ref):
    step = pl.program_id(0)

    @pl.when(step == 0)
    def _():
        term_ref[...] = jnp.zeros(term_ref.shape, FULL)

    q_cols = rawq_ref.shape[1]
    k_cols = kv_heads * HEAD_SIZE
    cosine, sine = cos_ref[...], sin_ref[...]
    gain = gk_ref[...]
    raw_ref[:, :q_cols] = rawq_ref[...]
    for head in range(kv_heads):
        turned = dk_ref[:, heads_of(head)] * SCALE
        d_normed = turned * cosine - pltpu.roll(turned, HEAD_SIZE // 2, 1) * sine
        _, unit, factor = rms_parts(rk_ref[:, heads_of(head)], gain)
        term_ref[...] += jnp.sum(d_normed * unit, axis=0, keepdims=True)
        raw_ref[:, q_cols + head * HEAD_SIZE : q_cols + (head + 1) * HEAD_SIZE] = norm_back(
            d_normed, unit, factor, gain
        ).astype(HALF)
    raw_ref[:, q_cols + k_cols :] = dv_ref[...].astype(HALF)
    put_halves(step, steps, mul(raw_ref[...], w_ref[...], NT), send_ref, keep_ref)
    both = mul(stacked(f_ref[...], (0, 1)), raw_ref[...], NT)
    thin_ref[...] = both[:RANK] + both[RANK:]


def raw_back(chunk, table, raw_q_back, d_keys, d_values, raw_k, g_key, cosine, sine, first_b, factor_t, after):
    size, q_cols = raw_q_back.shape
    half = size // 2
    k_cols = raw_k.shape[1]
    cols = q_cols + 2 * k_cols
    return call(
        functools.partial(raw_back_kernel, 2, k_cols // HEAD_SIZE),
        (2,),
        [stepped(half, q_cols), picked(half, k_cols), picked(half, k_cols), picked(half, k_cols),
         whole(1, HEAD_SIZE), picked(half, HEAD_SIZE), picked(half, HEAD_SIZE), whole(D, cols), whole(RANK, cols)],
        [pl.BlockSpec((half, cols), lambda i, tab: (tab[i] - chunk * 2, 0)),
         pl.BlockSpec((RANK, half), lambda i, tab: (0, tab[i] - chunk * 2)), made(1, HEAD_SIZE)]
        + halves_of(2, half, D),
        [shape_of((size, cols), HALF), shape_of((RANK, size), FULL), shape_of((1, HEAD_SIZE), FULL)]
        + half_shapes(size),
        (raw_q_back, d_keys, d_values, far(raw_k), g_key[None], far(cosine), far(sine), near(first_b), factor_t),
        table=table,
        flops=2 * size * D * cols,
        after=after,
        room=8,
    )


def mlp_kernel(tab_ref, grad_ref, theirs_ref, mine_ref, w_ref, ht_ref, act_ref, act_t_ref, dgu_ref, h_scr):
    take_halves(pl.program_id(0), 2, theirs_ref, mine_ref, h_scr)
    ff_cols = act_ref.shape[1]
    h_mlp = h_scr[...]
    d_mlp = grad_ref[...].astype(HALF)
    ht_ref[...] = h_mlp.T
    width = tile_of(ff_cols)
    for at in range(0, ff_cols, width):
        gate = mul(h_mlp, w_ref[:, at : at + width])
        up = mul(h_mlp, w_ref[:, ff_cols + at : ff_cols + at + width])
        d_activ = mul(d_mlp, w_ref[:, 2 * ff_cols + at : 2 * ff_cols + at + width])
        sig = jax.nn.sigmoid(gate)
        silu = gate * sig
        activ = (silu * up).astype(HALF)
        act_ref[:, at : at + width] = activ
        act_t_ref[at : at + width, :] = activ.T
        dgu_ref[:, at : at + width] = (d_activ * up * sig * (1.0 + gate * (1.0 - sig))).astype(HALF)
        dgu_ref[:, ff_cols + at : ff_cols + at + width] = (d_activ * silu).astype(HALF)


def feed_forward(table, out_grad, weights, pieces, after):
    half = pieces[0].shape[0]
    size = 2 * half
    w_cols = weights.shape[1]
    ff_cols = w_cols // 3
    return call(
        mlp_kernel,
        (2,),
        [picked(half, D), whole(half, D), whole(half, D), whole(D, w_cols)],
        [stepped_col(D, half), stepped(half, ff_cols), stepped_col(ff_cols, half), stepped(half, 2 * ff_cols)],
        [shape_of((D, size), HALF), shape_of((size, ff_cols), HALF), shape_of((ff_cols, size), HALF),
         shape_of((size, 2 * ff_cols), HALF)],
        (far(out_grad),) + tuple(far(piece) for piece in pieces) + (weights,),
        scratch=[pltpu.VMEM((half, D), HALF)],
        table=table,
        flops=2 * size * D * ff_cols * 3,
        after=after,
        room=12,
    )


def project_kernel(left_ref, right_ref, send_ref, keep_ref):
    put_halves(pl.program_id(0), 2, mul(left_ref[...], right_ref[...], NT), send_ref, keep_ref)


def project(left, weights, at, after, kept=shape_of):
    size, depth = left.shape
    half = size // 2
    return call(
        project_kernel,
        (2,),
        [stepped(half, depth), pl.BlockSpec((D, depth), lambda *_: (0, at))],
        halves_of(2, half, D),
        [shape_of((half, D), HALF), kept((half, D), FULL)],
        (left, weights),
        flops=2 * size * D * depth,
        after=after,
    )


def mid_kernel(tab_ref, x_ref, part_ref, other_ref, g_ref, resid_ref, h_ref):
    resid = x_ref[...] + (part_ref[...].astype(FULL) + other_ref[...].astype(FULL))
    resid_ref[...] = resid
    h_ref[...] = rms_parts(resid, g_ref[...])[0].astype(HALF)


def mid_back_kernel(tab_ref, grad_ref, part_ref, other_ref, g_ref, resid_ref, delta_ref, branch_ref, term_ref):
    d_h = part_ref[...].astype(FULL) + other_ref[...].astype(FULL)
    _, unit, factor = rms_parts(resid_ref[...], 1.0)
    delta = norm_back(d_h, unit, factor, g_ref[...])
    delta_ref[...] = delta
    branch_ref[...] = (grad_ref[...] + delta).astype(HALF)
    add_term(term_ref, d_h * unit)


def in_back_kernel(tab_ref, x_ref, part_ref, other_ref, g_ref, mid_ref, delta_ref, term_ref):
    d_h = part_ref[...].astype(FULL) + other_ref[...].astype(FULL)
    _, unit, factor = rms_parts(x_ref[...], 1.0)
    delta_ref[...] = (mid_ref[...] + norm_back(d_h, unit, factor, g_ref[...])).astype(HALF)
    add_term(term_ref, d_h * unit)


def add_term(term_ref, product):
    @pl.when(pl.program_id(0) == 0)
    def _():
        term_ref[...] = jnp.zeros(term_ref.shape, FULL)

    term_ref[...] += jnp.sum(product, axis=0, keepdims=True)


def norm_rows(kernel, own_half, base, part, other, gain, extra, kinds, with_term, after=()):
    half = part.shape[0]
    steps = half // ROWS
    rows = stepped(ROWS, D)
    return call(
        kernel,
        (steps,),
        [pl.BlockSpec((ROWS, D), lambda i, tab: (tab[0] * steps + i, 0)), rows, rows, whole(1, D)]
        + [rows] * len(extra),
        [rows] * len(kinds) + [made(1, D)] * with_term,
        [near_shape((half, D), dtype) if dtype == FULL else shape_of((half, D), dtype) for dtype in kinds] + [shape_of((1, D), FULL)] * with_term,
        (far(base), part, other, gain[None]) + tuple(near(item) for item in extra),
        table=own_half,
        after=after,
    )


def delta_kernel(a_ref, b_ref, c_ref, d_ref, out_ref):
    first = a_ref[...].astype(FULL) + b_ref[...].astype(FULL)
    out_ref[...] = (first + (c_ref[...].astype(FULL) + d_ref[...].astype(FULL))).astype(HALF)


def layer_delta(terms, after):
    rows = stepped(ROWS, D)
    half = terms[0].shape[0]
    return call(
        delta_kernel, (half // ROWS,), [rows] * 4, [rows], [shape_of((half, D), HALF)], terms, after=after
    )[0]


def stacked(values, order):
    high = values.astype(HALF).astype(FULL)
    low = values - high
    return jnp.concatenate([low if pick else high for pick in order], axis=0).astype(HALF)


def thin(factor, matrix, dims):
    result = mul(stacked(factor, (0, 1)), matrix.astype(HALF), dims)
    return result[:RANK] + result[RANK:]


def outer(left, right):
    return mul(stacked(left, (0, 0, 1, 1)), stacked(right, (0, 1, 0, 1)), TN)


def tile_of(size):
    return 256 if size % 256 == 0 else 128


def grad_kernel(flipped, thinned, lefts, rights, tab_ref, e_ref, f_ref, *refs):
    left_refs, right_refs, refs = refs[:lefts], refs[lefts : lefts + rights], refs[lefts + rights :]
    m_ref, right_scr = refs[0], refs[-1]
    depth = right_scr.shape[0] // rights
    for number, right in enumerate(right_refs):
        right_scr[number * depth : (number + 1) * depth, :] = right[...].astype(HALF)
    depth = right_scr.shape[0] // lefts
    total = e_ref[...]
    for number, left in enumerate(left_refs):
        total = total + mul(left[...], right_scr[number * depth : (number + 1) * depth, :])
    m_ref[...] = total
    p_ref = refs[1]
    if not thinned:
        p_ref[...] = jnp.zeros(p_ref.shape, FULL)
        return
    if flipped:
        p_ref[...] = thin(f_ref[...], total, NN)
    else:
        @pl.when(pl.program_id(0) == 0)
        def _():
            p_ref[...] = jnp.zeros(p_ref.shape, FULL)

        p_ref[...] += thin(f_ref[...], total, NT)


def merge_grad(table, lefts, rights, error, factor_t, flipped, thinned=True, after=()):
    height, width = error.shape
    tile = tile_of(width)
    by_col = lambda rows: pl.BlockSpec((rows, tile), lambda i, _: (0, i))
    rows = lefts[0][2] * len(lefts)
    depth = rows // len(rights)

    def left_spec(place, width):
        return pl.BlockSpec((height, width), lambda i, _: (0, place))

    def right_spec(place, given):
        return pl.BlockSpec((depth, tile), lambda i, tab: (tab[place] if given else place, i))

    p_shape = (RANK, width if flipped else height)
    p_spec = by_col(RANK) if flipped else made(*p_shape)
    if not thinned:
        p_shape = (RANK, 128)
        p_spec = made(*p_shape)
    return call(
        functools.partial(grad_kernel, flipped, thinned, len(lefts), len(rights)),
        (width // tile,),
        [by_col(height), whole(RANK, height) if flipped else by_col(RANK)]
        + [left_spec(place, size) for _, place, size in lefts]
        + [right_spec(place, given) for _, place, given in rights],
        [by_col(height), p_spec],
        [(far_shape if thinned else shape_of)((height, width), FULL), shape_of(p_shape, FULL)],
        (far(error), factor_t)
        + tuple(left[0] for left in lefts)
        + tuple(far(right[0]) if right[2] else right[0] for right in rights),
        scratch=[pltpu.VMEM((rows, tile), HALF)],
        table=table,
        flops=2 * height * width * rows,
        room=8,
        after=after,
    )


def error_kernel(e_ref, f_ref, p_ref):
    p_ref[...] = thin(f_ref[...], e_ref[...], NT)


def error_factor(error, factor_t, after):
    height, width = error.shape
    return call(
        error_kernel,
        (height // BLOCK,),
        [stepped(BLOCK, width), whole(RANK, width)],
        [stepped_col(RANK, BLOCK)],
        [shape_of((RANK, height), FULL)],
        (far(error), factor_t),
        after=after,
    )[0]


def first_kernel(e_ref, h_ref, *refs):
    p_ref = refs[-1]
    total, at = e_ref[...], 0
    for thin_ref in refs[:-1]:
        rows = thin_ref.shape[1]
        both = mul(stacked(thin_ref[...], (0, 1)), h_ref[:, at : at + rows], NT)
        total, at = total + both[:RANK] + both[RANK:], at + rows
    p_ref[...] = total


def first_factor(error_part, h_t, thins):
    return call(
        first_kernel,
        (1,),
        [whole(RANK, D), whole(*h_t.shape)] + [whole(*part.shape) for part in thins],
        [made(RANK, D)],
        [shape_of((RANK, D), FULL)],
        (error_part, h_t) + tuple(thins),
    )[0]


def orthonormal(block):
    rows = lax.broadcasted_iota(jnp.int32, block.shape, 0)
    for row_id in range(RANK):
        row = block[row_id : row_id + 1, :]
        inner = jnp.sum(block * row, axis=1, keepdims=True)
        inverse = lax.rsqrt(inner[row_id : row_id + 1, :] + 1e-12)
        finished = row * inverse
        later = block - (inner * inverse) * finished
        block = jnp.where(rows == row_id, finished, jnp.where(rows > row_id, later, block))
    return block


def second_kernel(flipped, workers, p_ref, m_ref, hat_ref, q_ref):
    step = pl.program_id(0)
    tile = m_ref.shape[0]

    @pl.when(step == 0)
    def _():
        hat_ref[...] = orthonormal(p_ref[...] / workers)
        if not flipped:
            q_ref[...] = jnp.zeros(q_ref.shape, FULL)

    if flipped:
        q_ref[...] = thin(hat_ref[...], m_ref[...], NT)
    else:
        q_ref[...] += thin(hat_ref[:, pl.ds(pl.multiple_of(step * tile, tile), tile)], m_ref[...], NN)


def second_factor(merged, p_sum, flipped, workers, after=()):
    height, width = merged.shape
    tile = tile_of(height)
    q_shape = (RANK, height if flipped else width)
    return call(
        functools.partial(second_kernel, flipped, workers),
        (height // tile,),
        [whole(RANK, D), pl.BlockSpec((tile, width), lambda i: (i, 0))],
        [made(RANK, D), pl.BlockSpec((RANK, tile), lambda i: (0, i)) if flipped else made(*q_shape)],
        [shape_of((RANK, D), FULL), shape_of(q_shape, FULL)],
        (p_sum, merged),
        flops=64 * height * width,
        after=after,
    )


def final_kernel(flipped, m_ref, hat_ref, q_ref, own_ref, moment_ref, weight_ref, err_ref, nw_ref, nm_ref):
    step = pl.program_id(0)
    tile = m_ref.shape[0]
    at = pl.ds(pl.multiple_of(step * tile, tile), tile)
    if flipped:
        err_ref[...] = m_ref[...] - outer(q_ref[:, at], hat_ref[...])
    else:
        err_ref[...] = m_ref[...] - outer(hat_ref[:, at], q_ref[...])

    @pl.when(step == 0)
    def _():
        if flipped:
            approx = outer(q_ref[...], own_ref[...])
        else:
            approx = outer(own_ref[...], q_ref[...])
        moment = MOMENTUM * moment_ref[...] + approx
        nm_ref[...] = moment
        nw_ref[...] = weight_ref[...] - STEP_RATE * moment


def final_update(merged, p_hat, q_new, p_own, moment, weight, flipped, after=()):
    height, width = merged.shape
    tile = tile_of(height)
    by_row = pl.BlockSpec((tile, width), lambda i: (i, 0))
    own, own_out = whole(*weight.shape), made(*weight.shape)
    return call(
        functools.partial(final_kernel, flipped),
        (height // tile,),
        [by_row, whole(*p_hat.shape), whole(*q_new.shape), whole(*p_own.shape), own, own],
        [by_row, own_out, own_out],
        [shape_of(merged.shape, FULL), shape_of(weight.shape, FULL), shape_of(weight.shape, FULL)],
        (merged, p_hat, q_new, p_own, moment, weight),
        flops=64 * height * width,
        after=after,
    )


def spread_kernel(steps, tab_ref, base_ref, theirs_ref, mine_ref, *refs):
    out_ref, step = refs[-1], pl.program_id(0)

    @pl.when(step < steps // 2)
    def _():
        out_ref[...] = base_ref[...] + theirs_ref[...].astype(FULL)

    @pl.when(step >= steps // 2)
    def _():
        out_ref[...] = base_ref[...] + mine_ref[...].astype(FULL)


def spread(table, base, pieces, before, after=()):
    half = pieces[0].shape[0]
    extra = [] if before is None else [far(before)]
    rows = pl.BlockSpec((half, D), lambda i, tab: (tab[i], 0))
    return call(
        functools.partial(spread_kernel, 2),
        (2,),
        [rows, whole(half, D), whole(half, D)] + [pl.BlockSpec(memory_space=pl.ANY)] * len(extra),
        [rows],
        [far_shape(base.shape, FULL)],
        [far(base)] + list(pieces) + extra,
        table=table,
        aliases={4: 0} if extra else None,
        after=after,
    )[0]


def add_kernel(a_ref, b_ref, out_ref):
    out_ref[...] = a_ref[...] + b_ref[...]


def butterfly_step(values, axis, count, span, after=()):
    if span >= count:
        return values
    other = lax.ppermute(values, axis, [(i, i ^ span) for i in range(count)])
    spec = whole(*values.shape)
    return call(
        add_kernel, (1,), [spec, spec], [made(*values.shape)], [shape_of(values.shape, FULL)], (values, other), after=after
    )[0]


def to_core_mate(values, count):
    return lax.ppermute(values, "tensor", [(i, i ^ 1) for i in range(count)])


def chip_kernel(keep_ref, other_ref, out_ref):
    out_ref[...] = (keep_ref[...] + other_ref[...].astype(FULL)).astype(HALF)


def chip_sum(send, keep, count, after=()):
    rows = stepped(BLOCK, D)
    return call(
        chip_kernel, (send.shape[0] // BLOCK,), [rows, rows], [rows], [shape_of(send.shape, HALF)],
        (keep, to_core_mate(send, count)), after=after,
    )[0]


def across_chips(part, count):
    span = 2
    while True:
        other = lax.ppermute(part, "tensor", [(i, i ^ span) for i in range(count)])
        span *= 2
        if span >= count:
            return part, other
        part = (part.astype(FULL) + other.astype(FULL)).astype(HALF)


def pieces_of(own, count):
    return to_core_mate(own, count), own


def local(
    hidden_in,
    seg_ids,
    token_mask,
    out_grad,
    proj_qkv,
    proj_out,
    proj_gate_up,
    proj_down,
    gains,
    moment_qkv,
    moment_out,
    moment_gate_up,
    moment_down,
    error_qkv,
    error_out,
    error_gate_up,
    error_down,
    factor_qkv,
    factor_out,
    factor_gate_up,
    factor_down,
    gain_moment,
):
    parts = lax.axis_size("tensor")
    workers = lax.axis_size("dp")
    rows = hidden_in.shape[0]
    q_heads = QUERY_HEADS // parts
    kv_heads = KEY_VALUE_HEADS // parts
    group = QUERY_HEADS // KEY_VALUE_HEADS
    half = rows // CHUNKS // 2
    order = list(range(CHUNKS))[::-1]
    first_own = jnp.concatenate([proj_qkv, proj_out.T], axis=1).astype(HALF)
    second_own = jnp.concatenate([proj_gate_up, proj_down.T], axis=1).astype(HALF)
    first_pieces, first_steps = ring_gather(first_own, workers)
    shard_places = ring_places(workers, first_own.shape[0])
    g_att = gains[:D]
    g_mlp = gains[D : 2 * D]
    g_query = gains[2 * D : 2 * D + HEAD_SIZE]
    g_key = gains[2 * D + HEAD_SIZE :]
    cosine, sine = rope_tables(rows)

    core = lax.axis_index("tensor") % 2
    seg_row, seg_col = seg_ids, seg_ids[0][:, None]
    key_row = jnp.where(token_mask == 1, seg_ids, -1)
    key_col = key_row[0][:, None]
    starts = jnp.sum(
        (seg_ids[0][None, :] < seg_ids[0][::BLOCK][:, None]).astype(jnp.int32), axis=1
    ) // BLOCK
    tables, half_tables = [], []
    each = half // BLOCK
    for chunk in range(CHUNKS):
        places = [2 * chunk + 1 - core, 2 * chunk + core]
        half_tables.append(jnp.stack(places).astype(jnp.int32))
        numbers = jnp.stack([place * each + i for place in places for i in range(each)]).astype(jnp.int32)
        tables.append(jnp.concatenate([numbers, starts[numbers]]))
    all_halves = jnp.concatenate([half_tables[chunk] for chunk in order])

    own_half = [table[1:] for table in half_tables]

    factors_t = [factor.T for factor in (factor_qkv, factor_out, factor_gate_up, factor_down)]
    h_att = input_norm(hidden_in, g_att)
    first_b, queries, keys, values, keys_t, raw_q, raw_k = make_qkv(
        shard_places, h_att, first_pieces, g_query, g_key, cosine, sine, q_heads, kv_heads, ()
    )
    second_b = lax.all_gather(stage(second_own, first_steps[-2] + (far(cosine), far(sine), far(key_col), shard_places) + tuple(tables)), "dp", axis=0, tiled=True)

    att, att_t, log_total, att_sum, resid, h_pieces = {}, {}, {}, {}, {}, {}
    after, arrived = (), ()
    for chunk in order:
        att[chunk], att_t[chunk], log_total[chunk] = attend(
            chunk, tables[chunk], queries, keys, values, seg_col, key_row, group, after
        )
        if chunk == order[-1]:
            error_part = error_factor(error_qkv[0], factors_t[0], (log_total[chunk],))
            h_t = turned(h_att, (error_part,))
            arrived = arrived + (far(h_t),)
        part = chip_sum(*project(att[chunk], near(first_b), 2, arrived), parts)
        after = (part,)
        att_sum[chunk] = across_chips(part, parts)
        arrived = att_sum[chunk][1:]
        resid[chunk], h_own = norm_rows(
            mid_kernel, own_half[chunk], hidden_in, *att_sum[chunk], g_mlp, (), (FULL, HALF), 0
        )
        h_pieces[chunk] = pieces_of(h_own, parts)

    two = [(chunk, place) for chunk in order for place in (0, 1)]
    size = 2 * half
    h_mlp_t, activ, activ_t, d_gu, mid_sum, mlp_part, mlp_sum = {}, {}, {}, {}, {}, {}, {}
    arrived = ()
    for chunk in order:
        h_mlp_t[chunk], activ[chunk], activ_t[chunk], d_gu[chunk] = feed_forward(
            half_tables[chunk], out_grad, second_b, h_pieces[chunk], after
        )
        if chunk == order[-1]:
            merged_down, p_down = merge_grad(
                all_halves,
                [(activ_t[other], 0, size) for other in order],
                [(out_grad, number, True) for number in range(len(two))],
                error_down[0], factors_t[3], True,
            )
            mlp_part[order[0]] = project(activ[order[0]], second_b, 2, (p_down,))
            arrived = arrived + mlp_part[order[0]][:1]
        part = chip_sum(*project(d_gu[chunk], second_b, 0, arrived), parts)
        after = (part,)
        mid_sum[chunk] = across_chips(part, parts)
        arrived = mid_sum[chunk][1:]

    merged_gu, p_gu = merge_grad(
        all_halves,
        [(h_mlp_t[chunk], 0, size) for chunk in order],
        [(d_gu[chunk], 0, False) for chunk in order],
        error_gate_up[0], factors_t[2], False, after=after,
    )
    after = (p_gu,)
    for chunk in order[1:]:
        mlp_part[chunk] = project(activ[chunk], second_b, 2, after, far_shape)
        after = mlp_part[chunk][:1]
    branch_pieces, mid_delta = {}, {}
    term_mlp = jnp.zeros((1, D), FULL)
    for chunk in order:
        mid_delta[chunk], d_branch, more = norm_rows(
            mid_back_kernel, own_half[chunk], out_grad, *mid_sum[chunk], g_mlp, (resid[chunk],), (FULL, HALF), 1,
            after if chunk == order[-1] else (),
        )
        term_mlp = term_mlp + more
        branch_pieces[chunk] = pieces_of(d_branch, parts)
    after = (d_branch,)
    mlp_sum[order[0]] = across_chips(chip_sum(*mlp_part[order[0]], parts, (p_gu,)), parts)
    d_raw, thins, in_sum = {}, {}, {}
    later = ()
    term_q, term_k = (jnp.zeros((1, HEAD_SIZE), FULL) for _ in range(2))
    deltas = {}
    arrived = ()
    for chunk in order:
        raw_q_back, more_q, d_keys, d_values = attend_back(
            chunk, tables[chunk], queries, keys, values, keys_t, seg_row, key_col, first_b, att[chunk],
            log_total[chunk], raw_q, g_query, cosine, sine, branch_pieces[chunk], later, group, after
        )
        later = (d_keys, d_values)
        if chunk == order[0]:
            deltas[chunk] = layer_delta(att_sum[chunk] + mlp_sum[chunk], later)
            arrived = (deltas[chunk],)
        d_raw[chunk], thins[chunk], more_k, send, keep = raw_back(
            chunk, half_tables[chunk], raw_q_back, d_keys, d_values, raw_k, g_key, cosine, sine, first_b,
            factors_t[0], arrived
        )
        term_q, term_k = term_q + more_q, term_k + more_k
        part = chip_sum(send, keep, parts)
        after = (part,)
        in_sum[chunk] = across_chips(part, parts)
        arrived = in_sum[chunk][1:]
        if chunk == order[0]:
            merged_out, p_out = merge_grad(
                all_halves,
                [(att_t[other], 0, size) for other in order],
                [(branch_pieces[other][place], 0, False) for other, place in two],
                error_out[0], factors_t[1], True, after=after,
            )
            after = (p_out,)

    p_qkv = first_factor(error_part, h_t, [thins[chunk] for chunk in range(CHUNKS)])
    for chunk in order[1:]:
        mlp_sum[chunk] = across_chips(chip_sum(*mlp_part[chunk], parts, after), parts)
    after = after + (p_qkv,)
    term_att = jnp.zeros((1, D), FULL)
    in_delta = {}
    for chunk in order[:-1]:
        in_delta[chunk], more = norm_rows(
            in_back_kernel, own_half[chunk], hidden_in, *in_sum[chunk], g_att, (mid_delta[chunk],), (HALF,), 1, after
        )
        term_att = term_att + more
    p_all = jnp.concatenate([p_down, p_gu, p_out, p_qkv], axis=1)
    p_all = butterfly_step(p_all, "dp", workers, 1, tuple(in_delta.values()))
    merged_qkv, token = merge_grad(
        all_halves,
        [(h_t, chunk, size) for chunk in order],
        [(d_raw[chunk], 0, False) for chunk in order],
        error_qkv[0], factors_t[0], False, False, (p_all,),
    )
    p_all = butterfly_step(p_all, "dp", workers, 2, (token,))
    layer_out = spread(
        half_tables[order[0]], hidden_in, pieces_of(deltas[order[0]], parts), None, (p_all,)
    )
    p_all = butterfly_step(p_all, "dp", workers, 4, (far(layer_out),))
    p_all = butterfly_step(p_all, "dp", workers, 8)
    in_delta[order[-1]], more = norm_rows(
        in_back_kernel, own_half[order[-1]], hidden_in, *in_sum[order[-1]], g_att, (mid_delta[order[-1]],), (HALF,),
        1, (p_all,),
    )
    term_att = term_att + more
    hat_down, q_down = second_factor(merged_down, p_all[:, :D], True, workers)
    hat_gu, q_gu = second_factor(merged_gu, p_all[:, D : 2 * D], False, workers)
    hat_out, q_out = second_factor(merged_out, p_all[:, 2 * D : 3 * D], True, workers)
    hat_qkv, q_qkv = second_factor(merged_qkv, p_all[:, 3 * D :], False, workers)
    share = 2.0 / parts
    gain_terms = jnp.concatenate(
        [term_att[0] * share, term_mlp[0] * share, term_q[0], term_k[0]]
    ).reshape(RANK, -1)
    q_all = jnp.concatenate([q_down, q_gu, q_out, q_qkv, gain_terms], axis=1)
    cuts = [0]
    for part in (q_down, q_gu, q_out, q_qkv, gain_terms):
        cuts.append(cuts[-1] + part.shape[1])
    after = (q_down, q_gu, q_out, q_qkv)
    input_grad = spread(
        half_tables[order[0]], out_grad, pieces_of(in_delta[order[0]], parts), None, after
    )
    q_all = butterfly_step(q_all, "dp", workers, 1, (far(input_grad),))
    for chunk in order[1:]:
        input_grad = spread(
            half_tables[chunk], out_grad, pieces_of(in_delta[chunk], parts), input_grad, (q_all,)
        )
        deltas[chunk] = layer_delta(att_sum[chunk] + mlp_sum[chunk], (far(input_grad),))
    q_all = butterfly_step(q_all, "dp", workers, 2, (far(input_grad),))
    q_all = butterfly_step(q_all, "dp", workers, 4)
    q_all = butterfly_step(q_all, "dp", workers, 8) / workers
    for chunk in order[1:]:
        layer_out = spread(half_tables[chunk], hidden_in, pieces_of(deltas[chunk], parts), layer_out)
    gain_grad = q_all[:, cuts[4] :]
    for span in (1, 2, 4):
        gain_grad = butterfly_step(gain_grad, "tensor", parts, span)
    new_gain_moment = MOMENTUM * gain_moment + gain_grad.reshape(-1)
    new_gains = gains - GAIN_RATE * new_gain_moment

    own_count = D // workers
    results = {}
    for number, (name, merged, p_hat, moment, weight, flipped) in enumerate((
        ("down", merged_down, hat_down, moment_down, proj_down, True),
        ("gu", merged_gu, hat_gu, moment_gate_up, proj_gate_up, False),
        ("out", merged_out, hat_out, moment_out, proj_out, True),
        ("qkv", merged_qkv, hat_qkv, moment_qkv, proj_qkv, False),
    )):
        q_new = q_all[:, cuts[number] : cuts[number + 1]]
        p_own = lax.dynamic_slice_in_dim(p_hat, lax.axis_index("dp") * own_count, own_count, 1)
        new_error, new_weight, new_moment = final_update(
            merged, p_hat, q_new, p_own, moment, weight, flipped
        )
        results[name] = (new_weight, new_moment, new_error[None], q_new.T)
    ordered = [results[name] for name in ("qkv", "out", "gu", "down")]
    return (
        (layer_out, input_grad)
        + tuple(r[0] for r in ordered)
        + tuple(r[1] for r in ordered)
        + tuple(r[2] for r in ordered)
        + tuple(r[3] for r in ordered)
        + (new_gains, new_gain_moment)
    )


def solution(mesh):
    in_specs = (
        P("dp", None),
        P("dp", None),
        P("dp", None),
        P("dp", None),
        P("dp", "tensor"),
        P("tensor", "dp"),
        P("dp", "tensor"),
        P("tensor", "dp"),
        P(),
        P("dp", "tensor"),
        P("tensor", "dp"),
        P("dp", "tensor"),
        P("tensor", "dp"),
        P("dp", None, "tensor"),
        P("dp", "tensor", None),
        P("dp", None, "tensor"),
        P("dp", "tensor", None),
        P("tensor", None),
        P("tensor", None),
        P("tensor", None),
        P("tensor", None),
        P(),
    )
    out_specs = (
        P("dp", None),
        P("dp", None),
        P("dp", "tensor"),
        P("tensor", "dp"),
        P("dp", "tensor"),
        P("tensor", "dp"),
        P("dp", "tensor"),
        P("tensor", "dp"),
        P("dp", "tensor"),
        P("tensor", "dp"),
        P("dp", None, "tensor"),
        P("dp", "tensor", None),
        P("dp", None, "tensor"),
        P("dp", "tensor", None),
        P("tensor", None),
        P("tensor", None),
        P("tensor", None),
        P("tensor", None),
        P(),
        P(),
    )
    return jax.shard_map(local, mesh=mesh, in_specs=in_specs, out_specs=out_specs, check_vma=False)
```

time: 1760 us -> 380 us (0.22)
  waiting for transfers between devices: 774 us -> 60.8 us
  other arithmetic: 428 us -> 10.3 us
  matrix products: 395 us -> 0 us
  Pallas kernels: 0 us -> 236 us
  local copies, waits for them, and re-layouts: 60.4 us -> 19.6 us
  blocking collectives: 39.5 us -> 0 us
  starting transfers between devices: 1.13 us -> 30.7 us
  between operations: 36.8 us -> 15.7 us
    psum x5 -> x0, waiting for transfers between devices: 646 us -> none  [the longest x3 526 us: tensor_total(): return lax.psum(partial_sum, 'tensor')]
    dot_general x56 -> x0, matrix products: 395 us -> none  [the longest x8 56 us: block_scores(): jnp.einsum('cwbn,zwn->wbcz', query_block, key_head_rows, preferred_elemen...]
    pallas_call x0 -> x60, Pallas kernels: none -> 236 us  [call(): pl.pallas_call(body, grid_spec=pltpu.PrefetchScalarGridSpec(num_scalar_pr...]
    reduce_sum x76 -> x1, other arithmetic: 214 us -> 0.9 us  [local(): jnp.sum((seg_ids[0][None, :] < seg_ids[0][::BLOCK][:, None]).astype(jnp.i...]
    all_gather x4 -> x1, waiting for transfers between devices: 128 us -> 0.01 us  [local(): lax.all_gather(stage(second_own, first_steps[-2] + (far(cosine), far(sine...]
    mul x6 -> x2, other arithmetic: 75.8 us -> 0.02 us  [the longest x1 0.01 us: local(): term_att[0] * share]
    ppermute x0 -> x40, waiting for transfers between devices: none -> 60.8 us  [the longest x8 22.4 us: across_chips(): other = lax.ppermute(part, 'tensor', [(i, i ^ span) for i in range(count)])]
    convert_element_type x8 -> x0, other arithmetic: 53.6 us -> none  [the longest x4 48.7 us: block_backward(): score_gradient = (probabilities * (d_probs - jnp.sum(probabilities * d_pr...]
  transfers between devices with their start and end apart: 9 -> 41, of which waited for: 8 -> 19; matrix products, arithmetic and copies ran while one was open for 14% -> 4% of each run, Pallas kernels for 0% -> 57%
where the time goes in v1:
time: 380 us; the launch traced here: 374 us
  Pallas kernels  236 us (62%)
  waiting for transfers between devices  60.8 us (16%)
  starting transfers between devices  30.7 us (8%)
  local copies, waits for them, and re-layouts  19.6 us (5%)
  between operations  15.7 us (4%)
  other arithmetic  10.3 us (3%)
    pallas_call x60, Pallas kernels, call(): pl.pallas_call(body, grid_spec=pltpu.PrefetchScalarGridSpec(num_scalar_pr...  236 us
    ppermute x8, waiting for transfers between devices, across_chips(): other = lax.ppermute(part, 'tensor', [(i, i ^ span) for i in range(count)])  22.4 us
    ppermute x4, waiting for transfers between devices, ring_step(): lax.ppermute(from_left, 'dp', ahead)  20.9 us
    unnamed x196, local copies, waits for them, and re-layouts  11.9 us
    ppermute x8, starting transfers between devices, across_chips(): other = lax.ppermute(part, 'tensor', [(i, i ^ span) for i in range(count)])  11.4 us
    ppermute x4, starting transfers between devices, ring_step(): lax.ppermute(from_left, 'dp', ahead)  7.92 us
  transfers between devices with their start and end apart: 41, of which 19 were waited for; matrix products, arithmetic and copies ran while one was open for 4% of the time, Pallas kernels for 57%

profile of v1, /device:TPU:0, one launch (start us, length us, event | category | flops | bytes accessed | tf_op | source)
XLA Modules:
  0.0 373.6 jit_solution(4511751688098938965)
XLA Ops:
  10.2 3.0 collective-permute-start
  14.9 3.9 %fusion.2 = (f32[2048,64]{1,0:T(8,128)S(1)}, f32[2048,64]{1,0:T(8,128)S(1)}, f32[2048,64]{1,0:T(8,128)S(1)}) fusion(f32[64]{0:T(128)S(1)} %negate_power_fusion), kind=kLoop, calls=%fused_computation.8 | loop fusion | flops 262144 | bytes 1573120 | tf_op jit(solution)/shard_map/neg | solution.py:124
  19.6 1.9 pad_maximum_fusion
  22.6 1.8 collective-permute-start.2
  24.6 8.4 %collective-permute-done.2.refs_9_ = bf16[128,1536]{1,0:T(8,128)(2,1)S(1)} collective-permute-done((bf16[128,1536]{1,0:T(8,128)(2,1)}, bf16[128,1536]{1,0:T(8,128)(2,1)S(1)}, u32[]{:S(2)}, u32[]{:S(2)}) %collective-permute-start.2) | collective-permute-done | bytes 393248 | tf_op jit(solution)/shard_map/ppermute | solution.py:138
  38.3 4.1 %collective-permute-done.4.refs_11_.refs_1_ = bf16[128,1536]{1,0:T(8,128)(2,1)S(1)} collective-permute-done((bf16[128,1536]{1,0:T(8,128)(2,1)S(1)}, bf16[128,1536]{1,0:T(8,128)(2,1)S(1)}, u32[]{:S(2)}, u32[]{:S(2)}) %collective-permute-start.4) | collective-permute-done | bytes 393248 | tf_op jit(solution)/shard_map/ppermute | solution.py:138
  45.6 6.3 %shard_map.374.refs_1_.refs_0_ = bf16[2048,1024]{1,0:T(8,128)(2,1)S(1)} custom-call(f32[2048,1024]{1,0:T(8,128)} %refs_1_.23, f32[1,1024]{1,0:T(1,128)S(1)} %bitcast.82), custom_call_target="tpu_custom_call" | custom-call | bytes 12587008 | tf_op jit(solution)/shard_map/pallas_call | solution.py:90
  52.0 1.6 collective-permute-start.6
  54.6 7.2 %collective-permute-done.6.refs_13_ = bf16[64,1536]{1,0:T(8,128)(2,1)S(1)} collective-permute-done((bf16[64,1536]{1,0:T(8,128)(2,1)S(1)}, bf16[64,1536]{1,0:T(8,128)(2,1)S(1)}, u32[]{:S(2)}, u32[]{:S(2)}) %collective-permute-start.6) | collective-permute-done | bytes 196640 | tf_op jit(solution)/shard_map/ppermute | solution.py:138
  61.8 6.3 %collective-permute-done.7.refs_14_ = bf16[64,1536]{1,0:T(8,128)(2,1)S(1)} collective-permute-done((bf16[64,1536]{1,0:T(8,128)(2,1)S(1)}, bf16[64,1536]{1,0:T(8,128)(2,1)S(1)}, u32[]{:S(2)}, u32[]{:S(2)}) %collective-permute-start.7) | collective-permute-done | bytes 196640 | tf_op jit(solution)/shard_map/ppermute | solution.py:138
  68.8 12.6 %shard_map.375 = (bf16[1024,1536]{1,0:T(8,128)(2,1)S(1)}, bf16[2048,512]{1,0:T(8,128)(2,1)S(1)}, bf16[2048,256]{1,0:T(8,128)(2,1)S(1)}, bf16[2048,512]{1,0:T(8,1...) custom-call(s32[9]{0:T(128)S(1)} %copy-done.69, ...), custom_call_target="tpu_custom_call" | custom-call | flops 4294967296 | bytes 25166848 | tf_op jit(solution)/shard_map/pallas_call | solution.py:90
  81.4 11.3 %shard_map.376 = (bf16[1024,512]{1,0:T(8,128)(2,1)S(1)}, bf16[512,1024]{1,0:T(8,128)(2,1)}, f32[4,1024]{1,0:T(4,128)S(1)}) custom-call(s32[8]{0:T(128)S(1)} %copy-done.67, bf16[2048,512]{1,0:T(8,128)(2,1)S(1)} %get-tuple-element.113.refs_1_, bf16[2048,256]{1,0:T(8,128)(2,1)S(1)} %get-tuple-element.114.refs_2_, ...), custom_call_target="tpu_custom_call" | custom-call | flops 3221225472 | bytes 7372800 | tf_op jit(solution)/shard_map/pallas_call | solution.py:90
  92.8 1.8 shard_map.377
  94.7 2.6 collective-permute-done.8.refs_1_
  97.6 1.5 collective-permute-start.9
  99.1 9.1 %shard_map.379 = (bf16[1024,512]{1,0:T(8,128)(2,1)S(1)}, bf16[512,1024]{1,0:T(8,128)(2,1)}, f32[4,1024]{1,0:T(4,128)S(1)}) custom-call(s32[8]{0:T(128)S(1)} %copy-done.63, bf16[2048,512]{1,0:T(8,128)(2,1)S(1)} %get-tuple-element.113.refs_1_, bf16[2048,256]{1,0:T(8,128)(2,1)S(1)} %get-tuple-element.114.refs_2_, ...), custom_call_target="tpu_custom_call" | custom-call | flops 3221225472 | bytes 7372800 | tf_op jit(solution)/shard_map/pallas_call | solution.py:90
  108.2 3.8 %shard_map.380.refs_1_.refs_0_ = f32[8,1024]{1,0:T(8,128)S(1)} custom-call(f32[1024,1024]{1,0:T(8,128)} %bitcast.89, f32[8,1024]{1,0:T(8,128)S(1)} %bitcast.71, f32[4,1024]{1,0:T(4,128)S(1)} %get-tuple-element.121.refs_2_.refs_9_), custom_call_target="tpu_custom_call" | custom-call | bytes 4259840 | tf_op jit(solution)/shard_map/pallas_call | solution.py:90
  111.9 4.2 %shard_map.381.refs_3_.refs_1_.refs_4_ = bf16[1024,2048]{1,0:T(8,128)(2,1)} custom-call(bf16[2048,1024]{1,0:T(8,128)(2,1)S(1)} %shard_map.374.refs_1_.refs_0_, f32[8,1024]{1,0:T(8,128)S(1)} %shard_map.380.refs_1_.refs_0_), custom_call_target="tpu_custom_call" | custom-call | bytes 8388608 | tf_op jit(solution)/shard_map/pallas_call | solution.py:90
  116.1 6.7 %collective-permute-done.9.refs_2_.refs_3_.refs_1_ = bf16[512,1024]{1,0:T(8,128)(2,1)S(1)} collective-permute-done((bf16[512,1024]{1,0:T(8,128)(2,1)S(1)}, bf16[512,1024]{1,0:T(8,128)(2,1)S(1)}, u32[]{:S(2)}, u32[]{:S(2)}) %collective-permute-start.9) | collective-permute-done | bytes 1048608 | tf_op jit(solution)/shard_map/ppermute | solution.py:909
  122.8 1.8 shard_map.382
  124.7 1.9 shard_map.386
  131.1 2.3 copy-done.1
  133.4 8.8 %shard_map.387 = (bf16[1024,1024]{1,0:T(8,128)(2,1)S(1)}, bf16[1024,768]{1,0:T(8,128)(2,1)S(1)}, bf16[768,1024]{1,0:T(8,128)(2,1)S(1)}, bf16[1024,1536]{1,0:T(8,128)(2,1)S(1)}) custom-call(s32[2]{0:T(128)S(1)} %pad_add_fusion.1.refs_0_, f32[2048,1024]{1,0:T(8,128)} %refs_1_.22, bf16[512,1024]{1,0:T(8,128)(2,1)} %collective-permute-done.13.refs_2_, ...), custom_call_target="tpu_custom_call" | custom-call | flops 4831838208 | bytes 23592960 | tf_op jit(solution)/shard_map/pallas_call | solution.py:90
  142.2 4.1 %shard_map.388 = (bf16[512,1024]{1,0:T(8,128)(2,1)S(1)}, f32[512,1024]{1,0:T(8,128)S(1)}) custom-call(bf16[1024,1536]{1,0:T(8,128)(2,1)S(1)} %get-tuple-element.126.refs_0_.refs_5_, bf16[1024,2304]{1,0:T(8,128)(2,1)S(1)} %copy-done.1), custom_call_target="tpu_custom_call" | custom-call | flops 3221225472 | bytes 11010048 | tf_op jit(solution)/shard_map/pallas_call | solution.py:90
  146.6 8.6 %collective-permute-done.11.refs_3_.refs_1_ = bf16[512,1024]{1,0:T(8,128)(2,1)} collective-permute-done((bf16[512,1024]{1,0:T(8,128)(2,1)}, bf16[512,1024]{1,0:T(8,128)(2,1)}, u32[]{:S(2)}, u32[]{:S(2)}) %collective-permute-start.11) | collective-permute-done | bytes 1048608 | tf_op jit(solution)/shard_map/ppermute | solution.py:909
  155.1 2.5 shard_map.384
  161.4 8.9 %shard_map.390 = (bf16[1024,1024]{1,0:T(8,128)(2,1)S(1)}, bf16[1024,768]{1,0:T(8,128)(2,1)S(1)}, bf16[768,1024]{1,0:T(8,128)(2,1)S(1)}, bf16[1024,1536]{1,0:T(8,128)(2,1)S(1)}) custom-call(s32[2]{0:T(128)S(1)} %pad_add_fusion.refs_0_, f32[2048,1024]{1,0:T(8,128)} %refs_1_.22, bf16[512,1024]{1,0:T(8,128)(2,1)} %copy-done.83, bf16[512,1024]{1,0:T(8,128)(2,1)} %copy-done.71, ...), custom_call_target="tpu_custom_call" | custom-call | flops 4831838208 | bytes 23592960 | tf_op jit(solution)/shard_map/pallas_call | solution.py:90
  170.4 10.0 %shard_map.391 = (f32[768,1024]{1,0:T(8,128)}, f32[8,1024]{1,0:T(8,128)S(1)}) custom-call(s32[4]{0:T(128)S(1)} %pad_add_fusion.2.refs_0_, f32[768,1024]{1,0:T(8,128)} %bitcast.91, f32[8,768]{1,0:T(8,128)S(1)} %bitcast.86, bf16[768,1024]{1,0:T(8,128)(2,1)S(1)} %get-tuple-element.134.refs_3_, bf16[768,1024]{1,0:T(8,128)(2,1)S(1)} %get-tuple-element.135.refs_4_, ...), custom_call_target="tpu_custom_call" | custom-call | flops 3221225472 | bytes 43048960 | tf_op jit(solution)/shard_map/pallas_call | solution.py:90
  180.4 2.4 shard_map.392
  183.6 4.1 %shard_map.393 = (bf16[512,1024]{1,0:T(8,128)(2,1)S(1)}, f32[512,1024]{1,0:T(8,128)S(1)}) custom-call(bf16[1024,1536]{1,0:T(8,128)(2,1)S(1)} %copy-done.74, bf16[1024,2304]{1,0:T(8,128)(2,1)S(1)} %bitcast.70, bf16[512,1024]{1,0:T(8,128)(2,1)S(1)} %collective-permute-done.15.refs_2_.refs_3_, bf16[512,1024]{1,0:T(8,128)(2,1)S(1)} %get-tuple-element.137.refs_3_), custom_call_target="tpu_custom_call" | custom-call | flops 3221225472 | bytes 11010048 | tf_op jit(solution)/shard_map/pallas_call | solution.py:90
  188.3 2.6 shard_map.398
  191.4 1.5 collective-permute-start.18
  193.0 13.2 %shard_map.395 = (f32[1024,1536]{1,0:T(8,128)}, f32[8,1024]{1,0:T(8,128)S(1)}) custom-call(s32[4]{0:T(128)S(1)} %pad_add_fusion.2.refs_0_, f32[1024,1536]{1,0:T(8,128)} %bitcast.97, f32[8,1536]{1,0:T(8,128)S(1)} %bitcast.88, bf16[1024,1024]{1,0:T(8,128)(2,1)S(1)} %copy-done.76, bf16[1024,1024]{1,0:T(8,128)(2,1)S(1)} %copy-done.78, ...), custom_call_target="tpu_custom_call" | custom-call | flops 6442450944 | bytes 23150592 | tf_op jit(solution)/shard_map/pallas_call | solution.py:90
  206.4 1.5 collective-permute-start.22
  207.9 3.7 shard_map.396
  211.6 5.8 %collective-permute-done.18.refs_3_ = bf16[512,1024]{1,0:T(8,128)(2,1)S(1)} collective-permute-done((bf16[512,1024]{1,0:T(8,128)(2,1)S(1)}, bf16[512,1024]{1,0:T(8,128)(2,1)S(1)}, u32[]{:S(2)}, u32[]{:S(2)}) %collective-permute-start.18) | collective-permute-done | bytes 1048608 | tf_op jit(solution)/shard_map/ppermute | solution.py:909
  217.4 2.7 shard_map.397
  221.5 20.8 %shard_map.399 = (bf16[1024,512]{1,0:T(8,128)(2,1)S(1)}, f32[1,128]{1,0:T(1,128)S(1)}, f32[2048,256]{1,0:T(8,128)S(1)}, f32[2048,256]{1,0:T(8,128)S(1)}) custom-call(s32[8]{0:T(128)S(1)} %copy-done.67, bf16[2048,512]{1,0:T(8,128)(2,1)S(1)} %copy-done.16, bf16[2048,256]{1,0:T(8,128)(2,1)S(1)} %copy-done.30, bf16[2048,512]{1,0:T(8,128)(2,1)S(1)} %copy-done.18, ...), custom_call_target="tpu_custom_call" | custom-call | flops 6442450944 | bytes 24151040 | tf_op jit(solution)/shard_map/pallas_call | solution.py:90
  242.9 7.2 %shard_map.402 = (bf16[1024,1024]{1,0:T(8,128)(2,1)S(1)}, f32[8,1024]{1,0:T(8,128)S(1)}, f32[1,128]{1,0:T(1,128)S(1)}, bf16[512,1024]{1,0:T(8,128)(2,1)S(1)}, f32[512,1024]{1,0:T(8,128)S(1)}) custom-call(s32[2]{0:T(128)S(1)} %pad_add_fusion.1.refs_0_, bf16[1024,512]{1,0:T(8,128)(2,1)S(1)} %get-tuple-element.154.refs_1_, ...), custom_call_target="tpu_custom_call" | custom-call | flops 2147483648 | bytes 17892352 | tf_op jit(solution)/shard_map/pallas_call | solution.py:90
  250.6 2.1 collective-permute-done.23.refs_1_
  253.1 1.5 collective-permute-start.24
  255.0 6.2 %shard_map.404 = (f32[512,1024]{1,0:T(8,128)}, f32[8,1024]{1,0:T(8,128)S(1)}) custom-call(s32[4]{0:T(128)S(1)} %pad_add_fusion.2.refs_0_, f32[512,1024]{1,0:T(8,128)} %bitcast.92, f32[8,512]{1,0:T(8,128)S(1)} %bitcast.87, bf16[512,1024]{1,0:T(8,128)(2,1)S(1)} %copy-done.31, bf16[512,1024]{1,0:T(8,128)(2,1)S(1)} %copy-done.32, ...), custom_call_target="tpu_custom_call" | custom-call | flops 2147483648 | bytes 10534912 | tf_op jit(solution)/shard_map/pallas_call | solution.py:90
  261.2 16.7 %shard_map.405 = (bf16[1024,512]{1,0:T(8,128)(2,1)S(1)}, f32[1,128]{1,0:T(1,128)S(1)}, f32[1024,256]{1,0:T(8,128)S(1)}, f32[1024,256]{1,0:T(8,128)S(1)}) custom-call(s32[8]{0:T(128)S(1)} %copy-done.63, bf16[2048,512]{1,0:T(8,128)(2,1)S(1)} %copy-done.16, bf16[2048,256]{1,0:T(8,128)(2,1)S(1)} %copy-done.30, bf16[2048,512]{1,0:T(8,128)(2,1)S(1)} %copy-done.18, ...), custom_call_target="tpu_custom_call" | custom-call | flops 6442450944 | bytes 26248192 | tf_op jit(solution)/shard_map/pallas_call | solution.py:90
  278.4 7.6 %shard_map.406 = (bf16[1024,1024]{1,0:T(8,128)(2,1)S(1)}, f32[8,1024]{1,0:T(8,128)S(1)}, f32[1,128]{1,0:T(1,128)S(1)}, bf16[512,1024]{1,0:T(8,128)(2,1)S(1)}, f32[512,1024]{1,0:T(8,128)S(1)}) custom-call(s32[2]{0:T(128)S(1)} %pad_add_fusion.refs_0_, bf16[1024,512]{1,0:T(8,128)(2,1)S(1)} %get-tuple-element.160.refs_1_, ...), custom_call_target="tpu_custom_call" | custom-call | flops 2147483648 | bytes 15795200 | tf_op jit(solution)/shard_map/pallas_call | solution.py:90
  289.0 1.5 collective-permute-start.27
  290.5 3.4 shard_map.410
  294.1 7.5 %shard_map.412 = (f32[1024,1024]{1,0:T(8,128)S(1)}, f32[8,128]{1,0:T(8,128)S(1)}) custom-call(s32[4]{0:T(128)S(1)} %pad_add_fusion.2.refs_0_, f32[1024,1024]{1,0:T(8,128)} %bitcast.90, f32[8,1024]{1,0:T(8,128)S(1)} %bitcast.74, bf16[1024,2048]{1,0:T(8,128)(2,1)S(1)} %copy-done, bf16[1024,2048]{1,0:T(8,128)(2,1)S(1)} %copy-done, ...), custom_call_target="tpu_custom_call" | custom-call | flops 4294967296 | bytes 21008384 | tf_op jit(solution)/shard_map/pallas_call | solution.py:90
  301.6 2.2 collective-permute-start.30
  305.7 4.4 %shard_map.414.refs_2_.refs_4_ = f32[2048,1024]{1,0:T(8,128)} custom-call(s32[2]{0:T(128)S(1)} %pad_add_fusion.1.refs_0_, f32[2048,1024]{1,0:T(8,128)} %refs_1_.23, bf16[512,1024]{1,0:T(8,128)(2,1)S(1)} %collective-permute-done.31.refs_2_, bf16[512,1024]{1,0:T(8,128)(2,1)S(1)} %shard_map.401.refs_10_.refs_3_, f32[8,4096]{1,0:T(8,128)S(1)} %shard_map.413.refs_4_.refs_0_), custom_call_target="tpu_custom_call" | custom-call | bytes 18874368 | tf_op jit(solution)/shard_map/pallas_call | solution.py:90
  310.7 1.9 copy-done.4
  312.5 1.5 shard_map.417
  314.1 1.7 shard_map.418
  315.9 3.3 shard_map.416
  320.6 1.5 shard_map.420
  324.0 4.9 %shard_map.421.refs_2_.refs_4_ = f32[2048,1024]{1,0:T(8,128)} custom-call(s32[2]{0:T(128)S(1)} %copy-done.65, f32[2048,1024]{1,0:T(8,128)} %refs_1_.22, bf16[512,1024]{1,0:T(8,128)(2,1)} %collective-permute-done.33.refs_2_, bf16[512,1024]{1,0:T(8,128)(2,1)} %get-tuple-element.169.refs_2_.refs_3_, f32[8,768]{1,0:T(8,128)S(1)} %get-tuple-element.175.refs_4_, ...), custom_call_target="tpu_custom_call" | custom-call | bytes 18874368 | tf_op jit(solution)/shard_map/pallas_call | solution.py:90
  329.7 4.9 %shard_map.423.refs_4_.refs_2_ = f32[2048,1024]{1,0:T(8,128)} custom-call(s32[2]{0:T(128)S(1)} %copy-done.61, f32[2048,1024]{1,0:T(8,128)} %refs_1_.22, bf16[512,1024]{1,0:T(8,128)(2,1)} %collective-permute-done.32.refs_2_, bf16[512,1024]{1,0:T(8,128)(2,1)} %get-tuple-element.173.refs_3_, ...), custom_call_target="tpu_custom_call", output_to_operand_aliasing={{}: (4, {})} | custom-call | bytes 27262976 | tf_op jit(solution)/shard_map/pallas_call | solution.py:90
  334.8 1.9 collective-permute-start.37
  336.8 3.4 shard_map.424.refs_3_
  340.2 4.1 %collective-permute-done.37.refs_1_ = f32[8,4128]{1,0:T(8,128)S(1)} collective-permute-done((f32[8,4128]{1,0:T(8,128)S(1)}, f32[8,4128]{1,0:T(8,128)S(1)}, u32[]{:S(2)}, u32[]{:S(2)}) %collective-permute-start.37) | collective-permute-done | bytes 132128 | tf_op jit(solution)/shard_map/ppermute | solution.py:883
  345.0 3.1 shard_map.431
  349.9 2.0 shard_map.429
  352.0 3.5 shard_map.428
  356.3 4.4 %shard_map.430 = (f32[1024,1536]{1,0:T(8,128)}, f32[128,1536]{1,0:T(8,128)}, f32[128,1536]{1,0:T(8,128)}) custom-call(f32[1024,1536]{1,0:T(8,128)S(1)} %bitcast.68, f32[8,1024]{1,0:T(8,128)S(1)} %copy-done.49, f32[8,1536]{1,0:T(8,128)S(1)} %get-tuple-element.211.refs_2_, f32[8,128]{1,0:T(8,128)S(1)} %constant_dynamic-slice_fusion.1.refs_3_, ...), custom_call_target="tpu_custom_call" | custom-call | flops 100663296 | bytes 15814656 | tf_op jit(solution)/shard_map/pallas_call | solution.py:90
  361.4 4.9 %shard_map.425 = f32[2048,1024]{1,0:T(8,128)} custom-call(s32[2]{0:T(128)S(1)} %copy-done.61, f32[2048,1024]{1,0:T(8,128)} %refs_1_.23, bf16[512,1024]{1,0:T(8,128)(2,1)} %collective-permute-done.35.refs_2_, bf16[512,1024]{1,0:T(8,128)(2,1)} %shard_map.424.refs_3_, f32[2048,1024]{1,0:T(8,128)} %shard_map.414.refs_2_.refs_4_), custom_call_target="tpu_custom_call", output_to_operand_aliasing={{}: (4, {})} | custom-call | bytes 27262976 | tf_op jit(solution)/shard_map/pallas_call | solution.py:90
  (327 shorter events, 44.7 us)
Async XLA Ops:
  7.2 123.9 %all-gather.2.cloned.1.call-start = ((), (), s32[]{:S(2)}) async-start(), calls=%async_computation | async-start | bytes 5308416 | tf_op jit(solution)/shard_map/all_gather | solution.py:985
  10.2 12.4 %collective-permute-start = (bf16[128,1536]{1,0:T(8,128)(2,1)}, bf16[128,1536]{1,0:T(8,128)(2,1)}, u32[]{:S(2)}, u32[]{:S(2)}) collective-permute-start(bf16[128,1536]{1,0:T(8,128)(2,1)} %pad_maximum_fusion.3.refs_6_), channel_id=1, source_target_pairs={{0,8},{8,16},{16,24},{24,28},{28,20},{20,12},{12,4},{4,0},{1,9},{9... | collective-permute-start | bytes 1179656 | tf_op jit(solution)/shard_map/ppermute | solution.py:138
  13.2 11.2 %collective-permute-start.1 = (bf16[128,1536]{1,0:T(8,128)(2,1)}, bf16[128,1536]{1,0:T(8,128)(2,1)}, u32[]{:S(2)}, u32[]{:S(2)}) collective-permute-start(bf16[128,1536]{1,0:T(8,128)(2,1)} %pad_maximum_fusion.3.refs_6_), channel_id=1, source_target_pairs={{8,0},{16,8},{24,16},{28,24},{20,28},{12,20},{4,12},{0,4},{9,1},{1... | collective-permute-start | bytes 1179656 | tf_op jit(solution)/shard_map/ppermute | solution.py:138
  18.9 24.5 %copy-start.68 = (s32[9]{0:T(128)}, s32[9]{0:T(128)S(1)}, u32[]{:S(2)}) copy-start(s32[9]{0:T(128)S(1)} %fusion.5.refs_0_.refs_6_) | copy-start | bytes 112
  19.6 17.0 %copy-start.27 = (f32[768,128]{1,0:T(8,128)S(1)}, f32[768,128]{1,0:T(8,128)}, u32[]{:S(2)}) copy-start(f32[768,128]{1,0:T(8,128)} %refs_5_.13) | copy-start | bytes 1179652
  21.5 15.2 %copy-start.13 = (f32[128,1536]{1,0:T(8,128)S(1)}, f32[128,1536]{1,0:T(8,128)}, u32[]{:S(2)}) copy-start(f32[128,1536]{1,0:T(8,128)} %refs_5_.12) | copy-start | bytes 2359300
  22.6 10.5 %collective-permute-start.2 = (bf16[128,1536]{1,0:T(8,128)(2,1)}, bf16[128,1536]{1,0:T(8,128)(2,1)S(1)}, u32[]{:S(2)}, u32[]{:S(2)}) collective-permute-start(bf16[128,1536]{1,0:T(8,128)(2,1)} %collective-permute-done.refs_7_), channel_id=1, source_target_pairs={{0,8},{8,16},{16,24},{24,28},{28,20},{20,12},{12,4},{4,0},{1,9},{9... | collective-permute-start | bytes 1179656 | tf_op jit(solution)/shard_map/ppermute | solution.py:138
  24.4 10.2 %collective-permute-start.3 = (bf16[128,1536]{1,0:T(8,128)(2,1)}, bf16[128,1536]{1,0:T(8,128)(2,1)S(1)}, u32[]{:S(2)}, u32[]{:S(2)}) collective-permute-start(bf16[128,1536]{1,0:T(8,128)(2,1)} %collective-permute-done.1.refs_8_), channel_id=1, source_target_pairs={{8,0},{16,8},{24,16},{28,24},{20,28},{12,20},{4,12},{0,4},{9,1},{1... | collective-permute-start | bytes 1179656 | tf_op jit(solution)/shard_map/ppermute | solution.py:138
  24.6 13.7 %copy-start.56 = (s32[1,2048]{1,0:T(1,128)}, s32[1,2048]{1,0:T(1,128)S(1)}, u32[]{:S(2)}) copy-start(s32[1,2048]{1,0:T(1,128)S(1)} %compare_select_fusion.refs_5_) | copy-start | bytes 24580
  33.1 9.4 %collective-permute-start.4 = (bf16[128,1536]{1,0:T(8,128)(2,1)S(1)}, bf16[128,1536]{1,0:T(8,128)(2,1)S(1)}, u32[]{:S(2)}, u32[]{:S(2)}) collective-permute-start(bf16[128,1536]{1,0:T(8,128)(2,1)S(1)} %collective-permute-done.2.refs_9_), channel_id=1, source_target_pairs={{0,8},{8,16},{16,24},{24,28},{28,20},{20,12},{12,4},{4,0},{1,9},{9... | collective-permute-start | bytes 1179656 | tf_op jit(solution)/shard_map/ppermute | solution.py:138
  34.6 8.8 %collective-permute-start.5 = (bf16[128,1536]{1,0:T(8,128)(2,1)S(1)}, bf16[128,1536]{1,0:T(8,128)(2,1)S(1)}, u32[]{:S(2)}, u32[]{:S(2)}) collective-permute-start(bf16[128,1536]{1,0:T(8,128)(2,1)S(1)} %collective-permute-done.3.refs_10_), channel_id=1, source_target_pairs={{8,0},{16,8},{24,16},{28,24},{20,28},{12,20},{4,12},{0,4},{9,1},{1... | collective-permute-start | bytes 1179656 | tf_op jit(solution)/shard_map/ppermute | solution.py:138
  45.6 23.1 %copy-start.69 = (s32[9]{0:T(128)S(1)}, s32[9]{0:T(128)}, u32[]{:S(2)}) copy-start(s32[9]{0:T(128)} %copy-done.68) | copy-start | bytes 112
  52.0 9.8 %collective-permute-start.6 = (bf16[64,1536]{1,0:T(8,128)(2,1)S(1)}, bf16[64,1536]{1,0:T(8,128)(2,1)S(1)}, u32[]{:S(2)}, u32[]{:S(2)}) collective-permute-start(bf16[64,1536]{1,0:T(8,128)(2,1)S(1)} %slice.68), channel_id=1, source_target_pairs={{0,8},{8,16},{16,24},{24,28},{28,20},{20,12},{12,4},{4,0},{1,9},{9... | collective-permute-start | bytes 589832 | tf_op jit(solution)/shard_map/ppermute | solution.py:138
  53.6 14.5 %collective-permute-start.7 = (bf16[64,1536]{1,0:T(8,128)(2,1)S(1)}, bf16[64,1536]{1,0:T(8,128)(2,1)S(1)}, u32[]{:S(2)}, u32[]{:S(2)}) collective-permute-start(bf16[64,1536]{1,0:T(8,128)(2,1)S(1)} %slice.69), channel_id=1, source_target_pairs={{8,0},{16,8},{24,16},{28,24},{20,28},{12,20},{4,12},{0,4},{9,1},{1... | collective-permute-start | bytes 589832 | tf_op jit(solution)/shard_map/ppermute | solution.py:138
  68.8 12.7 %copy-start.67 = (s32[8]{0:T(128)S(1)}, s32[8]{0:T(128)}, u32[]{:S(2)}) copy-start(s32[8]{0:T(128)} %copy-done.66) | copy-start | bytes 100
  81.4 17.7 %copy-start.15 = (bf16[2048,512]{1,0:T(8,128)(2,1)}, bf16[2048,512]{1,0:T(8,128)(2,1)S(1)}, u32[]{:S(2)}) copy-start(bf16[2048,512]{1,0:T(8,128)(2,1)S(1)} %get-tuple-element.113.refs_1_) | copy-start | bytes 6291460
  81.4 17.7 %copy-start.17 = (bf16[2048,512]{1,0:T(8,128)(2,1)}, bf16[2048,512]{1,0:T(8,128)(2,1)S(1)}, u32[]{:S(2)}) copy-start(bf16[2048,512]{1,0:T(8,128)(2,1)S(1)} %get-tuple-element.115.refs_3_) | copy-start | bytes 6291460
  81.4 17.7 %copy-start.29 = (bf16[2048,256]{1,0:T(8,128)(2,1)}, bf16[2048,256]{1,0:T(8,128)(2,1)S(1)}, u32[]{:S(2)}) copy-start(bf16[2048,256]{1,0:T(8,128)(2,1)S(1)} %get-tuple-element.114.refs_2_) | copy-start | bytes 3145732
  94.6 2.7 collective-permute-start.8
  97.5 27.2 %copy-start.7 = (bf16[512,1024]{1,0:T(8,128)(2,1)}, bf16[512,1024]{1,0:T(8,128)(2,1)S(1)}, u32[]{:S(2)}) copy-start(bf16[512,1024]{1,0:T(8,128)(2,1)S(1)} %shard_map.378.refs_6_.refs_2_.refs_0_) | copy-start | bytes 3145732
  97.6 25.3 %collective-permute-start.9 = (bf16[512,1024]{1,0:T(8,128)(2,1)S(1)}, bf16[512,1024]{1,0:T(8,128)(2,1)S(1)}, u32[]{:S(2)}, u32[]{:S(2)}) collective-permute-start(bf16[512,1024]{1,0:T(8,128)(2,1)S(1)} %shard_map.378.refs_6_.refs_2_.refs_0_), channel_id=1, source_target_pairs={{0,2},{1,3},{2,0},{3,1},{4,6},{5,7},{6,4},{7,5},{8,10},{9,11},{10,... | collective-permute-start | bytes 3145736 | tf_op jit(solution)/shard_map/ppermute | solution.py:909
  108.2 14.6 %copy-start.11 = (bf16[1024,512]{1,0:T(8,128)(2,1)}, bf16[1024,512]{1,0:T(8,128)(2,1)S(1)}, u32[]{:S(2)}) copy-start(bf16[1024,512]{1,0:T(8,128)(2,1)S(1)} %get-tuple-element.120.refs_0_.refs_8_) | copy-start | bytes 3145732
  124.6 3.8 %collective-permute-start.10 = (bf16[512,1024]{1,0:T(8,128)(2,1)S(1)}, bf16[512,1024]{1,0:T(8,128)(2,1)S(1)}, u32[]{:S(2)}, u32[]{:S(2)}) collective-permute-start(bf16[512,1024]{1,0:T(8,128)(2,1)S(1)} %get-tuple-element.123), channel_id=1, source_target_pairs={{0,1},{1,0},{2,3},{3,2},{4,5},{5,4},{6,7},{7,6},{8,9},{9,8},{10,11... | collective-permute-start | bytes 3145736 | tf_op jit(solution)/shard_map/ppermute | solution.py:891
  128.0 3.1 collective-permute-start.13
  129.5 25.6 %collective-permute-start.11 = (bf16[512,1024]{1,0:T(8,128)(2,1)}, bf16[512,1024]{1,0:T(8,128)(2,1)}, u32[]{:S(2)}, u32[]{:S(2)}) collective-permute-start(bf16[512,1024]{1,0:T(8,128)(2,1)} %shard_map.383.refs_2_.refs_5_.refs_0_), channel_id=1, source_target_pairs={{0,2},{1,3},{2,0},{3,1},{4,6},{5,7},{6,4},{7,5},{8,10},{9,11},{10,... | collective-permute-start | bytes 3145736 | tf_op jit(solution)/shard_map/ppermute | solution.py:909
  131.1 174.6 %copy-start.64 = (s32[2]{0:T(128)}, s32[2]{0:T(128)S(1)}, u32[]{:S(2)}) copy-start(s32[2]{0:T(128)S(1)} %pad_add_fusion.1.refs_0_) | copy-start | bytes 28
  142.2 19.2 %slice-start.4 = ((s8[4718592]{0:T(1024)(128)(4,1)}), s8[4194304]{0:T(1024)(128)(4,1)S(1)}, s32[]{:S(2)}) async-start(s8[4718592]{0:T(1024)(128)(4,1)} %bitcast.69), calls=%async_computation.5 | async-start | bytes 8388608
  146.4 11.4 %collective-permute-start.14 = (bf16[512,1024]{1,0:T(8,128)(2,1)S(1)}, bf16[512,1024]{1,0:T(8,128)(2,1)S(1)}, u32[]{:S(2)}, u32[]{:S(2)}) collective-permute-start(bf16[512,1024]{1,0:T(8,128)(2,1)S(1)} %get-tuple-element.128), channel_id=1, source_target_pairs={{0,1},{1,0},{2,3},{3,2},{4,5},{5,4},{6,7},{7,6},{8,9},{9,8},{10,11... | collective-permute-start | bytes 3145736 | tf_op jit(solution)/shard_map/ppermute | solution.py:891
  157.7 2.7 collective-permute-start.12
  158.7 25.0 %collective-permute-start.15 = (bf16[512,1024]{1,0:T(8,128)(2,1)S(1)}, bf16[512,1024]{1,0:T(8,128)(2,1)S(1)}, u32[]{:S(2)}, u32[]{:S(2)}) collective-permute-start(bf16[512,1024]{1,0:T(8,128)(2,1)S(1)} %shard_map.389.refs_5_.refs_2_), channel_id=1, source_target_pairs={{0,2},{1,3},{2,0},{3,1},{4,6},{5,7},{6,4},{7,5},{8,10},{9,11},{10,... | collective-permute-start | bytes 3145736 | tf_op jit(solution)/shard_map/ppermute | solution.py:909
  160.2 118.1 %copy-start.60 = (s32[2]{0:T(128)}, s32[2]{0:T(128)S(1)}, u32[]{:S(2)}) copy-start(s32[2]{0:T(128)S(1)} %pad_add_fusion.refs_0_) | copy-start | bytes 28
  187.7 3.4 collective-permute-start.16
  187.8 18.4 %collective-permute-start.21 = (bf16[512,1024]{1,0:T(8,128)(2,1)S(1)}, bf16[512,1024]{1,0:T(8,128)(2,1)S(1)}, u32[]{:S(2)}, u32[]{:S(2)}) collective-permute-start(bf16[512,1024]{1,0:T(8,128)(2,1)S(1)} %get-tuple-element.137.refs_3_), channel_id=1, source_target_pairs={{0,1},{1,0},{2,3},{3,2},{4,5},{5,4},{6,7},{7,6},{8,9},{9,8},{10,11... | collective-permute-start | bytes 3145736 | tf_op jit(solution)/shard_map/ppermute | solution.py:891
  191.0 30.4 %copy-start.33 = (bf16[512,1024]{1,0:T(8,128)(2,1)}, bf16[512,1024]{1,0:T(8,128)(2,1)S(1)}, u32[]{:S(2)}) copy-start(bf16[512,1024]{1,0:T(8,128)(2,1)S(1)} %get-tuple-element.149.refs_15_.refs_6_) | copy-start | bytes 3145732
  191.0 30.4 %collective-permute-start.20 = (bf16[512,1024]{1,0:T(8,128)(2,1)S(1)}, bf16[512,1024]{1,0:T(8,128)(2,1)S(1)}, u32[]{:S(2)}, u32[]{:S(2)}) collective-permute-start(bf16[512,1024]{1,0:T(8,128)(2,1)S(1)} %get-tuple-element.149.refs_15_.refs_6_), channel_id=1, source_target_pairs={{0,1},{1,0},{2,3},{3,2},{4,5},{5,4},{6,7},{7,6},{8,9},{9,8},{10,11... | collective-permute-start | bytes 3145736 | tf_op jit(solution)/shard_map/ppermute | solution.py:891
  191.4 26.0 %collective-permute-start.18 = (bf16[512,1024]{1,0:T(8,128)(2,1)S(1)}, bf16[512,1024]{1,0:T(8,128)(2,1)S(1)}, u32[]{:S(2)}, u32[]{:S(2)}) collective-permute-start(bf16[512,1024]{1,0:T(8,128)(2,1)S(1)} %shard_map.394.refs_7_.refs_2_), channel_id=1, source_target_pairs={{0,2},{1,3},{2,0},{3,1},{4,6},{5,7},{6,4},{7,5},{8,10},{9,11},{10,... | collective-permute-start | bytes 3145736 | tf_op jit(solution)/shard_map/ppermute | solution.py:909
  206.4 35.9 %collective-permute-start.22 = (bf16[512,1024]{1,0:T(8,128)(2,1)S(1)}, bf16[512,1024]{1,0:T(8,128)(2,1)S(1)}, u32[]{:S(2)}, u32[]{:S(2)}) collective-permute-start(bf16[512,1024]{1,0:T(8,128)(2,1)S(1)} %shard_map.400.refs_2_), channel_id=1, source_target_pairs={{0,2},{1,3},{2,0},{3,1},{4,6},{5,7},{6,4},{7,5},{8,10},{9,11},{10,... | collective-permute-start | bytes 3145736 | tf_op jit(solution)/shard_map/ppermute | solution.py:909
  221.4 20.9 %copy-start.35 = (bf16[512,1024]{1,0:T(8,128)(2,1)}, bf16[512,1024]{1,0:T(8,128)(2,1)S(1)}, u32[]{:S(2)}) copy-start(bf16[512,1024]{1,0:T(8,128)(2,1)S(1)} %collective-permute-done.20.refs_14_.refs_5_) | copy-start | bytes 3145732
  221.4 20.9 %copy-start.6 = (bf16[512,1024]{1,0:T(8,128)(2,1)S(1)}, bf16[512,1024]{1,0:T(8,128)(2,1)}, u32[]{:S(2)}) copy-start(bf16[512,1024]{1,0:T(8,128)(2,1)} %copy-done.5) | copy-start | bytes 3145732
  221.5 20.9 %copy-start.8 = (bf16[512,1024]{1,0:T(8,128)(2,1)S(1)}, bf16[512,1024]{1,0:T(8,128)(2,1)}, u32[]{:S(2)}) copy-start(bf16[512,1024]{1,0:T(8,128)(2,1)} %copy-done.7) | copy-start | bytes 3145732
  250.1 2.7 collective-permute-start.23
  250.2 4.5 %collective-permute-start.19 = (bf16[512,1024]{1,0:T(8,128)(2,1)S(1)}, bf16[512,1024]{1,0:T(8,128)(2,1)S(1)}, u32[]{:S(2)}, u32[]{:S(2)}) collective-permute-start(bf16[512,1024]{1,0:T(8,128)(2,1)S(1)} %get-tuple-element.146.refs_16_.refs_8_.refs_15_), channel_id=1, source_target_pairs={{0,1},{1,0},{2,3},{3,2},{4,5},{5,4},{6,7},{7,6},{8,9},{9,8},{10,11... | collective-permute-start | bytes 3145736 | tf_op jit(solution)/shard_map/ppermute | solution.py:891
  253.1 25.3 %collective-permute-start.24 = (bf16[512,1024]{1,0:T(8,128)(2,1)S(1)}, bf16[512,1024]{1,0:T(8,128)(2,1)S(1)}, u32[]{:S(2)}, u32[]{:S(2)}) collective-permute-start(bf16[512,1024]{1,0:T(8,128)(2,1)S(1)} %shard_map.403.refs_9_.refs_2_), channel_id=1, source_target_pairs={{0,2},{1,3},{2,0},{3,1},{4,6},{5,7},{6,4},{7,5},{8,10},{9,11},{10,... | collective-permute-start | bytes 3145736 | tf_op jit(solution)/shard_map/ppermute | solution.py:909
  286.0 2.7 collective-permute-start.25
  286.1 17.8 %collective-permute-start.17 = (bf16[512,1024]{1,0:T(8,128)(2,1)S(1)}, bf16[512,1024]{1,0:T(8,128)(2,1)S(1)}, u32[]{:S(2)}, u32[]{:S(2)}) collective-permute-start(bf16[512,1024]{1,0:T(8,128)(2,1)S(1)} %get-tuple-element.142.refs_6_), channel_id=1, source_target_pairs={{0,1},{1,0},{2,3},{3,2},{4,5},{5,4},{6,7},{7,6},{8,9},{9,8},{10,11... | collective-permute-start | bytes 3145736 | tf_op jit(solution)/shard_map/ppermute | solution.py:891
  286.6 19.1 %collective-permute-start.31 = (bf16[512,1024]{1,0:T(8,128)(2,1)S(1)}, bf16[512,1024]{1,0:T(8,128)(2,1)S(1)}, u32[]{:S(2)}, u32[]{:S(2)}) collective-permute-start(bf16[512,1024]{1,0:T(8,128)(2,1)S(1)} %shard_map.401.refs_10_.refs_3_), channel_id=1, source_target_pairs={{0,1},{1,0},{2,3},{3,2},{4,5},{5,4},{6,7},{7,6},{8,9},{9,8},{10,11... | collective-permute-start | bytes 3145736 | tf_op jit(solution)/shard_map/ppermute | solution.py:891
  287.9 6.1 %collective-permute-start.28 = (f32[8,4096]{1,0:T(8,128)S(1)}, f32[8,4096]{1,0:T(8,128)S(1)}, u32[]{:S(2)}, u32[]{:S(2)}) collective-permute-start(f32[8,4096]{1,0:T(8,128)S(1)} %pad_maximum_fusion.4.refs_0_), channel_id=1, source_target_pairs={{0,4},{4,0},{8,12},{12,8},{16,20},{20,16},{24,28},{28,24},{1,5},{5... | collective-permute-start | bytes 393224 | tf_op jit(solution)/shard_map/ppermute | solution.py:883
  289.0 26.9 %collective-permute-start.27 = (bf16[512,1024]{1,0:T(8,128)(2,1)S(1)}, bf16[512,1024]{1,0:T(8,128)(2,1)S(1)}, u32[]{:S(2)}, u32[]{:S(2)}) collective-permute-start(bf16[512,1024]{1,0:T(8,128)(2,1)S(1)} %shard_map.407.refs_2_.refs_6_), channel_id=1, source_target_pairs={{0,2},{1,3},{2,0},{3,1},{4,6},{5,7},{6,4},{7,5},{8,10},{9,11},{10,... | collective-permute-start | bytes 3145736 | tf_op jit(solution)/shard_map/ppermute | solution.py:909
  294.0 7.6 %collective-permute-start.29 = (f32[8,4096]{1,0:T(8,128)S(1)}, f32[8,4096]{1,0:T(8,128)S(1)}, u32[]{:S(2)}, u32[]{:S(2)}) collective-permute-start(f32[8,4096]{1,0:T(8,128)S(1)} %shard_map.411.refs_7_.refs_0_), channel_id=1, source_target_pairs={{0,8},{4,12},{8,0},{12,4},{16,24},{20,28},{24,16},{28,20},{1,9},{5... | collective-permute-start | bytes 393224 | tf_op jit(solution)/shard_map/ppermute | solution.py:883
  301.6 19.0 %copy-start.2 = (f32[1024,1024]{1,0:T(8,128)}, f32[1024,1024]{1,0:T(8,128)S(1)}, u32[]{:S(2)}) copy-start(f32[1024,1024]{1,0:T(8,128)S(1)} %get-tuple-element.180.refs_1_.refs_0_) | copy-start | bytes 12582916
  301.6 9.0 %collective-permute-start.30 = (f32[8,4096]{1,0:T(8,128)S(1)}, f32[8,4096]{1,0:T(8,128)S(1)}, u32[]{:S(2)}, u32[]{:S(2)}) collective-permute-start(f32[8,4096]{1,0:T(8,128)S(1)} %shard_map.413.refs_4_.refs_0_), channel_id=1, source_target_pairs={{0,16},{4,20},{8,24},{12,28},{16,0},{20,4},{24,8},{28,12},{1,17},{... | collective-permute-start | bytes 393224 | tf_op jit(solution)/shard_map/ppermute | solution.py:883
  303.9 20.1 %collective-permute-start.33 = (bf16[512,1024]{1,0:T(8,128)(2,1)}, bf16[512,1024]{1,0:T(8,128)(2,1)}, u32[]{:S(2)}, u32[]{:S(2)}) collective-permute-start(bf16[512,1024]{1,0:T(8,128)(2,1)} %get-tuple-element.169.refs_2_.refs_3_), channel_id=1, source_target_pairs={{0,1},{1,0},{2,3},{3,2},{4,5},{5,4},{6,7},{7,6},{8,9},{9,8},{10,11... | collective-permute-start | bytes 3145736 | tf_op jit(solution)/shard_map/ppermute | solution.py:891
  305.0 31.8 %collective-permute-start.26 = (bf16[512,1024]{1,0:T(8,128)(2,1)}, bf16[512,1024]{1,0:T(8,128)(2,1)}, u32[]{:S(2)}, u32[]{:S(2)}) collective-permute-start(bf16[512,1024]{1,0:T(8,128)(2,1)} %shard_map.408.refs_2_), channel_id=1, source_target_pairs={{0,2},{1,3},{2,0},{3,1},{4,6},{5,7},{6,4},{7,5},{8,10},{9,11},{10,... | collective-permute-start | bytes 3145736 | tf_op jit(solution)/shard_map/ppermute | solution.py:909
  319.2 10.5 %collective-permute-start.32 = (bf16[512,1024]{1,0:T(8,128)(2,1)}, bf16[512,1024]{1,0:T(8,128)(2,1)}, u32[]{:S(2)}, u32[]{:S(2)}) collective-permute-start(bf16[512,1024]{1,0:T(8,128)(2,1)} %get-tuple-element.173.refs_3_), channel_id=1, source_target_pairs={{0,1},{1,0},{2,3},{3,2},{4,5},{5,4},{6,7},{7,6},{8,9},{9,8},{10,11... | collective-permute-start | bytes 3145736 | tf_op jit(solution)/shard_map/ppermute | solution.py:891
  322.7 6.2 %collective-permute-start.34 = (f32[8,4128]{1,0:T(8,128)S(1)}, f32[8,4128]{1,0:T(8,128)S(1)}, u32[]{:S(2)}, u32[]{:S(2)}) collective-permute-start(f32[8,4128]{1,0:T(8,128)S(1)} %constant_dynamic-update-slice_fusion.refs_0_), channel_id=1, source_target_pairs={{0,4},{4,0},{8,12},{12,8},{16,20},{20,16},{24,28},{28,24},{1,5},{5... | collective-permute-start | bytes 396296 | tf_op jit(solution)/shard_map/ppermute | solution.py:883
  329.0 5.8 %collective-permute-start.36 = (f32[8,4128]{1,0:T(8,128)S(1)}, f32[8,4128]{1,0:T(8,128)S(1)}, u32[]{:S(2)}, u32[]{:S(2)}) collective-permute-start(f32[8,4128]{1,0:T(8,128)S(1)} %shard_map.422.refs_5_.refs_0_), channel_id=1, source_target_pairs={{0,8},{4,12},{8,0},{12,4},{16,24},{20,28},{24,16},{28,20},{1,9},{5... | collective-permute-start | bytes 396296 | tf_op jit(solution)/shard_map/ppermute | solution.py:883
  334.8 9.5 %collective-permute-start.37 = (f32[8,4128]{1,0:T(8,128)S(1)}, f32[8,4128]{1,0:T(8,128)S(1)}, u32[]{:S(2)}, u32[]{:S(2)}) collective-permute-start(f32[8,4128]{1,0:T(8,128)S(1)} %shard_map.426.refs_0_), channel_id=1, source_target_pairs={{0,16},{4,20},{8,24},{12,28},{16,0},{20,4},{24,8},{28,12},{1,17},{... | collective-permute-start | bytes 396296 | tf_op jit(solution)/shard_map/ppermute | solution.py:883
  336.8 13.1 %copy-start.10 = (f32[512,1024]{1,0:T(8,128)S(1)}, f32[512,1024]{1,0:T(8,128)}, u32[]{:S(2)}) copy-start(f32[512,1024]{1,0:T(8,128)} %get-tuple-element.178.refs_1_.refs_0_) | copy-start | bytes 6291460
  336.8 13.1 %copy-start.39 = (f32[512,128]{1,0:T(8,128)S(1)}, f32[512,128]{1,0:T(8,128)}, u32[]{:S(2)}) copy-start(f32[512,128]{1,0:T(8,128)} %refs_5_.11) | copy-start | bytes 786436
  336.8 13.1 %copy-start.46 = (f32[512,128]{1,0:T(8,128)S(1)}, f32[512,128]{1,0:T(8,128)}, u32[]{:S(2)}) copy-start(f32[512,128]{1,0:T(8,128)} %refs_4_.5) | copy-start | bytes 786436
  336.8 19.4 %copy-start.42 = (f32[128,1536]{1,0:T(8,128)S(1)}, f32[128,1536]{1,0:T(8,128)}, u32[]{:S(2)}) copy-start(f32[128,1536]{1,0:T(8,128)} %refs_4_.6) | copy-start | bytes 2359300
  340.2 21.2 %collective-permute-start.35 = (bf16[512,1024]{1,0:T(8,128)(2,1)}, bf16[512,1024]{1,0:T(8,128)(2,1)}, u32[]{:S(2)}, u32[]{:S(2)}) collective-permute-start(bf16[512,1024]{1,0:T(8,128)(2,1)} %shard_map.424.refs_3_), channel_id=1, source_target_pairs={{0,1},{1,0},{2,3},{3,2},{4,5},{5,4},{6,7},{7,6},{8,9},{9,8},{10,11... | collective-permute-start | bytes 3145736 | tf_op jit(solution)/shard_map/ppermute | solution.py:891
  344.9 10.6 %collective-permute-start.38 = (f32[8,288]{1,0:T(8,128)S(1)}, f32[8,288]{1,0:T(8,128)S(1)}, u32[]{:S(2)}, u32[]{:S(2)}) collective-permute-start(f32[8,288]{1,0:T(8,128)S(1)} %slice.78.refs_0_), channel_id=1, source_target_pairs={{0,1},{1,0},{2,3},{3,2},{4,5},{5,4},{6,7},{7,6},{8,9},{9,8},{10,11... | collective-permute-start | bytes 27656 | tf_op jit(solution)/shard_map/ppermute | solution.py:883
  355.6 5.1 %collective-permute-start.39 = (f32[8,288]{1,0:T(8,128)S(1)}, f32[8,288]{1,0:T(8,128)S(1)}, u32[]{:S(2)}, u32[]{:S(2)}) collective-permute-start(f32[8,288]{1,0:T(8,128)S(1)} %shard_map.432.refs_0_), channel_id=1, source_target_pairs={{0,2},{1,3},{2,0},{3,1},{4,6},{5,7},{6,4},{7,5},{8,10},{9,11},{10,... | collective-permute-start | bytes 27656 | tf_op jit(solution)/shard_map/ppermute | solution.py:883
  (72 other events, 342.0 us)
Sparse Core Ops, SparseCore 0:
  44.4 82.1 all-gather.1

commit v2 on v1

--- a/solution.py
+++ b/solution.py
@@ -524,11 +524,12 @@
     )
 
 
-def mlp_kernel(tab_ref, grad_ref, theirs_ref, mine_ref, w_ref, ht_ref, act_ref, act_t_ref, dgu_ref, h_scr):
+def mlp_kernel(tab_ref, grad_ref, theirs_ref, mine_ref, w_ref, ht_ref, dm_ref, act_ref, act_t_ref, dgu_ref, h_scr):
     take_halves(pl.program_id(0), 2, theirs_ref, mine_ref, h_scr)
     ff_cols = act_ref.shape[1]
     h_mlp = h_scr[...]
     d_mlp = grad_ref[...].astype(HALF)
+    dm_ref[...] = d_mlp
     ht_ref[...] = h_mlp.T
     width = tile_of(ff_cols)
     for at in range(0, ff_cols, width):
@@ -553,8 +554,10 @@
         mlp_kernel,
         (2,),
         [picked(half, D), whole(half, D), whole(half, D), whole(D, w_cols)],
-        [stepped_col(D, half), stepped(half, ff_cols), stepped_col(ff_cols, half), stepped(half, 2 * ff_cols)],
-        [shape_of((D, size), HALF), shape_of((size, ff_cols), HALF), shape_of((ff_cols, size), HALF),
+        [stepped_col(D, half), stepped(half, D), stepped(half, ff_cols), stepped_col(ff_cols, half),
+         stepped(half, 2 * ff_cols)],
+        [shape_of((D, size), HALF), shape_of((size, D), HALF), shape_of((size, ff_cols), HALF),
+         shape_of((ff_cols, size), HALF),
          shape_of((size, 2 * ff_cols), HALF)],
         (far(out_grad),) + tuple(far(piece) for piece in pieces) + (weights,),
         scratch=[pltpu.VMEM((half, D), HALF)],
@@ -984,7 +987,7 @@
     )
     second_b = lax.all_gather(stage(second_own, first_steps[-2] + (far(cosine), far(sine), far(key_col), shard_places) + tuple(tables)), "dp", axis=0, tiled=True)
 
-    att, att_t, log_total, att_sum, resid, h_pieces = {}, {}, {}, {}, {}, {}
+    att, att_t, log_total, att_sum = {}, {}, {}, {}
     after, arrived = (), ()
     for chunk in order:
         att[chunk], att_t[chunk], log_total[chunk] = attend(
@@ -998,29 +1001,33 @@
         after = (part,)
         att_sum[chunk] = across_chips(part, parts)
         arrived = att_sum[chunk][1:]
+
+    two = [(chunk, place) for chunk in order for place in (0, 1)]
+    size = 2 * half
+    h_mlp_t, d_mlp, activ, activ_t, d_gu, mid_sum, mlp_part, mlp_sum = {}, {}, {}, {}, {}, {}, {}, {}
+    resid, h_pieces = {}, {}
+    arrived = ()
+    for chunk in order:
+        filled = () if chunk == order[0] else mlp_part[order[0]][:1]
         resid[chunk], h_own = norm_rows(
-            mid_kernel, own_half[chunk], hidden_in, *att_sum[chunk], g_mlp, (), (FULL, HALF), 0
+            mid_kernel, own_half[chunk], hidden_in, *att_sum[chunk], g_mlp, (), (FULL, HALF), 0, filled
         )
         h_pieces[chunk] = pieces_of(h_own, parts)
-
-    two = [(chunk, place) for chunk in order for place in (0, 1)]
-    size = 2 * half
-    h_mlp_t, activ, activ_t, d_gu, mid_sum, mlp_part, mlp_sum = {}, {}, {}, {}, {}, {}, {}
-    arrived = ()
-    for chunk in order:
-        h_mlp_t[chunk], activ[chunk], activ_t[chunk], d_gu[chunk] = feed_forward(
+        h_mlp_t[chunk], d_mlp[chunk], activ[chunk], activ_t[chunk], d_gu[chunk] = feed_forward(
             half_tables[chunk], out_grad, second_b, h_pieces[chunk], after
         )
         if chunk == order[-1]:
             merged_down, p_down = merge_grad(
                 all_halves,
                 [(activ_t[other], 0, size) for other in order],
-                [(out_grad, number, True) for number in range(len(two))],
+                [(d_mlp[other], 0, False) for other in order],
                 error_down[0], factors_t[3], True,
             )
-            mlp_part[order[0]] = project(activ[order[0]], second_b, 2, (p_down,))
-            arrived = arrived + mlp_part[order[0]][:1]
-        part = chip_sum(*project(d_gu[chunk], second_b, 0, arrived), parts)
+            arrived = arrived + (p_down,)
+        summed = project(d_gu[chunk], second_b, 0, arrived)
+        if chunk == order[0]:
+            mlp_part[chunk] = project(activ[chunk], second_b, 2, summed[:1], far_shape)
+        part = chip_sum(*summed, parts)
         after = (part,)
         mid_sum[chunk] = across_chips(part, parts)
         arrived = mid_sum[chunk][1:]
@@ -1126,12 +1133,13 @@
     )
     q_all = butterfly_step(q_all, "dp", workers, 1, (far(input_grad),))
     for chunk in order[1:]:
+        deltas[chunk] = layer_delta(att_sum[chunk] + mlp_sum[chunk], (q_all,))
+    q_all = butterfly_step(q_all, "dp", workers, 2, (deltas[order[-1]],))
+    for chunk in order[1:]:
         input_grad = spread(
             half_tables[chunk], out_grad, pieces_of(in_delta[chunk], parts), input_grad, (q_all,)
         )
-        deltas[chunk] = layer_delta(att_sum[chunk] + mlp_sum[chunk], (far(input_grad),))
-    q_all = butterfly_step(q_all, "dp", workers, 2, (far(input_grad),))
-    q_all = butterfly_step(q_all, "dp", workers, 4)
+    q_all = butterfly_step(q_all, "dp", workers, 4, (far(input_grad),))
     q_all = butterfly_step(q_all, "dp", workers, 8) / workers
     for chunk in order[1:]:
         layer_out = spread(half_tables[chunk], hidden_in, pieces_of(deltas[chunk], parts), layer_out)

time: 380 us -> 383 us (level)
  starting transfers between devices: 30.7 us -> 37.7 us
  Pallas kernels: 236 us -> 232 us
    ppermute x8, starting transfers between devices: 6.77 us -> 13.1 us  [butterfly_step(): other = lax.ppermute(values, axis, [(i, i ^ span) for i in range(count)])]
    pallas_call x60, Pallas kernels: 236 us -> 232 us  [call(): pl.pallas_call(body, grid_spec=pltpu.PrefetchScalarGridSpec(num_scalar_pr...]
    unnamed x196 -> x202, local copies, waits for them, and re-layouts: 11.9 us -> 13.6 us
  transfers between devices with their start and end apart: 41 -> 41, of which waited for: 19 -> 18; matrix products, arithmetic and copies ran while one was open for 4% -> 4% of each run, Pallas kernels for 57% -> 55%
where the time goes in v2:
time: 383 us; the launch traced here: 375 us
  Pallas kernels  232 us (61%)
  waiting for transfers between devices  58.7 us (15%)
  starting transfers between devices  37.7 us (10%)
  local copies, waits for them, and re-layouts  21.3 us (6%)
  between operations  15.6 us (4%)
  other arithmetic  10.3 us (3%)
    pallas_call x60, Pallas kernels, call(): pl.pallas_call(body, grid_spec=pltpu.PrefetchScalarGridSpec(num_scalar_pr...  232 us
    ppermute x8, waiting for transfers between devices, across_chips(): other = lax.ppermute(part, 'tensor', [(i, i ^ span) for i in range(count)])  24 us
    ppermute x4, waiting for transfers between devices, ring_step(): lax.ppermute(from_left, 'dp', ahead)  20.9 us
    unnamed x202, local copies, waits for them, and re-layouts  13.6 us
    ppermute x8, starting transfers between devices, butterfly_step(): other = lax.ppermute(values, axis, [(i, i ^ span) for i in range(count)])  13.1 us
    ppermute x8, starting transfers between devices, across_chips(): other = lax.ppermute(part, 'tensor', [(i, i ^ span) for i in range(count)])  12 us
    ppermute x4, starting transfers between devices, ring_step(): lax.ppermute(from_left, 'dp', ahead)  7.92 us
  transfers between devices with their start and end apart: 41, of which 18 were waited for; matrix products, arithmetic and copies ran while one was open for 4% of the time, Pallas kernels for 55%

profile of v2, /device:TPU:0, one launch (start us, length us, event | category | flops | bytes accessed | tf_op | source)
XLA Modules:
  0.0 375.4 jit_solution(8885430433299598361)
XLA Ops:
  10.2 3.0 collective-permute-start
  14.9 3.9 %fusion.2 = (f32[2048,64]{1,0:T(8,128)S(1)}, f32[2048,64]{1,0:T(8,128)S(1)}, f32[2048,64]{1,0:T(8,128)S(1)}) fusion(f32[64]{0:T(128)S(1)} %negate_power_fusion), kind=kLoop, calls=%fused_computation.8 | loop fusion | flops 262144 | bytes 1573120 | tf_op jit(solution)/shard_map/neg | solution.py:124
  19.6 1.9 pad_maximum_fusion
  22.6 1.8 collective-permute-start.2
  24.6 8.4 %collective-permute-done.2.refs_9_ = bf16[128,1536]{1,0:T(8,128)(2,1)S(1)} collective-permute-done((bf16[128,1536]{1,0:T(8,128)(2,1)}, bf16[128,1536]{1,0:T(8,128)(2,1)S(1)}, u32[]{:S(2)}, u32[]{:S(2)}) %collective-permute-start.2) | collective-permute-done | bytes 393248 | tf_op jit(solution)/shard_map/ppermute | solution.py:138
  38.3 4.2 %collective-permute-done.4.refs_11_.refs_1_ = bf16[128,1536]{1,0:T(8,128)(2,1)S(1)} collective-permute-done((bf16[128,1536]{1,0:T(8,128)(2,1)S(1)}, bf16[128,1536]{1,0:T(8,128)(2,1)S(1)}, u32[]{:S(2)}, u32[]{:S(2)}) %collective-permute-start.4) | collective-permute-done | bytes 393248 | tf_op jit(solution)/shard_map/ppermute | solution.py:138
  45.6 6.3 %shard_map.374.refs_1_.refs_0_ = bf16[2048,1024]{1,0:T(8,128)(2,1)S(1)} custom-call(f32[2048,1024]{1,0:T(8,128)} %refs_1_.22, f32[1,1024]{1,0:T(1,128)S(1)} %bitcast.82), custom_call_target="tpu_custom_call" | custom-call | bytes 12587008 | tf_op jit(solution)/shard_map/pallas_call | solution.py:90
  52.0 1.6 collective-permute-start.6
  54.6 7.2 %collective-permute-done.6.refs_13_ = bf16[64,1536]{1,0:T(8,128)(2,1)S(1)} collective-permute-done((bf16[64,1536]{1,0:T(8,128)(2,1)S(1)}, bf16[64,1536]{1,0:T(8,128)(2,1)S(1)}, u32[]{:S(2)}, u32[]{:S(2)}) %collective-permute-start.6) | collective-permute-done | bytes 196640 | tf_op jit(solution)/shard_map/ppermute | solution.py:138
  61.8 6.3 %collective-permute-done.7.refs_14_ = bf16[64,1536]{1,0:T(8,128)(2,1)S(1)} collective-permute-done((bf16[64,1536]{1,0:T(8,128)(2,1)S(1)}, bf16[64,1536]{1,0:T(8,128)(2,1)S(1)}, u32[]{:S(2)}, u32[]{:S(2)}) %collective-permute-start.7) | collective-permute-done | bytes 196640 | tf_op jit(solution)/shard_map/ppermute | solution.py:138
  68.8 12.6 %shard_map.375 = (bf16[1024,1536]{1,0:T(8,128)(2,1)S(1)}, bf16[2048,512]{1,0:T(8,128)(2,1)S(1)}, bf16[2048,256]{1,0:T(8,128)(2,1)S(1)}, bf16[2048,512]{1,0:T(8,1...) custom-call(s32[9]{0:T(128)S(1)} %copy-done.71, ...), custom_call_target="tpu_custom_call" | custom-call | flops 4294967296 | bytes 25166848 | tf_op jit(solution)/shard_map/pallas_call | solution.py:90
  81.4 9.3 %shard_map.376 = (bf16[1024,512]{1,0:T(8,128)(2,1)S(1)}, bf16[512,1024]{1,0:T(8,128)(2,1)}, f32[4,1024]{1,0:T(4,128)S(1)}) custom-call(s32[8]{0:T(128)S(1)} %copy-done.69, bf16[2048,512]{1,0:T(8,128)(2,1)S(1)} %get-tuple-element.115.refs_1_, bf16[2048,256]{1,0:T(8,128)(2,1)S(1)} %get-tuple-element.116.refs_2_, ...), custom_call_target="tpu_custom_call" | custom-call | flops 3221225472 | bytes 7372800 | tf_op jit(solution)/shard_map/pallas_call | solution.py:90
  90.7 1.8 shard_map.377
  92.6 2.6 collective-permute-done.8.refs_1_
  95.4 1.5 collective-permute-start.9
  97.0 9.1 %shard_map.379 = (bf16[1024,512]{1,0:T(8,128)(2,1)S(1)}, bf16[512,1024]{1,0:T(8,128)(2,1)}, f32[4,1024]{1,0:T(4,128)S(1)}) custom-call(s32[8]{0:T(128)S(1)} %copy-done.65, bf16[2048,512]{1,0:T(8,128)(2,1)S(1)} %get-tuple-element.115.refs_1_, bf16[2048,256]{1,0:T(8,128)(2,1)S(1)} %get-tuple-element.116.refs_2_, ...), custom_call_target="tpu_custom_call" | custom-call | flops 3221225472 | bytes 7372800 | tf_op jit(solution)/shard_map/pallas_call | solution.py:90
  106.1 3.7 shard_map.380.refs_1_.refs_0_
  109.8 4.2 %shard_map.381.refs_3_.refs_1_.refs_4_ = bf16[1024,2048]{1,0:T(8,128)(2,1)} custom-call(bf16[2048,1024]{1,0:T(8,128)(2,1)S(1)} %shard_map.374.refs_1_.refs_0_, f32[8,1024]{1,0:T(8,128)S(1)} %shard_map.380.refs_1_.refs_0_), custom_call_target="tpu_custom_call" | custom-call | bytes 8388608 | tf_op jit(solution)/shard_map/pallas_call | solution.py:90
  114.0 6.7 %collective-permute-done.9.refs_2_.refs_3_.refs_1_ = bf16[512,1024]{1,0:T(8,128)(2,1)S(1)} collective-permute-done((bf16[512,1024]{1,0:T(8,128)(2,1)S(1)}, bf16[512,1024]{1,0:T(8,128)(2,1)S(1)}, u32[]{:S(2)}, u32[]{:S(2)}) %collective-permute-start.9) | collective-permute-done | bytes 1048608 | tf_op jit(solution)/shard_map/ppermute | solution.py:912
  120.7 1.8 shard_map.382
  122.6 1.9 shard_map.384
  129.1 2.3 copy-done.1
  131.4 9.0 %shard_map.386 = (bf16[1024,1024]{1,0:T(8,128)(2,1)S(1)}, bf16[1024,1024]{1,0:T(8,128)(2,1)S(1)}, bf16[1024,768]{1,0:T(8,128)(2,1)S(1)}, bf16[768,1024]{1,0:T(8,128)(2,1)S(1)}, bf16[1024,1536]{1,0:T(8,128)(2,1)S(1)}) custom-call(s32[2]{0:T(128)S(1)} %pad_add_fusion.1.refs_0_, f32[2048,1024]{1,0:T(8,128)} %refs_1_.23, ...), custom_call_target="tpu_custom_call" | custom-call | flops 4831838208 | bytes 25690112 | tf_op jit(solution)/shard_map/pallas_call | solution.py:90
  140.4 4.1 %shard_map.387 = (bf16[512,1024]{1,0:T(8,128)(2,1)S(1)}, f32[512,1024]{1,0:T(8,128)S(1)}) custom-call(bf16[1024,1536]{1,0:T(8,128)(2,1)S(1)} %get-tuple-element.128.refs_0_.refs_5_, bf16[1024,2304]{1,0:T(8,128)(2,1)S(1)} %copy-done.1), custom_call_target="tpu_custom_call" | custom-call | flops 3221225472 | bytes 11010048 | tf_op jit(solution)/shard_map/pallas_call | solution.py:90
  144.8 3.9 %shard_map.388 = (bf16[512,1024]{1,0:T(8,128)(2,1)S(1)}, f32[512,1024]{1,0:T(8,128)}) custom-call(bf16[1024,768]{1,0:T(8,128)(2,1)S(1)} %get-tuple-element.127.refs_0_, bf16[1024,2304]{1,0:T(8,128)(2,1)S(1)} %copy-done.1, bf16[512,1024]{1,0:T(8,128)(2,1)S(1)} %get-tuple-element.129.refs_2_), custom_call_target="tpu_custom_call" | custom-call | flops 1610612736 | bytes 9437184 | tf_op jit(solution)/shard_map/pallas_call | solution.py:90
  148.6 4.5 %collective-permute-done.11.refs_3_.refs_1_ = bf16[512,1024]{1,0:T(8,128)(2,1)} collective-permute-done((bf16[512,1024]{1,0:T(8,128)(2,1)}, bf16[512,1024]{1,0:T(8,128)(2,1)}, u32[]{:S(2)}, u32[]{:S(2)}) %collective-permute-start.11) | collective-permute-done | bytes 1048608 | tf_op jit(solution)/shard_map/ppermute | solution.py:912
  153.1 2.5 shard_map.389
  159.4 8.9 %shard_map.391 = (bf16[1024,1024]{1,0:T(8,128)(2,1)S(1)}, bf16[1024,1024]{1,0:T(8,128)(2,1)S(1)}, bf16[1024,768]{1,0:T(8,128)(2,1)S(1)}, bf16[768,1024]{1,0:T(8,128)(2,1)S(1)}, bf16[1024,1536]{1,0:T(8,128)(2,1)S(1)}) custom-call(s32[2]{0:T(128)S(1)} %pad_add_fusion.refs_0_, f32[2048,1024]{1,0:T(8,128)} %refs_1_.23, bf16[512,1024]{1,0:T(8,128)(2,1)} %copy-done.86, ...), custom_call_target="tpu_custom_call" | custom-call | flops 4831838208 | bytes 25690112 | tf_op jit(solution)/shard_map/pallas_call | solution.py:90
  168.4 7.6 %shard_map.392 = (f32[768,1024]{1,0:T(8,128)}, f32[8,1024]{1,0:T(8,128)S(1)}) custom-call(s32[4]{0:T(128)S(1)} %pad_add_fusion.2.refs_0_, f32[768,1024]{1,0:T(8,128)} %bitcast.99, f32[8,768]{1,0:T(8,128)S(1)} %bitcast.88, bf16[768,1024]{1,0:T(8,128)(2,1)S(1)} %get-tuple-element.137.refs_3_, bf16[768,1024]{1,0:T(8,128)(2,1)S(1)} %get-tuple-element.138.refs_4_, ...), custom_call_target="tpu_custom_call" | custom-call | flops 3221225472 | bytes 13688832 | tf_op jit(solution)/shard_map/pallas_call | solution.py:90
  176.0 5.6 %collective-permute-done.15.refs_2_.refs_3_ = bf16[512,1024]{1,0:T(8,128)(2,1)S(1)} collective-permute-done((bf16[512,1024]{1,0:T(8,128)(2,1)S(1)}, bf16[512,1024]{1,0:T(8,128)(2,1)S(1)}, u32[]{:S(2)}, u32[]{:S(2)}) %collective-permute-start.15) | collective-permute-done | bytes 1048608 | tf_op jit(solution)/shard_map/ppermute | solution.py:912
  181.6 4.1 %shard_map.393 = (bf16[512,1024]{1,0:T(8,128)(2,1)S(1)}, f32[512,1024]{1,0:T(8,128)S(1)}) custom-call(bf16[1024,1536]{1,0:T(8,128)(2,1)S(1)} %get-tuple-element.136.refs_0_.refs_6_, bf16[1024,2304]{1,0:T(8,128)(2,1)S(1)} %bitcast.70, bf16[512,1024]{1,0:T(8,128)(2,1)S(1)} %collective-permute-done.15.refs_2_.refs_3_, f32[8,1024]{1,0:T(8,128)S(1)} %get-tuple-element.141.refs_3_), custom_call_target="tpu_custom_call" | custom-call | flops 3221225472 | bytes 11010048 | tf_op jit(solution)/shard_map/pallas_call | solution.py:90
  186.3 2.6 shard_map.398
  189.3 1.5 collective-permute-start.18
  191.3 13.3 %shard_map.395 = (f32[1024,1536]{1,0:T(8,128)}, f32[8,1024]{1,0:T(8,128)S(1)}) custom-call(s32[4]{0:T(128)S(1)} %pad_add_fusion.2.refs_0_, f32[1024,1536]{1,0:T(8,128)} %bitcast.96, f32[8,1536]{1,0:T(8,128)S(1)} %bitcast.87, bf16[1024,1024]{1,0:T(8,128)(2,1)S(1)} %copy-done.79, bf16[1024,1024]{1,0:T(8,128)(2,1)S(1)} %copy-done.81, ...), custom_call_target="tpu_custom_call" | custom-call | flops 6442450944 | bytes 23150592 | tf_op jit(solution)/shard_map/pallas_call | solution.py:90
  204.8 1.5 collective-permute-start.22
  206.4 3.7 shard_map.396
  210.1 5.3 %collective-permute-done.18.refs_3_ = bf16[512,1024]{1,0:T(8,128)(2,1)S(1)} collective-permute-done((bf16[512,1024]{1,0:T(8,128)(2,1)S(1)}, bf16[512,1024]{1,0:T(8,128)(2,1)S(1)}, u32[]{:S(2)}, u32[]{:S(2)}) %collective-permute-start.18) | collective-permute-done | bytes 1048608 | tf_op jit(solution)/shard_map/ppermute | solution.py:912
  215.4 2.7 shard_map.397
  219.5 17.6 %shard_map.399 = (bf16[1024,512]{1,0:T(8,128)(2,1)S(1)}, f32[1,128]{1,0:T(1,128)S(1)}, f32[2048,256]{1,0:T(8,128)S(1)}, f32[2048,256]{1,0:T(8,128)S(1)}) custom-call(s32[8]{0:T(128)S(1)} %copy-done.69, bf16[2048,512]{1,0:T(8,128)(2,1)S(1)} %copy-done.16, bf16[2048,256]{1,0:T(8,128)(2,1)S(1)} %copy-done.31, bf16[2048,512]{1,0:T(8,128)(2,1)S(1)} %copy-done.18, ...), custom_call_target="tpu_custom_call" | custom-call | flops 6442450944 | bytes 24151040 | tf_op jit(solution)/shard_map/pallas_call | solution.py:90
  237.5 1.6 shard_map.401.refs_10_.refs_3_
  239.1 7.1 %shard_map.402 = (bf16[1024,1024]{1,0:T(8,128)(2,1)S(1)}, f32[8,1024]{1,0:T(8,128)S(1)}, f32[1,128]{1,0:T(1,128)S(1)}, bf16[512,1024]{1,0:T(8,128)(2,1)S(1)}, f32[512,1024]{1,0:T(8,128)S(1)}) custom-call(s32[2]{0:T(128)S(1)} %pad_add_fusion.1.refs_0_, bf16[1024,512]{1,0:T(8,128)(2,1)S(1)} %get-tuple-element.158.refs_1_, ...), custom_call_target="tpu_custom_call" | custom-call | flops 2147483648 | bytes 17892352 | tf_op jit(solution)/shard_map/pallas_call | solution.py:90
  246.8 2.1 collective-permute-done.23.refs_1_
  249.3 1.5 collective-permute-start.24
  251.1 6.2 %shard_map.404 = (f32[512,1024]{1,0:T(8,128)}, f32[8,1024]{1,0:T(8,128)S(1)}) custom-call(s32[4]{0:T(128)S(1)} %pad_add_fusion.2.refs_0_, f32[512,1024]{1,0:T(8,128)} %bitcast.91, f32[8,512]{1,0:T(8,128)S(1)} %bitcast.86, bf16[512,1024]{1,0:T(8,128)(2,1)S(1)} %copy-done.32, bf16[512,1024]{1,0:T(8,128)(2,1)S(1)} %copy-done.33, ...), custom_call_target="tpu_custom_call" | custom-call | flops 2147483648 | bytes 10534912 | tf_op jit(solution)/shard_map/pallas_call | solution.py:90
  257.4 16.7 %shard_map.405 = (bf16[1024,512]{1,0:T(8,128)(2,1)S(1)}, f32[1,128]{1,0:T(1,128)S(1)}, f32[1024,256]{1,0:T(8,128)S(1)}, f32[1024,256]{1,0:T(8,128)S(1)}) custom-call(s32[8]{0:T(128)S(1)} %copy-done.65, bf16[2048,512]{1,0:T(8,128)(2,1)S(1)} %copy-done.16, bf16[2048,256]{1,0:T(8,128)(2,1)S(1)} %copy-done.31, bf16[2048,512]{1,0:T(8,128)(2,1)S(1)} %copy-done.18, ...), custom_call_target="tpu_custom_call" | custom-call | flops 6442450944 | bytes 26248192 | tf_op jit(solution)/shard_map/pallas_call | solution.py:90
  274.5 7.6 %shard_map.406 = (bf16[1024,1024]{1,0:T(8,128)(2,1)S(1)}, f32[8,1024]{1,0:T(8,128)S(1)}, f32[1,128]{1,0:T(1,128)S(1)}, bf16[512,1024]{1,0:T(8,128)(2,1)S(1)}, f32[512,1024]{1,0:T(8,128)S(1)}) custom-call(s32[2]{0:T(128)S(1)} %pad_add_fusion.refs_0_, bf16[1024,512]{1,0:T(8,128)(2,1)S(1)} %get-tuple-element.164.refs_1_, ...), custom_call_target="tpu_custom_call" | custom-call | flops 2147483648 | bytes 15795200 | tf_op jit(solution)/shard_map/pallas_call | solution.py:90
  285.7 1.6 collective-permute-start.31
  287.3 3.4 shard_map.410
  290.8 5.9 %collective-permute-start.28 = (f32[8,4096]{1,0:T(8,128)S(1)}, f32[8,4096]{1,0:T(8,128)S(1)}, u32[]{:S(2)}, u32[]{:S(2)}) collective-permute-start(f32[8,4096]{1,0:T(8,128)S(1)} %shard_map.411.refs_7_.refs_0_), channel_id=1, source_target_pairs={{0,8},{4,12},{8,0},{12,4},{16,24},{20,28},{24,16},{28,20},{1,9},{5... | collective-permute-start | bytes 393224 | tf_op jit(solution)/shard_map/ppermute | solution.py:886
  296.8 7.5 %shard_map.412 = (f32[1024,1024]{1,0:T(8,128)S(1)}, f32[8,128]{1,0:T(8,128)S(1)}) custom-call(s32[4]{0:T(128)S(1)} %pad_add_fusion.2.refs_0_, f32[1024,1024]{1,0:T(8,128)} %bitcast.90, f32[8,1024]{1,0:T(8,128)S(1)} %bitcast.74, bf16[1024,2048]{1,0:T(8,128)(2,1)S(1)} %copy-done, bf16[1024,2048]{1,0:T(8,128)(2,1)S(1)} %copy-done, ...), custom_call_target="tpu_custom_call" | custom-call | flops 4294967296 | bytes 21008384 | tf_op jit(solution)/shard_map/pallas_call | solution.py:90
  307.0 4.7 %shard_map.414.refs_2_.refs_4_ = f32[2048,1024]{1,0:T(8,128)} custom-call(s32[2]{0:T(128)S(1)} %pad_add_fusion.1.refs_0_, f32[2048,1024]{1,0:T(8,128)} %refs_1_.22, bf16[512,1024]{1,0:T(8,128)(2,1)S(1)} %collective-permute-done.30.refs_2_, bf16[512,1024]{1,0:T(8,128)(2,1)S(1)} %shard_map.401.refs_10_.refs_3_, f32[8,4096]{1,0:T(8,128)S(1)} %shard_map.413.refs_4_.refs_0_), custom_call_target="tpu_custom_call" | custom-call | bytes 18874368 | tf_op jit(solution)/shard_map/pallas_call | solution.py:90
  312.8 1.9 copy-done.4
  316.9 1.7 shard_map.417
  322.1 3.3 shard_map.420
  326.8 4.9 %shard_map.421.refs_2_.refs_4_ = f32[2048,1024]{1,0:T(8,128)} custom-call(s32[2]{0:T(128)S(1)} %copy-done.67, f32[2048,1024]{1,0:T(8,128)} %refs_1_.23, bf16[512,1024]{1,0:T(8,128)(2,1)} %collective-permute-done.33.refs_2_, bf16[512,1024]{1,0:T(8,128)(2,1)} %get-tuple-element.172.refs_2_.refs_3_, f32[8,768]{1,0:T(8,128)S(1)} %get-tuple-element.177.refs_4_, ...), custom_call_target="tpu_custom_call" | custom-call | bytes 18874368 | tf_op jit(solution)/shard_map/pallas_call | solution.py:90
  333.6 3.3 shard_map.423.refs_3_.refs_2_
  337.6 2.1 collective-permute-start.37
  339.8 4.9 %shard_map.426.refs_2_ = f32[2048,1024]{1,0:T(8,128)} custom-call(s32[2]{0:T(128)S(1)} %copy-done.63, f32[2048,1024]{1,0:T(8,128)} %refs_1_.23, bf16[512,1024]{1,0:T(8,128)(2,1)} %collective-permute-done.35.refs_2_, bf16[512,1024]{1,0:T(8,128)(2,1)} %get-tuple-element.193.refs_3_, ...), custom_call_target="tpu_custom_call", output_to_operand_aliasing={{}: (4, {})} | custom-call | bytes 27262976 | tf_op jit(solution)/shard_map/pallas_call | solution.py:90
  345.9 3.1 shard_map.431
  350.9 2.0 shard_map.429
  353.0 3.5 shard_map.428
  356.5 1.5 collective-permute-start.39
  358.1 4.4 %shard_map.430 = (f32[1024,1536]{1,0:T(8,128)}, f32[128,1536]{1,0:T(8,128)}, f32[128,1536]{1,0:T(8,128)}) custom-call(f32[1024,1536]{1,0:T(8,128)S(1)} %bitcast.68, f32[8,1024]{1,0:T(8,128)S(1)} %copy-done.52, f32[8,1536]{1,0:T(8,128)S(1)} %get-tuple-element.215.refs_2_, f32[8,128]{1,0:T(8,128)S(1)} %constant_dynamic-slice_fusion.1.refs_3_, ...), custom_call_target="tpu_custom_call" | custom-call | flops 100663296 | bytes 15814656 | tf_op jit(solution)/shard_map/pallas_call | solution.py:90
  363.2 4.9 %shard_map.424 = f32[2048,1024]{1,0:T(8,128)} custom-call(s32[2]{0:T(128)S(1)} %copy-done.63, f32[2048,1024]{1,0:T(8,128)} %refs_1_.22, bf16[512,1024]{1,0:T(8,128)(2,1)} %collective-permute-done.34.refs_2_, bf16[512,1024]{1,0:T(8,128)(2,1)} %shard_map.423.refs_3_.refs_2_, f32[2048,1024]{1,0:T(8,128)} %shard_map.414.refs_2_.refs_4_), custom_call_target="tpu_custom_call", output_to_operand_aliasing={{}: (4, {})} | custom-call | bytes 27262976 | tf_op jit(solution)/shard_map/pallas_call | solution.py:90
  (333 shorter events, 51.3 us)
Async XLA Ops:
  7.2 121.9 %all-gather.2.cloned.1.call-start = ((), (), s32[]{:S(2)}) async-start(), calls=%async_computation | async-start | bytes 5308416 | tf_op jit(solution)/shard_map/all_gather | solution.py:988
  10.2 12.4 %collective-permute-start = (bf16[128,1536]{1,0:T(8,128)(2,1)}, bf16[128,1536]{1,0:T(8,128)(2,1)}, u32[]{:S(2)}, u32[]{:S(2)}) collective-permute-start(bf16[128,1536]{1,0:T(8,128)(2,1)} %pad_maximum_fusion.3.refs_6_), channel_id=1, source_target_pairs={{0,8},{8,16},{16,24},{24,28},{28,20},{20,12},{12,4},{4,0},{1,9},{9... | collective-permute-start | bytes 1179656 | tf_op jit(solution)/shard_map/ppermute | solution.py:138
  13.2 11.2 %collective-permute-start.1 = (bf16[128,1536]{1,0:T(8,128)(2,1)}, bf16[128,1536]{1,0:T(8,128)(2,1)}, u32[]{:S(2)}, u32[]{:S(2)}) collective-permute-start(bf16[128,1536]{1,0:T(8,128)(2,1)} %pad_maximum_fusion.3.refs_6_), channel_id=1, source_target_pairs={{8,0},{16,8},{24,16},{28,24},{20,28},{12,20},{4,12},{0,4},{9,1},{1... | collective-permute-start | bytes 1179656 | tf_op jit(solution)/shard_map/ppermute | solution.py:138
  18.9 24.5 %copy-start.70 = (s32[9]{0:T(128)}, s32[9]{0:T(128)S(1)}, u32[]{:S(2)}) copy-start(s32[9]{0:T(128)S(1)} %fusion.5.refs_0_.refs_6_) | copy-start | bytes 112
  19.6 17.0 %copy-start.28 = (f32[768,128]{1,0:T(8,128)S(1)}, f32[768,128]{1,0:T(8,128)}, u32[]{:S(2)}) copy-start(f32[768,128]{1,0:T(8,128)} %refs_5_.11) | copy-start | bytes 1179652
  21.5 15.1 %copy-start.13 = (f32[128,1536]{1,0:T(8,128)S(1)}, f32[128,1536]{1,0:T(8,128)}, u32[]{:S(2)}) copy-start(f32[128,1536]{1,0:T(8,128)} %refs_5_.10) | copy-start | bytes 2359300
  22.6 10.5 %collective-permute-start.2 = (bf16[128,1536]{1,0:T(8,128)(2,1)}, bf16[128,1536]{1,0:T(8,128)(2,1)S(1)}, u32[]{:S(2)}, u32[]{:S(2)}) collective-permute-start(bf16[128,1536]{1,0:T(8,128)(2,1)} %collective-permute-done.refs_7_), channel_id=1, source_target_pairs={{0,8},{8,16},{16,24},{24,28},{28,20},{20,12},{12,4},{4,0},{1,9},{9... | collective-permute-start | bytes 1179656 | tf_op jit(solution)/shard_map/ppermute | solution.py:138
  24.4 10.2 %collective-permute-start.3 = (bf16[128,1536]{1,0:T(8,128)(2,1)}, bf16[128,1536]{1,0:T(8,128)(2,1)S(1)}, u32[]{:S(2)}, u32[]{:S(2)}) collective-permute-start(bf16[128,1536]{1,0:T(8,128)(2,1)} %collective-permute-done.1.refs_8_), channel_id=1, source_target_pairs={{8,0},{16,8},{24,16},{28,24},{20,28},{12,20},{4,12},{0,4},{9,1},{1... | collective-permute-start | bytes 1179656 | tf_op jit(solution)/shard_map/ppermute | solution.py:138
  24.6 13.7 %copy-start.59 = (s32[1,2048]{1,0:T(1,128)}, s32[1,2048]{1,0:T(1,128)S(1)}, u32[]{:S(2)}) copy-start(s32[1,2048]{1,0:T(1,128)S(1)} %compare_select_fusion.refs_5_) | copy-start | bytes 24580
  33.1 9.4 %collective-permute-start.4 = (bf16[128,1536]{1,0:T(8,128)(2,1)S(1)}, bf16[128,1536]{1,0:T(8,128)(2,1)S(1)}, u32[]{:S(2)}, u32[]{:S(2)}) collective-permute-start(bf16[128,1536]{1,0:T(8,128)(2,1)S(1)} %collective-permute-done.2.refs_9_), channel_id=1, source_target_pairs={{0,8},{8,16},{16,24},{24,28},{28,20},{20,12},{12,4},{4,0},{1,9},{9... | collective-permute-start | bytes 1179656 | tf_op jit(solution)/shard_map/ppermute | solution.py:138
  34.6 8.8 %collective-permute-start.5 = (bf16[128,1536]{1,0:T(8,128)(2,1)S(1)}, bf16[128,1536]{1,0:T(8,128)(2,1)S(1)}, u32[]{:S(2)}, u32[]{:S(2)}) collective-permute-start(bf16[128,1536]{1,0:T(8,128)(2,1)S(1)} %collective-permute-done.3.refs_10_), channel_id=1, source_target_pairs={{8,0},{16,8},{24,16},{28,24},{20,28},{12,20},{4,12},{0,4},{9,1},{1... | collective-permute-start | bytes 1179656 | tf_op jit(solution)/shard_map/ppermute | solution.py:138
  45.6 23.1 %copy-start.71 = (s32[9]{0:T(128)S(1)}, s32[9]{0:T(128)}, u32[]{:S(2)}) copy-start(s32[9]{0:T(128)} %copy-done.70) | copy-start | bytes 112
  52.0 9.8 %collective-permute-start.6 = (bf16[64,1536]{1,0:T(8,128)(2,1)S(1)}, bf16[64,1536]{1,0:T(8,128)(2,1)S(1)}, u32[]{:S(2)}, u32[]{:S(2)}) collective-permute-start(bf16[64,1536]{1,0:T(8,128)(2,1)S(1)} %slice.68), channel_id=1, source_target_pairs={{0,8},{8,16},{16,24},{24,28},{28,20},{20,12},{12,4},{4,0},{1,9},{9... | collective-permute-start | bytes 589832 | tf_op jit(solution)/shard_map/ppermute | solution.py:138
  53.6 14.5 %collective-permute-start.7 = (bf16[64,1536]{1,0:T(8,128)(2,1)S(1)}, bf16[64,1536]{1,0:T(8,128)(2,1)S(1)}, u32[]{:S(2)}, u32[]{:S(2)}) collective-permute-start(bf16[64,1536]{1,0:T(8,128)(2,1)S(1)} %slice.69), channel_id=1, source_target_pairs={{8,0},{16,8},{24,16},{28,24},{20,28},{12,20},{4,12},{0,4},{9,1},{1... | collective-permute-start | bytes 589832 | tf_op jit(solution)/shard_map/ppermute | solution.py:138
  68.8 12.6 %copy-start.60 = (s32[1,2048]{1,0:T(1,128)S(1)}, s32[1,2048]{1,0:T(1,128)}, u32[]{:S(2)}) copy-start(s32[1,2048]{1,0:T(1,128)} %copy-done.59) | copy-start | bytes 24580
  68.8 12.6 %copy-start.69 = (s32[8]{0:T(128)S(1)}, s32[8]{0:T(128)}, u32[]{:S(2)}) copy-start(s32[8]{0:T(128)} %copy-done.68) | copy-start | bytes 100
  81.3 15.6 %copy-start.15 = (bf16[2048,512]{1,0:T(8,128)(2,1)}, bf16[2048,512]{1,0:T(8,128)(2,1)S(1)}, u32[]{:S(2)}) copy-start(bf16[2048,512]{1,0:T(8,128)(2,1)S(1)} %get-tuple-element.115.refs_1_) | copy-start | bytes 6291460
  81.3 15.6 %copy-start.17 = (bf16[2048,512]{1,0:T(8,128)(2,1)}, bf16[2048,512]{1,0:T(8,128)(2,1)S(1)}, u32[]{:S(2)}) copy-start(bf16[2048,512]{1,0:T(8,128)(2,1)S(1)} %get-tuple-element.117.refs_3_) | copy-start | bytes 6291460
  81.4 15.6 %copy-start.30 = (bf16[2048,256]{1,0:T(8,128)(2,1)}, bf16[2048,256]{1,0:T(8,128)(2,1)S(1)}, u32[]{:S(2)}) copy-start(bf16[2048,256]{1,0:T(8,128)(2,1)S(1)} %get-tuple-element.116.refs_2_) | copy-start | bytes 3145732
  92.5 2.7 collective-permute-start.8
  95.4 27.2 %copy-start.7 = (bf16[512,1024]{1,0:T(8,128)(2,1)}, bf16[512,1024]{1,0:T(8,128)(2,1)S(1)}, u32[]{:S(2)}) copy-start(bf16[512,1024]{1,0:T(8,128)(2,1)S(1)} %shard_map.378.refs_6_.refs_2_.refs_0_) | copy-start | bytes 3145732
  95.4 25.3 %collective-permute-start.9 = (bf16[512,1024]{1,0:T(8,128)(2,1)S(1)}, bf16[512,1024]{1,0:T(8,128)(2,1)S(1)}, u32[]{:S(2)}, u32[]{:S(2)}) collective-permute-start(bf16[512,1024]{1,0:T(8,128)(2,1)S(1)} %shard_map.378.refs_6_.refs_2_.refs_0_), channel_id=1, source_target_pairs={{0,2},{1,3},{2,0},{3,1},{4,6},{5,7},{6,4},{7,5},{8,10},{9,11},{10,... | collective-permute-start | bytes 3145736 | tf_op jit(solution)/shard_map/ppermute | solution.py:912
  106.1 14.6 %copy-start.11 = (bf16[1024,512]{1,0:T(8,128)(2,1)}, bf16[1024,512]{1,0:T(8,128)(2,1)S(1)}, u32[]{:S(2)}) copy-start(bf16[1024,512]{1,0:T(8,128)(2,1)S(1)} %get-tuple-element.122.refs_0_.refs_8_) | copy-start | bytes 3145732
  122.5 3.9 %collective-permute-start.10 = (bf16[512,1024]{1,0:T(8,128)(2,1)S(1)}, bf16[512,1024]{1,0:T(8,128)(2,1)S(1)}, u32[]{:S(2)}, u32[]{:S(2)}) collective-permute-start(bf16[512,1024]{1,0:T(8,128)(2,1)S(1)} %get-tuple-element.125), channel_id=1, source_target_pairs={{0,1},{1,0},{2,3},{3,2},{4,5},{5,4},{6,7},{7,6},{8,9},{9,8},{10,11... | collective-permute-start | bytes 3145736 | tf_op jit(solution)/shard_map/ppermute | solution.py:894
  126.0 3.1 collective-permute-start.12
  127.5 25.6 %collective-permute-start.11 = (bf16[512,1024]{1,0:T(8,128)(2,1)}, bf16[512,1024]{1,0:T(8,128)(2,1)}, u32[]{:S(2)}, u32[]{:S(2)}) collective-permute-start(bf16[512,1024]{1,0:T(8,128)(2,1)} %shard_map.383.refs_5_.refs_2_.refs_0_), channel_id=1, source_target_pairs={{0,2},{1,3},{2,0},{3,1},{4,6},{5,7},{6,4},{7,5},{8,10},{9,11},{10,... | collective-permute-start | bytes 3145736 | tf_op jit(solution)/shard_map/ppermute | solution.py:912
  129.1 178.0 %copy-start.66 = (s32[2]{0:T(128)}, s32[2]{0:T(128)S(1)}, u32[]{:S(2)}) copy-start(s32[2]{0:T(128)S(1)} %pad_add_fusion.1.refs_0_) | copy-start | bytes 28
  144.5 11.2 %collective-permute-start.14 = (bf16[512,1024]{1,0:T(8,128)(2,1)S(1)}, bf16[512,1024]{1,0:T(8,128)(2,1)S(1)}, u32[]{:S(2)}, u32[]{:S(2)}) collective-permute-start(bf16[512,1024]{1,0:T(8,128)(2,1)S(1)} %get-tuple-element.129.refs_2_), channel_id=1, source_target_pairs={{0,1},{1,0},{2,3},{3,2},{4,5},{5,4},{6,7},{7,6},{8,9},{9,8},{10,11... | collective-permute-start | bytes 3145736 | tf_op jit(solution)/shard_map/ppermute | solution.py:894
  144.8 14.7 %slice-start.4 = ((s8[4718592]{0:T(1024)(128)(4,1)}), s8[4194304]{0:T(1024)(128)(4,1)S(1)}, s32[]{:S(2)}) async-start(s8[4718592]{0:T(1024)(128)(4,1)} %bitcast.69), calls=%async_computation.5 | async-start | bytes 8388608
  155.7 2.7 collective-permute-start.13
  156.6 25.0 %collective-permute-start.15 = (bf16[512,1024]{1,0:T(8,128)(2,1)S(1)}, bf16[512,1024]{1,0:T(8,128)(2,1)S(1)}, u32[]{:S(2)}, u32[]{:S(2)}) collective-permute-start(bf16[512,1024]{1,0:T(8,128)(2,1)S(1)} %shard_map.390.refs_5_.refs_2_), channel_id=1, source_target_pairs={{0,2},{1,3},{2,0},{3,1},{4,6},{5,7},{6,4},{7,5},{8,10},{9,11},{10,... | collective-permute-start | bytes 3145736 | tf_op jit(solution)/shard_map/ppermute | solution.py:912
  158.2 116.3 %copy-start.62 = (s32[2]{0:T(128)}, s32[2]{0:T(128)S(1)}, u32[]{:S(2)}) copy-start(s32[2]{0:T(128)S(1)} %pad_add_fusion.refs_0_) | copy-start | bytes 28
  185.7 3.4 collective-permute-start.16
  185.8 18.8 %collective-permute-start.21 = (bf16[512,1024]{1,0:T(8,128)(2,1)S(1)}, bf16[512,1024]{1,0:T(8,128)(2,1)S(1)}, u32[]{:S(2)}, u32[]{:S(2)}) collective-permute-start(bf16[512,1024]{1,0:T(8,128)(2,1)S(1)} %get-tuple-element.130.refs_5_), channel_id=1, source_target_pairs={{0,1},{1,0},{2,3},{3,2},{4,5},{5,4},{6,7},{7,6},{8,9},{9,8},{10,11... | collective-permute-start | bytes 3145736 | tf_op jit(solution)/shard_map/ppermute | solution.py:894
  189.0 30.5 %copy-start.36 = (bf16[512,1024]{1,0:T(8,128)(2,1)}, bf16[512,1024]{1,0:T(8,128)(2,1)S(1)}, u32[]{:S(2)}) copy-start(bf16[512,1024]{1,0:T(8,128)(2,1)S(1)} %get-tuple-element.153.refs_15_.refs_6_) | copy-start | bytes 3145732
  189.0 30.5 %collective-permute-start.20 = (bf16[512,1024]{1,0:T(8,128)(2,1)S(1)}, bf16[512,1024]{1,0:T(8,128)(2,1)S(1)}, u32[]{:S(2)}, u32[]{:S(2)}) collective-permute-start(bf16[512,1024]{1,0:T(8,128)(2,1)S(1)} %get-tuple-element.153.refs_15_.refs_6_), channel_id=1, source_target_pairs={{0,1},{1,0},{2,3},{3,2},{4,5},{5,4},{6,7},{7,6},{8,9},{9,8},{10,11... | collective-permute-start | bytes 3145736 | tf_op jit(solution)/shard_map/ppermute | solution.py:894
  189.3 26.0 %collective-permute-start.18 = (bf16[512,1024]{1,0:T(8,128)(2,1)S(1)}, bf16[512,1024]{1,0:T(8,128)(2,1)S(1)}, u32[]{:S(2)}, u32[]{:S(2)}) collective-permute-start(bf16[512,1024]{1,0:T(8,128)(2,1)S(1)} %shard_map.394.refs_7_.refs_2_), channel_id=1, source_target_pairs={{0,2},{1,3},{2,0},{3,1},{4,6},{5,7},{6,4},{7,5},{8,10},{9,11},{10,... | collective-permute-start | bytes 3145736 | tf_op jit(solution)/shard_map/ppermute | solution.py:912
  191.3 13.3 %copy-start.23 = (f32[512,1024]{1,0:T(8,128)S(1)}, f32[512,1024]{1,0:T(8,128)}, u32[]{:S(2)}) copy-start(f32[512,1024]{1,0:T(8,128)} %get-tuple-element.160.refs_0_) | copy-start | bytes 6291460
  204.8 32.6 %collective-permute-start.22 = (bf16[512,1024]{1,0:T(8,128)(2,1)S(1)}, bf16[512,1024]{1,0:T(8,128)(2,1)}, u32[]{:S(2)}, u32[]{:S(2)}) collective-permute-start(bf16[512,1024]{1,0:T(8,128)(2,1)S(1)} %shard_map.400.refs_2_), channel_id=1, source_target_pairs={{0,2},{1,3},{2,0},{3,1},{4,6},{5,7},{6,4},{7,5},{8,10},{9,11},{10,... | collective-permute-start | bytes 3145736 | tf_op jit(solution)/shard_map/ppermute | solution.py:912
  219.5 17.6 %copy-start.38 = (bf16[512,1024]{1,0:T(8,128)(2,1)}, bf16[512,1024]{1,0:T(8,128)(2,1)S(1)}, u32[]{:S(2)}) copy-start(bf16[512,1024]{1,0:T(8,128)(2,1)S(1)} %collective-permute-done.20.refs_14_.refs_5_) | copy-start | bytes 3145732
  219.5 18.0 %copy-start.6 = (bf16[512,1024]{1,0:T(8,128)(2,1)S(1)}, bf16[512,1024]{1,0:T(8,128)(2,1)}, u32[]{:S(2)}) copy-start(bf16[512,1024]{1,0:T(8,128)(2,1)} %copy-done.5) | copy-start | bytes 3145732
  219.5 18.0 %copy-start.8 = (bf16[512,1024]{1,0:T(8,128)(2,1)S(1)}, bf16[512,1024]{1,0:T(8,128)(2,1)}, u32[]{:S(2)}) copy-start(bf16[512,1024]{1,0:T(8,128)(2,1)} %copy-done.7) | copy-start | bytes 3145732
  246.2 2.7 collective-permute-start.23
  246.3 4.5 %collective-permute-start.19 = (bf16[512,1024]{1,0:T(8,128)(2,1)S(1)}, bf16[512,1024]{1,0:T(8,128)(2,1)S(1)}, u32[]{:S(2)}, u32[]{:S(2)}) collective-permute-start(bf16[512,1024]{1,0:T(8,128)(2,1)S(1)} %get-tuple-element.150.refs_16_.refs_8_.refs_15_), channel_id=1, source_target_pairs={{0,1},{1,0},{2,3},{3,2},{4,5},{5,4},{6,7},{7,6},{8,9},{9,8},{10,11... | collective-permute-start | bytes 3145736 | tf_op jit(solution)/shard_map/ppermute | solution.py:894
  249.3 25.3 %collective-permute-start.24 = (bf16[512,1024]{1,0:T(8,128)(2,1)S(1)}, bf16[512,1024]{1,0:T(8,128)(2,1)S(1)}, u32[]{:S(2)}, u32[]{:S(2)}) collective-permute-start(bf16[512,1024]{1,0:T(8,128)(2,1)S(1)} %shard_map.403.refs_9_.refs_2_), channel_id=1, source_target_pairs={{0,2},{1,3},{2,0},{3,1},{4,6},{5,7},{6,4},{7,5},{8,10},{9,11},{10,... | collective-permute-start | bytes 3145736 | tf_op jit(solution)/shard_map/ppermute | solution.py:912
  282.2 3.2 collective-permute-start.25
  282.3 22.4 %collective-permute-start.17 = (bf16[512,1024]{1,0:T(8,128)(2,1)S(1)}, bf16[512,1024]{1,0:T(8,128)(2,1)S(1)}, u32[]{:S(2)}, u32[]{:S(2)}) collective-permute-start(bf16[512,1024]{1,0:T(8,128)(2,1)S(1)} %copy-done.35), channel_id=1, source_target_pairs={{0,1},{1,0},{2,3},{3,2},{4,5},{5,4},{6,7},{7,6},{8,9},{9,8},{10,11... | collective-permute-start | bytes 3145736 | tf_op jit(solution)/shard_map/ppermute | solution.py:894
  282.8 24.3 %collective-permute-start.30 = (bf16[512,1024]{1,0:T(8,128)(2,1)S(1)}, bf16[512,1024]{1,0:T(8,128)(2,1)S(1)}, u32[]{:S(2)}, u32[]{:S(2)}) collective-permute-start(bf16[512,1024]{1,0:T(8,128)(2,1)S(1)} %shard_map.401.refs_10_.refs_3_), channel_id=1, source_target_pairs={{0,1},{1,0},{2,3},{3,2},{4,5},{5,4},{6,7},{7,6},{8,9},{9,8},{10,11... | collective-permute-start | bytes 3145736 | tf_op jit(solution)/shard_map/ppermute | solution.py:894
  284.1 6.7 %collective-permute-start.27 = (f32[8,4096]{1,0:T(8,128)S(1)}, f32[8,4096]{1,0:T(8,128)S(1)}, u32[]{:S(2)}, u32[]{:S(2)}) collective-permute-start(f32[8,4096]{1,0:T(8,128)S(1)} %pad_maximum_fusion.4.refs_0_), channel_id=1, source_target_pairs={{0,4},{4,0},{8,12},{12,8},{16,20},{20,16},{24,28},{28,24},{1,5},{5... | collective-permute-start | bytes 393224 | tf_op jit(solution)/shard_map/ppermute | solution.py:886
  285.7 36.3 %collective-permute-start.31 = (bf16[512,1024]{1,0:T(8,128)(2,1)S(1)}, bf16[512,1024]{1,0:T(8,128)(2,1)S(1)}, u32[]{:S(2)}, u32[]{:S(2)}) collective-permute-start(bf16[512,1024]{1,0:T(8,128)(2,1)S(1)} %shard_map.407.refs_2_.refs_6_), channel_id=1, source_target_pairs={{0,2},{1,3},{2,0},{3,1},{4,6},{5,7},{6,4},{7,5},{8,10},{9,11},{10,... | collective-permute-start | bytes 3145736 | tf_op jit(solution)/shard_map/ppermute | solution.py:912
  290.8 13.5 %collective-permute-start.28 = (f32[8,4096]{1,0:T(8,128)S(1)}, f32[8,4096]{1,0:T(8,128)S(1)}, u32[]{:S(2)}, u32[]{:S(2)}) collective-permute-start(f32[8,4096]{1,0:T(8,128)S(1)} %shard_map.411.refs_7_.refs_0_), channel_id=1, source_target_pairs={{0,8},{4,12},{8,0},{12,4},{16,24},{20,28},{24,16},{28,20},{1,9},{5... | collective-permute-start | bytes 393224 | tf_op jit(solution)/shard_map/ppermute | solution.py:886
  304.3 16.2 %copy-start.2 = (f32[1024,1024]{1,0:T(8,128)}, f32[1024,1024]{1,0:T(8,128)S(1)}, u32[]{:S(2)}) copy-start(f32[1024,1024]{1,0:T(8,128)S(1)} %get-tuple-element.182.refs_1_.refs_0_) | copy-start | bytes 12582916
  304.3 8.5 %collective-permute-start.29 = (f32[8,4096]{1,0:T(8,128)S(1)}, f32[8,4096]{1,0:T(8,128)S(1)}, u32[]{:S(2)}, u32[]{:S(2)}) collective-permute-start(f32[8,4096]{1,0:T(8,128)S(1)} %shard_map.413.refs_4_.refs_0_), channel_id=1, source_target_pairs={{0,16},{4,20},{8,24},{12,28},{16,0},{20,4},{24,8},{28,12},{1,17},{... | collective-permute-start | bytes 393224 | tf_op jit(solution)/shard_map/ppermute | solution.py:886
  304.6 22.2 %collective-permute-start.33 = (bf16[512,1024]{1,0:T(8,128)(2,1)}, bf16[512,1024]{1,0:T(8,128)(2,1)}, u32[]{:S(2)}, u32[]{:S(2)}) collective-permute-start(bf16[512,1024]{1,0:T(8,128)(2,1)} %get-tuple-element.172.refs_2_.refs_3_), channel_id=1, source_target_pairs={{0,1},{1,0},{2,3},{3,2},{4,5},{5,4},{6,7},{7,6},{8,9},{9,8},{10,11... | collective-permute-start | bytes 3145736 | tf_op jit(solution)/shard_map/ppermute | solution.py:894
  304.6 12.2 %slice-start = ((s8[6291456]{0:T(1024)(128)(4,1)}), s8[4194304]{0:T(1024)(128)(4,1)S(1)}, s32[]{:S(2)}) async-start(s8[6291456]{0:T(1024)(128)(4,1)} %bitcast.65), calls=%async_computation.1 | async-start | bytes 8388608
  305.7 27.9 %collective-permute-start.26 = (bf16[512,1024]{1,0:T(8,128)(2,1)}, bf16[512,1024]{1,0:T(8,128)(2,1)}, u32[]{:S(2)}, u32[]{:S(2)}) collective-permute-start(bf16[512,1024]{1,0:T(8,128)(2,1)} %shard_map.408.refs_2_), channel_id=1, source_target_pairs={{0,2},{1,3},{2,0},{3,1},{4,6},{5,7},{6,4},{7,5},{8,10},{9,11},{10,... | collective-permute-start | bytes 3145736 | tf_op jit(solution)/shard_map/ppermute | solution.py:912
  325.4 14.4 %collective-permute-start.35 = (bf16[512,1024]{1,0:T(8,128)(2,1)}, bf16[512,1024]{1,0:T(8,128)(2,1)}, u32[]{:S(2)}, u32[]{:S(2)}) collective-permute-start(bf16[512,1024]{1,0:T(8,128)(2,1)} %get-tuple-element.193.refs_3_), channel_id=1, source_target_pairs={{0,1},{1,0},{2,3},{3,2},{4,5},{5,4},{6,7},{7,6},{8,9},{9,8},{10,11... | collective-permute-start | bytes 3145736 | tf_op jit(solution)/shard_map/ppermute | solution.py:894
  325.5 6.3 %collective-permute-start.32 = (f32[8,4128]{1,0:T(8,128)S(1)}, f32[8,4128]{1,0:T(8,128)S(1)}, u32[]{:S(2)}, u32[]{:S(2)}) collective-permute-start(f32[8,4128]{1,0:T(8,128)S(1)} %constant_dynamic-update-slice_fusion.refs_0_), channel_id=1, source_target_pairs={{0,4},{4,0},{8,12},{12,8},{16,20},{20,16},{24,28},{28,24},{1,5},{5... | collective-permute-start | bytes 396296 | tf_op jit(solution)/shard_map/ppermute | solution.py:886
  331.8 5.8 %collective-permute-start.36 = (f32[8,4128]{1,0:T(8,128)S(1)}, f32[8,4128]{1,0:T(8,128)S(1)}, u32[]{:S(2)}, u32[]{:S(2)}) collective-permute-start(f32[8,4128]{1,0:T(8,128)S(1)} %shard_map.422.refs_4_.refs_0_), channel_id=1, source_target_pairs={{0,8},{4,12},{8,0},{12,4},{16,24},{20,28},{24,16},{28,20},{1,9},{5... | collective-permute-start | bytes 396296 | tf_op jit(solution)/shard_map/ppermute | solution.py:886
  337.6 7.2 %collective-permute-start.37 = (f32[8,4128]{1,0:T(8,128)S(1)}, f32[8,4128]{1,0:T(8,128)S(1)}, u32[]{:S(2)}, u32[]{:S(2)}) collective-permute-start(f32[8,4128]{1,0:T(8,128)S(1)} %shard_map.425.refs_5_.refs_0_), channel_id=1, source_target_pairs={{0,16},{4,20},{8,24},{12,28},{16,0},{20,4},{24,8},{28,12},{1,17},{... | collective-permute-start | bytes 396296 | tf_op jit(solution)/shard_map/ppermute | solution.py:886
  339.7 23.5 %collective-permute-start.34 = (bf16[512,1024]{1,0:T(8,128)(2,1)}, bf16[512,1024]{1,0:T(8,128)(2,1)}, u32[]{:S(2)}, u32[]{:S(2)}) collective-permute-start(bf16[512,1024]{1,0:T(8,128)(2,1)} %shard_map.423.refs_3_.refs_2_), channel_id=1, source_target_pairs={{0,1},{1,0},{2,3},{3,2},{4,5},{5,4},{6,7},{7,6},{8,9},{9,8},{10,11... | collective-permute-start | bytes 3145736 | tf_op jit(solution)/shard_map/ppermute | solution.py:894
  344.8 13.3 %copy-start.45 = (f32[128,1536]{1,0:T(8,128)S(1)}, f32[128,1536]{1,0:T(8,128)}, u32[]{:S(2)}) copy-start(f32[128,1536]{1,0:T(8,128)} %refs_4_.6) | copy-start | bytes 2359300
  345.4 11.1 %collective-permute-start.38 = (f32[8,288]{1,0:T(8,128)S(1)}, f32[8,288]{1,0:T(8,128)S(1)}, u32[]{:S(2)}, u32[]{:S(2)}) collective-permute-start(f32[8,288]{1,0:T(8,128)S(1)} %slice.78.refs_0_), channel_id=1, source_target_pairs={{0,1},{1,0},{2,3},{3,2},{4,5},{5,4},{6,7},{7,6},{8,9},{9,8},{10,11... | collective-permute-start | bytes 27656 | tf_op jit(solution)/shard_map/ppermute | solution.py:886
  356.5 5.9 %collective-permute-start.39 = (f32[8,288]{1,0:T(8,128)S(1)}, f32[8,288]{1,0:T(8,128)S(1)}, u32[]{:S(2)}, u32[]{:S(2)}) collective-permute-start(f32[8,288]{1,0:T(8,128)S(1)} %shard_map.432.refs_0_), channel_id=1, source_target_pairs={{0,2},{1,3},{2,0},{3,1},{4,6},{5,7},{6,4},{7,5},{8,10},{9,11},{10,... | collective-permute-start | bytes 27656 | tf_op jit(solution)/shard_map/ppermute | solution.py:886
  (75 other events, 359.2 us)
Sparse Core Ops, SparseCore 0:
  44.4 82.1 all-gather.1

commit v3 on v2

--- a/solution.py
+++ b/solution.py
@@ -82,7 +82,8 @@
     prefetch = () if table is None else (table,)
     first = len(prefetch) + len(args)
     need = sum(block_bytes(*pair) for pair in zip(list(in_specs) + list(out_specs), list(args) + list(out_shape)))
-    need += sum(math.prod(item.shape) * jnp.dtype(item.dtype).itemsize for item in scratch) + room * MIB
+    held = [item for item in scratch if item.memory_space == pltpu.VMEM]
+    need += sum(math.prod(item.shape) * jnp.dtype(item.dtype).itemsize for item in held) + room * MIB
 
     def body(*refs):
         kernel(*refs[:first], *refs[first + len(after) :])
@@ -847,29 +848,42 @@
     )
 
 
-def spread_kernel(steps, tab_ref, base_ref, theirs_ref, mine_ref, *refs):
-    out_ref, step = refs[-1], pl.program_id(0)
-
-    @pl.when(step < steps // 2)
-    def _():
-        out_ref[...] = base_ref[...] + theirs_ref[...].astype(FULL)
-
-    @pl.when(step >= steps // 2)
-    def _():
-        out_ref[...] = base_ref[...] + mine_ref[...].astype(FULL)
+def spread_kernel(tab_ref, base_ref, theirs_ref, mine_ref, *refs):
+    out_ref, rows_scr, in_sems, out_sems = refs[-4:]
+    half = theirs_ref.shape[0]
+    count, block = rows_scr.shape[0], rows_scr.shape[1]
+    each = half // block
+    copies_in, copies_out = [], []
+    for number in range(count):
+        place = tab_ref[number // each] * half + number % each * block
+        rows = pl.ds(pl.multiple_of(place, block), block)
+        copies_in.append(pltpu.make_async_copy(base_ref.at[rows, :], rows_scr.at[number], in_sems.at[number]))
+        copies_out.append(pltpu.make_async_copy(rows_scr.at[number], out_ref.at[rows, :], out_sems.at[number]))
+        copies_in[number].start()
+    for number in range(count):
+        copies_in[number].wait()
+        piece = theirs_ref if number < each else mine_ref
+        at = number % each * block
+        rows_scr[number] = rows_scr[number] + piece[at : at + block, :].astype(FULL)
+        copies_out[number].start()
+    for number in range(count):
+        copies_out[number].wait()
 
 
 def spread(table, base, pieces, before, after=()):
     half = pieces[0].shape[0]
+    count = 2 * half // BLOCK
     extra = [] if before is None else [far(before)]
-    rows = pl.BlockSpec((half, D), lambda i, tab: (tab[i], 0))
-    return call(
-        functools.partial(spread_kernel, 2),
-        (2,),
-        [rows, whole(half, D), whole(half, D)] + [pl.BlockSpec(memory_space=pl.ANY)] * len(extra),
-        [rows],
+    anywhere = pl.BlockSpec(memory_space=pl.ANY)
+    return call(
+        spread_kernel,
+        (1,),
+        [anywhere, whole(half, D), whole(half, D)] + [anywhere] * len(extra),
+        [anywhere],
         [far_shape(base.shape, FULL)],
         [far(base)] + list(pieces) + extra,
+        scratch=[pltpu.VMEM((count, BLOCK, D), FULL), pltpu.SemaphoreType.DMA((count,)),
+                 pltpu.SemaphoreType.DMA((count,))],
         table=table,
         aliases={4: 0} if extra else None,
         after=after,
@@ -985,7 +999,7 @@
     first_b, queries, keys, values, keys_t, raw_q, raw_k = make_qkv(
         shard_places, h_att, first_pieces, g_query, g_key, cosine, sine, q_heads, kv_heads, ()
     )
-    second_b = lax.all_gather(stage(second_own, first_steps[-2] + (far(cosine), far(sine), far(key_col), shard_places) + tuple(tables)), "dp", axis=0, tiled=True)
+    second_b = lax.all_gather(stage(second_own, first_steps[-1] + (far(cosine), far(sine), far(key_col), shard_places) + tuple(tables)), "dp", axis=0, tiled=True)
 
     att, att_t, log_total, att_sum = {}, {}, {}, {}
     after, arrived = (), ()
@@ -1014,7 +1028,7 @@
         )
         h_pieces[chunk] = pieces_of(h_own, parts)
         h_mlp_t[chunk], d_mlp[chunk], activ[chunk], activ_t[chunk], d_gu[chunk] = feed_forward(
-            half_tables[chunk], out_grad, second_b, h_pieces[chunk], after
+            half_tables[chunk], out_grad, far(second_b) if chunk == order[0] else second_b, h_pieces[chunk], after
         )
         if chunk == order[-1]:
             merged_down, p_down = merge_grad(

time: 383 us -> 382 us (level)
  waiting for transfers between devices: 58.7 us -> 63.2 us
  local copies, waits for them, and re-layouts: 21.3 us -> 17.2 us
    all_gather x1, waiting for transfers between devices: 0.01 us -> 12.1 us  [local(): lax.all_gather(stage(second_own, first_steps[-1] + (far(cosine), far(sine...]
    ppermute x4, waiting for transfers between devices: 7.19 us -> 1.86 us  [ring_step(): lax.ppermute(from_right, 'dp', back)]
    unnamed x202 -> x190, local copies, waits for them, and re-layouts: 13.6 us -> 9.63 us
  transfers between devices with their start and end apart: 41 -> 41, of which waited for: 18 -> 17; matrix products, arithmetic and copies ran while one was open for 4% -> 4% of each run, Pallas kernels for 55% -> 55%
where the time goes in v3:
time: 382 us; the launch traced here: 376 us
  Pallas kernels  234 us (61%)
  waiting for transfers between devices  63.2 us (17%)
  starting transfers between devices  35.9 us (9%)
  local copies, waits for them, and re-layouts  17.2 us (5%)
  between operations  15.7 us (4%)
  other arithmetic  9.73 us (3%)
    pallas_call x60, Pallas kernels, call(): pl.pallas_call(body, grid_spec=pltpu.PrefetchScalarGridSpec(num_scalar_pr...  234 us
    ppermute x8, waiting for transfers between devices, across_chips(): other = lax.ppermute(part, 'tensor', [(i, i ^ span) for i in range(count)])  24.6 us
    ppermute x4, waiting for transfers between devices, ring_step(): lax.ppermute(from_left, 'dp', ahead)  17.4 us
    all_gather x1, waiting for transfers between devices, local(): lax.all_gather(stage(second_own, first_steps[-1] + (far(cosine), far(sine...  12.1 us
    ppermute x8, starting transfers between devices, across_chips(): other = lax.ppermute(part, 'tensor', [(i, i ^ span) for i in range(count)])  12 us
    ppermute x8, starting transfers between devices, butterfly_step(): other = lax.ppermute(values, axis, [(i, i ^ span) for i in range(count)])  11 us
    unnamed x190, local copies, waits for them, and re-layouts  9.63 us
    ppermute x4, starting transfers between devices, ring_step(): lax.ppermute(from_left, 'dp', ahead)  7.67 us
  transfers between devices with their start and end apart: 41, of which 17 were waited for; matrix products, arithmetic and copies ran while one was open for 4% of the time, Pallas kernels for 55%

profile of v3, /device:TPU:0, one launch (start us, length us, event | category | flops | bytes accessed | tf_op | source)
XLA Modules:
  0.0 376.1 jit_solution(3571117868295274810)
XLA Ops:
  10.1 3.0 collective-permute-start
  14.9 3.9 %fusion.2 = (f32[2048,64]{1,0:T(8,128)S(1)}, f32[2048,64]{1,0:T(8,128)S(1)}, f32[2048,64]{1,0:T(8,128)S(1)}) fusion(f32[64]{0:T(128)S(1)} %negate_power_fusion), kind=kLoop, calls=%fused_computation.8 | loop fusion | flops 262144 | bytes 1573120 | tf_op jit(solution)/shard_map/neg | solution.py:125
  18.9 2.0 pad_maximum_fusion
  20.9 1.7 collective-permute-done.refs_7_
  22.5 1.8 collective-permute-start.2
  24.6 8.5 %collective-permute-done.2.refs_9_ = bf16[128,1536]{1,0:T(8,128)(2,1)S(1)} collective-permute-done((bf16[128,1536]{1,0:T(8,128)(2,1)}, bf16[128,1536]{1,0:T(8,128)(2,1)S(1)}, u32[]{:S(2)}, u32[]{:S(2)}) %collective-permute-start.2) | collective-permute-done | bytes 393248 | tf_op jit(solution)/shard_map/ppermute | solution.py:139
  38.2 4.2 %collective-permute-done.4.refs_11_ = bf16[128,1536]{1,0:T(8,128)(2,1)S(1)} collective-permute-done((bf16[128,1536]{1,0:T(8,128)(2,1)S(1)}, bf16[128,1536]{1,0:T(8,128)(2,1)S(1)}, u32[]{:S(2)}, u32[]{:S(2)}) %collective-permute-start.4) | collective-permute-done | bytes 393248 | tf_op jit(solution)/shard_map/ppermute | solution.py:139
  45.1 3.1 collective-permute-done.6.refs_13_.refs_1_
  48.2 1.8 collective-permute-done.7.refs_14_.refs_2_
  52.3 6.3 %shard_map.374.refs_1_.refs_0_ = bf16[2048,1024]{1,0:T(8,128)(2,1)S(1)} custom-call(f32[2048,1024]{1,0:T(8,128)} %refs_1_.22, f32[1,1024]{1,0:T(1,128)S(1)} %bitcast.80), custom_call_target="tpu_custom_call" | custom-call | bytes 12587008 | tf_op jit(solution)/shard_map/pallas_call | solution.py:91
  58.7 12.8 %shard_map.375 = (bf16[1024,1536]{1,0:T(8,128)(2,1)S(1)}, bf16[2048,512]{1,0:T(8,128)(2,1)S(1)}, bf16[2048,256]{1,0:T(8,128)(2,1)S(1)}, bf16[2048,512]{1,0:T(8,1...) custom-call(s32[9]{0:T(128)S(1)} %copy-done.65, ...), custom_call_target="tpu_custom_call" | custom-call | flops 4294967296 | bytes 25166848 | tf_op jit(solution)/shard_map/pallas_call | solution.py:91
  71.5 9.2 %shard_map.376 = (bf16[1024,512]{1,0:T(8,128)(2,1)S(1)}, bf16[512,1024]{1,0:T(8,128)(2,1)}, f32[4,1024]{1,0:T(4,128)S(1)}) custom-call(s32[8]{0:T(128)S(1)} %copy-done.63, bf16[2048,512]{1,0:T(8,128)(2,1)S(1)} %get-tuple-element.115.refs_1_, bf16[2048,256]{1,0:T(8,128)(2,1)S(1)} %get-tuple-element.116.refs_2_, ...), custom_call_target="tpu_custom_call" | custom-call | flops 3221225472 | bytes 7372800 | tf_op jit(solution)/shard_map/pallas_call | solution.py:91
  80.7 1.8 shard_map.377
  82.6 2.6 collective-permute-done.8.refs_1_
  85.5 1.6 collective-permute-start.9
  87.1 9.1 %shard_map.379 = (bf16[1024,512]{1,0:T(8,128)(2,1)S(1)}, bf16[512,1024]{1,0:T(8,128)(2,1)}, f32[4,1024]{1,0:T(4,128)S(1)}) custom-call(s32[8]{0:T(128)S(1)} %copy-done.61, bf16[2048,512]{1,0:T(8,128)(2,1)S(1)} %get-tuple-element.115.refs_1_, bf16[2048,256]{1,0:T(8,128)(2,1)S(1)} %get-tuple-element.116.refs_2_, ...), custom_call_target="tpu_custom_call" | custom-call | flops 3221225472 | bytes 7372800 | tf_op jit(solution)/shard_map/pallas_call | solution.py:91
  96.2 3.7 shard_map.380.refs_1_.refs_0_
  99.9 4.2 %shard_map.381.refs_3_.refs_1_.refs_4_ = bf16[1024,2048]{1,0:T(8,128)(2,1)} custom-call(bf16[2048,1024]{1,0:T(8,128)(2,1)S(1)} %shard_map.374.refs_1_.refs_0_, f32[8,1024]{1,0:T(8,128)S(1)} %shard_map.380.refs_1_.refs_0_), custom_call_target="tpu_custom_call" | custom-call | bytes 8388608 | tf_op jit(solution)/shard_map/pallas_call | solution.py:91
  104.0 6.8 %collective-permute-done.9.refs_2_.refs_3_.refs_1_ = bf16[512,1024]{1,0:T(8,128)(2,1)S(1)} collective-permute-done((bf16[512,1024]{1,0:T(8,128)(2,1)S(1)}, bf16[512,1024]{1,0:T(8,128)(2,1)S(1)}, u32[]{:S(2)}, u32[]{:S(2)}) %collective-permute-start.9) | collective-permute-done | bytes 1048608 | tf_op jit(solution)/shard_map/ppermute | solution.py:926
  110.8 1.8 shard_map.382
  112.7 1.9 shard_map.384
  119.2 12.1 %all-gather.2.cloned.1.call-done.refs_4_.refs_1_ = bf16[1024,2304]{1,0:T(8,128)(2,1)} async-done(((bf16[128,2304]{1,0:T(8,128)(2,1)}), bf16[1024,2304]{1,0:T(8,128)(2,1)}) %all-gather.2.cloned.1.call-update) | async-done | bytes 4718608 | tf_op jit(solution)/shard_map/all_gather | solution.py:1002
  131.3 10.7 %shard_map.386 = (bf16[1024,1024]{1,0:T(8,128)(2,1)S(1)}, bf16[1024,1024]{1,0:T(8,128)(2,1)S(1)}, bf16[1024,768]{1,0:T(8,128)(2,1)S(1)}, bf16[768,1024]{1,0:T(8,128)(2,1)S(1)}, bf16[1024,1536]{1,0:T(8,128)(2,1)S(1)}) custom-call(s32[2]{0:T(128)S(1)} %pad_add_fusion.1.refs_0_, f32[2048,1024]{1,0:T(8,128)} %refs_1_.23, ...), custom_call_target="tpu_custom_call" | custom-call | flops 4831838208 | bytes 25690112 | tf_op jit(solution)/shard_map/pallas_call | solution.py:91
  142.0 4.1 %shard_map.387 = (bf16[512,1024]{1,0:T(8,128)(2,1)S(1)}, f32[512,1024]{1,0:T(8,128)S(1)}) custom-call(bf16[1024,1536]{1,0:T(8,128)(2,1)S(1)} %get-tuple-element.128.refs_0_.refs_5_, bf16[1024,2304]{1,0:T(8,128)(2,1)S(1)} %copy-done.1), custom_call_target="tpu_custom_call" | custom-call | flops 3221225472 | bytes 11010048 | tf_op jit(solution)/shard_map/pallas_call | solution.py:91
  146.2 3.9 %shard_map.388 = (bf16[512,1024]{1,0:T(8,128)(2,1)S(1)}, f32[512,1024]{1,0:T(8,128)}) custom-call(bf16[1024,768]{1,0:T(8,128)(2,1)S(1)} %get-tuple-element.127.refs_0_, bf16[1024,2304]{1,0:T(8,128)(2,1)S(1)} %copy-done.1, bf16[512,1024]{1,0:T(8,128)(2,1)S(1)} %get-tuple-element.129.refs_2_), custom_call_target="tpu_custom_call" | custom-call | flops 1610612736 | bytes 9437184 | tf_op jit(solution)/shard_map/pallas_call | solution.py:91
  150.1 2.5 shard_map.389
  156.4 8.9 %shard_map.391 = (bf16[1024,1024]{1,0:T(8,128)(2,1)S(1)}, bf16[1024,1024]{1,0:T(8,128)(2,1)S(1)}, bf16[1024,768]{1,0:T(8,128)(2,1)S(1)}, bf16[768,1024]{1,0:T(8,128)(2,1)S(1)}, bf16[1024,1536]{1,0:T(8,128)(2,1)S(1)}) custom-call(s32[2]{0:T(128)S(1)} %pad_add_fusion.refs_0_, f32[2048,1024]{1,0:T(8,128)} %refs_1_.23, bf16[512,1024]{1,0:T(8,128)(2,1)} %copy-done.84, ...), custom_call_target="tpu_custom_call" | custom-call | flops 4831838208 | bytes 25690112 | tf_op jit(solution)/shard_map/pallas_call | solution.py:91
  165.4 7.6 %shard_map.392 = (f32[768,1024]{1,0:T(8,128)}, f32[8,1024]{1,0:T(8,128)S(1)}) custom-call(s32[4]{0:T(128)S(1)} %pad_add_fusion.2.refs_0_, f32[768,1024]{1,0:T(8,128)} %bitcast.97, f32[8,768]{1,0:T(8,128)S(1)} %bitcast.86, bf16[768,1024]{1,0:T(8,128)(2,1)S(1)} %copy-done.77, bf16[768,1024]{1,0:T(8,128)(2,1)S(1)} %get-tuple-element.138.refs_4_, ...), custom_call_target="tpu_custom_call" | custom-call | flops 3221225472 | bytes 13688832 | tf_op jit(solution)/shard_map/pallas_call | solution.py:91
  173.0 6.1 %collective-permute-done.15.refs_2_.refs_3_ = bf16[512,1024]{1,0:T(8,128)(2,1)S(1)} collective-permute-done((bf16[512,1024]{1,0:T(8,128)(2,1)S(1)}, bf16[512,1024]{1,0:T(8,128)(2,1)S(1)}, u32[]{:S(2)}, u32[]{:S(2)}) %collective-permute-start.15) | collective-permute-done | bytes 1048608 | tf_op jit(solution)/shard_map/ppermute | solution.py:926
  179.2 4.1 %shard_map.393 = (bf16[512,1024]{1,0:T(8,128)(2,1)S(1)}, f32[512,1024]{1,0:T(8,128)S(1)}) custom-call(bf16[1024,1536]{1,0:T(8,128)(2,1)S(1)} %get-tuple-element.136.refs_0_.refs_6_, bf16[1024,2304]{1,0:T(8,128)(2,1)S(1)} %copy-done.1, bf16[512,1024]{1,0:T(8,128)(2,1)S(1)} %collective-permute-done.15.refs_2_.refs_3_, f32[8,1024]{1,0:T(8,128)S(1)} %get-tuple-element.141.refs_3_), custom_call_target="tpu_custom_call" | custom-call | flops 3221225472 | bytes 11010048 | tf_op jit(solution)/shard_map/pallas_call | solution.py:91
  183.8 2.6 shard_map.398
  186.9 1.5 collective-permute-start.18
  188.8 13.3 %shard_map.395 = (f32[1024,1536]{1,0:T(8,128)}, f32[8,1024]{1,0:T(8,128)S(1)}) custom-call(s32[4]{0:T(128)S(1)} %pad_add_fusion.2.refs_0_, f32[1024,1536]{1,0:T(8,128)} %bitcast.94, f32[8,1536]{1,0:T(8,128)S(1)} %bitcast.85, bf16[1024,1024]{1,0:T(8,128)(2,1)S(1)} %copy-done.73, bf16[1024,1024]{1,0:T(8,128)(2,1)S(1)} %copy-done.75, ...), custom_call_target="tpu_custom_call" | custom-call | flops 6442450944 | bytes 23150592 | tf_op jit(solution)/shard_map/pallas_call | solution.py:91
  202.3 1.5 collective-permute-start.22
  203.9 3.7 shard_map.396
  207.6 5.3 %collective-permute-done.18.refs_3_ = bf16[512,1024]{1,0:T(8,128)(2,1)S(1)} collective-permute-done((bf16[512,1024]{1,0:T(8,128)(2,1)S(1)}, bf16[512,1024]{1,0:T(8,128)(2,1)S(1)}, u32[]{:S(2)}, u32[]{:S(2)}) %collective-permute-start.18) | collective-permute-done | bytes 1048608 | tf_op jit(solution)/shard_map/ppermute | solution.py:926
  212.9 2.7 shard_map.397
  217.1 17.5 %shard_map.399 = (bf16[1024,512]{1,0:T(8,128)(2,1)S(1)}, f32[1,128]{1,0:T(1,128)S(1)}, f32[2048,256]{1,0:T(8,128)S(1)}, f32[2048,256]{1,0:T(8,128)S(1)}) custom-call(s32[8]{0:T(128)S(1)} %copy-done.63, bf16[2048,512]{1,0:T(8,128)(2,1)S(1)} %copy-done.16, bf16[2048,256]{1,0:T(8,128)(2,1)S(1)} %copy-done.31, bf16[2048,512]{1,0:T(8,128)(2,1)S(1)} %copy-done.18, ...), custom_call_target="tpu_custom_call" | custom-call | flops 6442450944 | bytes 24151040 | tf_op jit(solution)/shard_map/pallas_call | solution.py:91
  235.0 1.6 shard_map.401.refs_10_.refs_3_
  236.7 7.2 %shard_map.402 = (bf16[1024,1024]{1,0:T(8,128)(2,1)S(1)}, f32[8,1024]{1,0:T(8,128)S(1)}, f32[1,128]{1,0:T(1,128)S(1)}, bf16[512,1024]{1,0:T(8,128)(2,1)S(1)}, f32[512,1024]{1,0:T(8,128)S(1)}) custom-call(s32[2]{0:T(128)S(1)} %pad_add_fusion.1.refs_0_, bf16[1024,512]{1,0:T(8,128)(2,1)S(1)} %get-tuple-element.158.refs_1_, ...), custom_call_target="tpu_custom_call" | custom-call | flops 2147483648 | bytes 17892352 | tf_op jit(solution)/shard_map/pallas_call | solution.py:91
  244.4 2.1 collective-permute-done.23.refs_1_
  246.9 1.5 collective-permute-start.24
  248.7 6.2 %shard_map.404 = (f32[512,1024]{1,0:T(8,128)}, f32[8,1024]{1,0:T(8,128)S(1)}) custom-call(s32[4]{0:T(128)S(1)} %pad_add_fusion.2.refs_0_, f32[512,1024]{1,0:T(8,128)} %bitcast.89, f32[8,512]{1,0:T(8,128)S(1)} %bitcast.84, bf16[512,1024]{1,0:T(8,128)(2,1)S(1)} %copy-done.32, bf16[512,1024]{1,0:T(8,128)(2,1)S(1)} %copy-done.33, ...), custom_call_target="tpu_custom_call" | custom-call | flops 2147483648 | bytes 10534912 | tf_op jit(solution)/shard_map/pallas_call | solution.py:91
  254.9 16.7 %shard_map.405 = (bf16[1024,512]{1,0:T(8,128)(2,1)S(1)}, f32[1,128]{1,0:T(1,128)S(1)}, f32[1024,256]{1,0:T(8,128)S(1)}, f32[1024,256]{1,0:T(8,128)S(1)}) custom-call(s32[8]{0:T(128)S(1)} %copy-done.61, bf16[2048,512]{1,0:T(8,128)(2,1)S(1)} %copy-done.16, bf16[2048,256]{1,0:T(8,128)(2,1)S(1)} %copy-done.31, bf16[2048,512]{1,0:T(8,128)(2,1)S(1)} %copy-done.18, ...), custom_call_target="tpu_custom_call" | custom-call | flops 6442450944 | bytes 26248192 | tf_op jit(solution)/shard_map/pallas_call | solution.py:91
  272.1 7.7 %shard_map.406 = (bf16[1024,1024]{1,0:T(8,128)(2,1)S(1)}, f32[8,1024]{1,0:T(8,128)S(1)}, f32[1,128]{1,0:T(1,128)S(1)}, bf16[512,1024]{1,0:T(8,128)(2,1)S(1)}, f32[512,1024]{1,0:T(8,128)S(1)}) custom-call(s32[2]{0:T(128)S(1)} %pad_add_fusion.refs_0_, bf16[1024,512]{1,0:T(8,128)(2,1)S(1)} %get-tuple-element.164.refs_1_, ...), custom_call_target="tpu_custom_call" | custom-call | flops 2147483648 | bytes 15795200 | tf_op jit(solution)/shard_map/pallas_call | solution.py:91
  281.7 3.6 collective-permute-start.27
  285.5 1.5 collective-permute-start.31
  287.1 3.4 shard_map.410
  291.3 7.5 %shard_map.412 = (f32[1024,1024]{1,0:T(8,128)S(1)}, f32[8,128]{1,0:T(8,128)S(1)}) custom-call(s32[4]{0:T(128)S(1)} %pad_add_fusion.2.refs_0_, f32[1024,1024]{1,0:T(8,128)} %bitcast.88, f32[8,1024]{1,0:T(8,128)S(1)} %bitcast.72, bf16[1024,2048]{1,0:T(8,128)(2,1)S(1)} %copy-done, bf16[1024,2048]{1,0:T(8,128)(2,1)S(1)} %copy-done, ...), custom_call_target="tpu_custom_call" | custom-call | flops 4294967296 | bytes 21008384 | tf_op jit(solution)/shard_map/pallas_call | solution.py:91
  298.9 1.5 collective-permute-start.29
  302.9 4.0 %shard_map.414.refs_2_.refs_4_ = f32[2048,1024]{1,0:T(8,128)} custom-call(s32[2]{0:T(128)S(1)} %pad_add_fusion.1.refs_0_, f32[2048,1024]{1,0:T(8,128)} %refs_1_.22, bf16[512,1024]{1,0:T(8,128)(2,1)S(1)} %collective-permute-done.30.refs_2_, bf16[512,1024]{1,0:T(8,128)(2,1)S(1)} %shard_map.401.refs_10_.refs_3_, f32[8,4096]{1,0:T(8,128)S(1)} %shard_map.413.refs_4_.refs_0_), custom_call_target="tpu_custom_call" | custom-call | bytes 18874368 | tf_op jit(solution)/shard_map/pallas_call | solution.py:91
  307.7 1.8 copy-done.4
  311.7 1.7 shard_map.417
  316.9 3.3 shard_map.420
  321.7 5.5 %shard_map.421.refs_2_.refs_4_ = f32[2048,1024]{1,0:T(8,128)} custom-call(s32[2]{0:T(128)S(1)} %pad_add_fusion.1.refs_0_, f32[2048,1024]{1,0:T(8,128)} %refs_1_.23, bf16[512,1024]{1,0:T(8,128)(2,1)} %collective-permute-done.33.refs_2_, bf16[512,1024]{1,0:T(8,128)(2,1)} %get-tuple-element.172.refs_2_.refs_3_, f32[8,768]{1,0:T(8,128)S(1)} %get-tuple-element.177.refs_4_, ...), custom_call_target="tpu_custom_call" | custom-call | bytes 18874368 | tf_op jit(solution)/shard_map/pallas_call | solution.py:91
  327.9 5.5 %collective-permute-done.26.refs_3_ = bf16[512,1024]{1,0:T(8,128)(2,1)} collective-permute-done((bf16[512,1024]{1,0:T(8,128)(2,1)}, bf16[512,1024]{1,0:T(8,128)(2,1)}, u32[]{:S(2)}, u32[]{:S(2)}) %collective-permute-start.26) | collective-permute-done | bytes 1048608 | tf_op jit(solution)/shard_map/ppermute | solution.py:926
  333.4 3.2 shard_map.423.refs_3_.refs_2_
  336.6 1.7 collective-permute-start.37
  338.5 5.5 %shard_map.426.refs_2_ = f32[2048,1024]{1,0:T(8,128)} custom-call(s32[2]{0:T(128)S(1)} %pad_add_fusion.refs_0_, f32[2048,1024]{1,0:T(8,128)} %refs_1_.23, bf16[512,1024]{1,0:T(8,128)(2,1)} %collective-permute-done.35.refs_2_, bf16[512,1024]{1,0:T(8,128)(2,1)} %get-tuple-element.193.refs_3_, ...), custom_call_target="tpu_custom_call", output_to_operand_aliasing={{}: (4, {})} | custom-call | bytes 27262976 | tf_op jit(solution)/shard_map/pallas_call | solution.py:91
  346.0 3.1 shard_map.431
  351.0 2.0 shard_map.429
  353.1 3.5 shard_map.428
  358.2 4.4 %shard_map.430 = (f32[1024,1536]{1,0:T(8,128)}, f32[128,1536]{1,0:T(8,128)}, f32[128,1536]{1,0:T(8,128)}) custom-call(f32[1024,1536]{1,0:T(8,128)S(1)} %bitcast.68, f32[8,1024]{1,0:T(8,128)S(1)} %copy-done.52, f32[8,1536]{1,0:T(8,128)S(1)} %get-tuple-element.215.refs_2_, f32[8,128]{1,0:T(8,128)S(1)} %constant_dynamic-slice_fusion.1.refs_3_, ...), custom_call_target="tpu_custom_call" | custom-call | flops 100663296 | bytes 15814656 | tf_op jit(solution)/shard_map/pallas_call | solution.py:91
  363.3 5.5 %shard_map.424 = f32[2048,1024]{1,0:T(8,128)} custom-call(s32[2]{0:T(128)S(1)} %pad_add_fusion.refs_0_, f32[2048,1024]{1,0:T(8,128)} %refs_1_.22, bf16[512,1024]{1,0:T(8,128)(2,1)} %collective-permute-done.34.refs_2_, bf16[512,1024]{1,0:T(8,128)(2,1)} %shard_map.423.refs_3_.refs_2_, ...), custom_call_target="tpu_custom_call", output_to_operand_aliasing={{}: (4, {})} | custom-call | bytes 27262976 | tf_op jit(solution)/shard_map/pallas_call | solution.py:91
  (320 shorter events, 49.2 us)
Async XLA Ops:
  7.2 124.1 %all-gather.2.cloned.1.call-start = ((), (), s32[]{:S(2)}) async-start(), calls=%async_computation | async-start | bytes 5308416 | tf_op jit(solution)/shard_map/all_gather | solution.py:1002
  10.1 12.4 %collective-permute-start = (bf16[128,1536]{1,0:T(8,128)(2,1)}, bf16[128,1536]{1,0:T(8,128)(2,1)}, u32[]{:S(2)}, u32[]{:S(2)}) collective-permute-start(bf16[128,1536]{1,0:T(8,128)(2,1)} %pad_maximum_fusion.3.refs_6_), channel_id=1, source_target_pairs={{0,8},{8,16},{16,24},{24,28},{28,20},{20,12},{12,4},{4,0},{1,9},{9... | collective-permute-start | bytes 1179656 | tf_op jit(solution)/shard_map/ppermute | solution.py:139
  13.2 11.2 %collective-permute-start.1 = (bf16[128,1536]{1,0:T(8,128)(2,1)}, bf16[128,1536]{1,0:T(8,128)(2,1)}, u32[]{:S(2)}, u32[]{:S(2)}) collective-permute-start(bf16[128,1536]{1,0:T(8,128)(2,1)} %pad_maximum_fusion.3.refs_6_), channel_id=1, source_target_pairs={{8,0},{16,8},{24,16},{28,24},{20,28},{12,20},{4,12},{0,4},{9,1},{1... | collective-permute-start | bytes 1179656 | tf_op jit(solution)/shard_map/ppermute | solution.py:139
  18.9 17.5 %copy-start.28 = (f32[768,128]{1,0:T(8,128)S(1)}, f32[768,128]{1,0:T(8,128)}, u32[]{:S(2)}) copy-start(f32[768,128]{1,0:T(8,128)} %refs_5_.11) | copy-start | bytes 1179652
  20.9 15.6 %copy-start.13 = (f32[128,1536]{1,0:T(8,128)S(1)}, f32[128,1536]{1,0:T(8,128)}, u32[]{:S(2)}) copy-start(f32[128,1536]{1,0:T(8,128)} %refs_5_.10) | copy-start | bytes 2359300
  22.5 10.5 %collective-permute-start.2 = (bf16[128,1536]{1,0:T(8,128)(2,1)}, bf16[128,1536]{1,0:T(8,128)(2,1)S(1)}, u32[]{:S(2)}, u32[]{:S(2)}) collective-permute-start(bf16[128,1536]{1,0:T(8,128)(2,1)} %collective-permute-done.refs_7_), channel_id=1, source_target_pairs={{0,8},{8,16},{16,24},{24,28},{28,20},{20,12},{12,4},{4,0},{1,9},{9... | collective-permute-start | bytes 1179656 | tf_op jit(solution)/shard_map/ppermute | solution.py:139
  24.3 10.2 %collective-permute-start.3 = (bf16[128,1536]{1,0:T(8,128)(2,1)}, bf16[128,1536]{1,0:T(8,128)(2,1)S(1)}, u32[]{:S(2)}, u32[]{:S(2)}) collective-permute-start(bf16[128,1536]{1,0:T(8,128)(2,1)} %collective-permute-done.1.refs_8_), channel_id=1, source_target_pairs={{8,0},{16,8},{24,16},{28,24},{20,28},{12,20},{4,12},{0,4},{9,1},{1... | collective-permute-start | bytes 1179656 | tf_op jit(solution)/shard_map/ppermute | solution.py:139
  33.1 9.4 %collective-permute-start.4 = (bf16[128,1536]{1,0:T(8,128)(2,1)S(1)}, bf16[128,1536]{1,0:T(8,128)(2,1)S(1)}, u32[]{:S(2)}, u32[]{:S(2)}) collective-permute-start(bf16[128,1536]{1,0:T(8,128)(2,1)S(1)} %collective-permute-done.2.refs_9_), channel_id=1, source_target_pairs={{0,8},{8,16},{16,24},{24,28},{28,20},{20,12},{12,4},{4,0},{1,9},{9... | collective-permute-start | bytes 1179656 | tf_op jit(solution)/shard_map/ppermute | solution.py:139
  34.5 9.3 %collective-permute-start.5 = (bf16[128,1536]{1,0:T(8,128)(2,1)S(1)}, bf16[128,1536]{1,0:T(8,128)(2,1)S(1)}, u32[]{:S(2)}, u32[]{:S(2)}) collective-permute-start(bf16[128,1536]{1,0:T(8,128)(2,1)S(1)} %collective-permute-done.3.refs_10_), channel_id=1, source_target_pairs={{8,0},{16,8},{24,16},{28,24},{20,28},{12,20},{4,12},{0,4},{9,1},{1... | collective-permute-start | bytes 1179656 | tf_op jit(solution)/shard_map/ppermute | solution.py:139
  38.0 12.9 %copy-start.60 = (s32[8]{0:T(128)}, s32[8]{0:T(128)S(1)}, u32[]{:S(2)}) copy-start(s32[8]{0:T(128)S(1)} %concatenate.73.refs_0_.refs_7_) | copy-start | bytes 100
  38.1 12.8 %copy-start.62 = (s32[8]{0:T(128)}, s32[8]{0:T(128)S(1)}, u32[]{:S(2)}) copy-start(s32[8]{0:T(128)S(1)} %concatenate.77.refs_0_.refs_8_) | copy-start | bytes 100
  42.5 5.7 %collective-permute-start.6 = (bf16[64,1536]{1,0:T(8,128)(2,1)S(1)}, bf16[64,1536]{1,0:T(8,128)(2,1)S(1)}, u32[]{:S(2)}, u32[]{:S(2)}) collective-permute-start(bf16[64,1536]{1,0:T(8,128)(2,1)S(1)} %slice.68), channel_id=1, source_target_pairs={{0,8},{8,16},{16,24},{24,28},{28,20},{20,12},{12,4},{4,0},{1,9},{9... | collective-permute-start | bytes 589832 | tf_op jit(solution)/shard_map/ppermute | solution.py:139
  43.8 6.2 %collective-permute-start.7 = (bf16[64,1536]{1,0:T(8,128)(2,1)S(1)}, bf16[64,1536]{1,0:T(8,128)(2,1)S(1)}, u32[]{:S(2)}, u32[]{:S(2)}) collective-permute-start(bf16[64,1536]{1,0:T(8,128)(2,1)S(1)} %slice.69), channel_id=1, source_target_pairs={{8,0},{16,8},{24,16},{28,24},{20,28},{12,20},{4,12},{0,4},{9,1},{1... | collective-permute-start | bytes 589832 | tf_op jit(solution)/shard_map/ppermute | solution.py:139
  58.6 12.8 %copy-start.63 = (s32[8]{0:T(128)S(1)}, s32[8]{0:T(128)}, u32[]{:S(2)}) copy-start(s32[8]{0:T(128)} %copy-done.62) | copy-start | bytes 100
  71.5 15.6 %copy-start.15 = (bf16[2048,512]{1,0:T(8,128)(2,1)}, bf16[2048,512]{1,0:T(8,128)(2,1)S(1)}, u32[]{:S(2)}) copy-start(bf16[2048,512]{1,0:T(8,128)(2,1)S(1)} %get-tuple-element.115.refs_1_) | copy-start | bytes 6291460
  71.5 15.6 %copy-start.17 = (bf16[2048,512]{1,0:T(8,128)(2,1)}, bf16[2048,512]{1,0:T(8,128)(2,1)S(1)}, u32[]{:S(2)}) copy-start(bf16[2048,512]{1,0:T(8,128)(2,1)S(1)} %get-tuple-element.117.refs_3_) | copy-start | bytes 6291460
  71.5 15.6 %copy-start.30 = (bf16[2048,256]{1,0:T(8,128)(2,1)}, bf16[2048,256]{1,0:T(8,128)(2,1)S(1)}, u32[]{:S(2)}) copy-start(bf16[2048,256]{1,0:T(8,128)(2,1)S(1)} %get-tuple-element.116.refs_2_) | copy-start | bytes 3145732
  82.6 2.7 collective-permute-start.8
  85.5 27.2 %copy-start.7 = (bf16[512,1024]{1,0:T(8,128)(2,1)}, bf16[512,1024]{1,0:T(8,128)(2,1)S(1)}, u32[]{:S(2)}) copy-start(bf16[512,1024]{1,0:T(8,128)(2,1)S(1)} %shard_map.378.refs_6_.refs_2_.refs_0_) | copy-start | bytes 3145732
  85.5 10.6 %copy-start.44 = (f32[1024,8]{0,1:T(8,128)S(1)}, f32[1024,8]{0,1:T(8,128)}, u32[]{:S(2)}) copy-start(f32[1024,8]{0,1:T(8,128)} %param.40) | copy-start | bytes 98308
  85.5 25.3 %collective-permute-start.9 = (bf16[512,1024]{1,0:T(8,128)(2,1)S(1)}, bf16[512,1024]{1,0:T(8,128)(2,1)S(1)}, u32[]{:S(2)}, u32[]{:S(2)}) collective-permute-start(bf16[512,1024]{1,0:T(8,128)(2,1)S(1)} %shard_map.378.refs_6_.refs_2_.refs_0_), channel_id=1, source_target_pairs={{0,2},{1,3},{2,0},{3,1},{4,6},{5,7},{6,4},{7,5},{8,10},{9,11},{10,... | collective-permute-start | bytes 3145736 | tf_op jit(solution)/shard_map/ppermute | solution.py:926
  96.2 14.6 %copy-start.11 = (bf16[1024,512]{1,0:T(8,128)(2,1)}, bf16[1024,512]{1,0:T(8,128)(2,1)S(1)}, u32[]{:S(2)}) copy-start(bf16[1024,512]{1,0:T(8,128)(2,1)S(1)} %get-tuple-element.122.refs_0_.refs_8_) | copy-start | bytes 3145732
  112.6 3.9 %collective-permute-start.10 = (bf16[512,1024]{1,0:T(8,128)(2,1)S(1)}, bf16[512,1024]{1,0:T(8,128)(2,1)S(1)}, u32[]{:S(2)}, u32[]{:S(2)}) collective-permute-start(bf16[512,1024]{1,0:T(8,128)(2,1)S(1)} %get-tuple-element.125), channel_id=1, source_target_pairs={{0,1},{1,0},{2,3},{3,2},{4,5},{5,4},{6,7},{7,6},{8,9},{9,8},{10,11... | collective-permute-start | bytes 3145736 | tf_op jit(solution)/shard_map/ppermute | solution.py:908
  116.1 3.1 collective-permute-start.12
  117.6 32.5 %collective-permute-start.11 = (bf16[512,1024]{1,0:T(8,128)(2,1)}, bf16[512,1024]{1,0:T(8,128)(2,1)}, u32[]{:S(2)}, u32[]{:S(2)}) collective-permute-start(bf16[512,1024]{1,0:T(8,128)(2,1)} %shard_map.383.refs_5_.refs_2_.refs_0_), channel_id=1, source_target_pairs={{0,2},{1,3},{2,0},{3,1},{4,6},{5,7},{6,4},{7,5},{8,10},{9,11},{10,... | collective-permute-start | bytes 3145736 | tf_op jit(solution)/shard_map/ppermute | solution.py:926
  131.3 10.7 %copy-start.1 = (bf16[1024,2304]{1,0:T(8,128)(2,1)S(1)}, bf16[1024,2304]{1,0:T(8,128)(2,1)}, u32[]{:S(2)}) copy-start(bf16[1024,2304]{1,0:T(8,128)(2,1)} %all-gather.2.cloned.1.call-done.refs_4_.refs_1_) | copy-start | bytes 14155780
  146.2 7.0 %collective-permute-start.14 = (bf16[512,1024]{1,0:T(8,128)(2,1)S(1)}, bf16[512,1024]{1,0:T(8,128)(2,1)S(1)}, u32[]{:S(2)}, u32[]{:S(2)}) collective-permute-start(bf16[512,1024]{1,0:T(8,128)(2,1)S(1)} %get-tuple-element.129.refs_2_), channel_id=1, source_target_pairs={{0,1},{1,0},{2,3},{3,2},{4,5},{5,4},{6,7},{7,6},{8,9},{9,8},{10,11... | collective-permute-start | bytes 3145736 | tf_op jit(solution)/shard_map/ppermute | solution.py:908
  152.6 2.8 collective-permute-start.13
  153.6 25.5 %collective-permute-start.15 = (bf16[512,1024]{1,0:T(8,128)(2,1)S(1)}, bf16[512,1024]{1,0:T(8,128)(2,1)S(1)}, u32[]{:S(2)}, u32[]{:S(2)}) collective-permute-start(bf16[512,1024]{1,0:T(8,128)(2,1)S(1)} %shard_map.390.refs_5_.refs_2_), channel_id=1, source_target_pairs={{0,2},{1,3},{2,0},{3,1},{4,6},{5,7},{6,4},{7,5},{8,10},{9,11},{10,... | collective-permute-start | bytes 3145736 | tf_op jit(solution)/shard_map/ppermute | solution.py:926
  183.3 3.4 collective-permute-start.16
  183.3 18.7 %collective-permute-start.21 = (bf16[512,1024]{1,0:T(8,128)(2,1)S(1)}, bf16[512,1024]{1,0:T(8,128)(2,1)S(1)}, u32[]{:S(2)}, u32[]{:S(2)}) collective-permute-start(bf16[512,1024]{1,0:T(8,128)(2,1)S(1)} %get-tuple-element.130.refs_5_), channel_id=1, source_target_pairs={{0,1},{1,0},{2,3},{3,2},{4,5},{5,4},{6,7},{7,6},{8,9},{9,8},{10,11... | collective-permute-start | bytes 3145736 | tf_op jit(solution)/shard_map/ppermute | solution.py:908
  186.5 30.5 %copy-start.36 = (bf16[512,1024]{1,0:T(8,128)(2,1)}, bf16[512,1024]{1,0:T(8,128)(2,1)S(1)}, u32[]{:S(2)}) copy-start(bf16[512,1024]{1,0:T(8,128)(2,1)S(1)} %get-tuple-element.153.refs_15_.refs_6_) | copy-start | bytes 3145732
  186.5 30.5 %collective-permute-start.20 = (bf16[512,1024]{1,0:T(8,128)(2,1)S(1)}, bf16[512,1024]{1,0:T(8,128)(2,1)S(1)}, u32[]{:S(2)}, u32[]{:S(2)}) collective-permute-start(bf16[512,1024]{1,0:T(8,128)(2,1)S(1)} %get-tuple-element.153.refs_15_.refs_6_), channel_id=1, source_target_pairs={{0,1},{1,0},{2,3},{3,2},{4,5},{5,4},{6,7},{7,6},{8,9},{9,8},{10,11... | collective-permute-start | bytes 3145736 | tf_op jit(solution)/shard_map/ppermute | solution.py:908
  186.9 26.0 %collective-permute-start.18 = (bf16[512,1024]{1,0:T(8,128)(2,1)S(1)}, bf16[512,1024]{1,0:T(8,128)(2,1)S(1)}, u32[]{:S(2)}, u32[]{:S(2)}) collective-permute-start(bf16[512,1024]{1,0:T(8,128)(2,1)S(1)} %shard_map.394.refs_7_.refs_2_), channel_id=1, source_target_pairs={{0,2},{1,3},{2,0},{3,1},{4,6},{5,7},{6,4},{7,5},{8,10},{9,11},{10,... | collective-permute-start | bytes 3145736 | tf_op jit(solution)/shard_map/ppermute | solution.py:926
  188.8 13.3 %copy-start.23 = (f32[512,1024]{1,0:T(8,128)S(1)}, f32[512,1024]{1,0:T(8,128)}, u32[]{:S(2)}) copy-start(f32[512,1024]{1,0:T(8,128)} %get-tuple-element.160.refs_0_) | copy-start | bytes 6291460
  202.3 32.7 %collective-permute-start.22 = (bf16[512,1024]{1,0:T(8,128)(2,1)S(1)}, bf16[512,1024]{1,0:T(8,128)(2,1)}, u32[]{:S(2)}, u32[]{:S(2)}) collective-permute-start(bf16[512,1024]{1,0:T(8,128)(2,1)S(1)} %shard_map.400.refs_2_), channel_id=1, source_target_pairs={{0,2},{1,3},{2,0},{3,1},{4,6},{5,7},{6,4},{7,5},{8,10},{9,11},{10,... | collective-permute-start | bytes 3145736 | tf_op jit(solution)/shard_map/ppermute | solution.py:926
  217.0 17.6 %copy-start.38 = (bf16[512,1024]{1,0:T(8,128)(2,1)}, bf16[512,1024]{1,0:T(8,128)(2,1)S(1)}, u32[]{:S(2)}) copy-start(bf16[512,1024]{1,0:T(8,128)(2,1)S(1)} %collective-permute-done.20.refs_14_.refs_5_) | copy-start | bytes 3145732
  217.0 18.0 %copy-start.6 = (bf16[512,1024]{1,0:T(8,128)(2,1)S(1)}, bf16[512,1024]{1,0:T(8,128)(2,1)}, u32[]{:S(2)}) copy-start(bf16[512,1024]{1,0:T(8,128)(2,1)} %copy-done.5) | copy-start | bytes 3145732
  217.0 18.0 %copy-start.8 = (bf16[512,1024]{1,0:T(8,128)(2,1)S(1)}, bf16[512,1024]{1,0:T(8,128)(2,1)}, u32[]{:S(2)}) copy-start(bf16[512,1024]{1,0:T(8,128)(2,1)} %copy-done.7) | copy-start | bytes 3145732
  236.7 11.7 %copy-start.59 = (f32[512,8]{0,1:T(8,128)S(1)}, f32[512,8]{0,1:T(8,128)}, u32[]{:S(2)}) copy-start(f32[512,8]{0,1:T(8,128)} %param.41) | copy-start | bytes 49156
  243.8 2.7 collective-permute-start.23
  243.9 4.5 %collective-permute-start.19 = (bf16[512,1024]{1,0:T(8,128)(2,1)S(1)}, bf16[512,1024]{1,0:T(8,128)(2,1)S(1)}, u32[]{:S(2)}, u32[]{:S(2)}) collective-permute-start(bf16[512,1024]{1,0:T(8,128)(2,1)S(1)} %get-tuple-element.150.refs_16_.refs_8_.refs_15_), channel_id=1, source_target_pairs={{0,1},{1,0},{2,3},{3,2},{4,5},{5,4},{6,7},{7,6},{8,9},{9,8},{10,11... | collective-permute-start | bytes 3145736 | tf_op jit(solution)/shard_map/ppermute | solution.py:908
  246.9 25.3 %collective-permute-start.24 = (bf16[512,1024]{1,0:T(8,128)(2,1)S(1)}, bf16[512,1024]{1,0:T(8,128)(2,1)S(1)}, u32[]{:S(2)}, u32[]{:S(2)}) collective-permute-start(bf16[512,1024]{1,0:T(8,128)(2,1)S(1)} %shard_map.403.refs_9_.refs_2_), channel_id=1, source_target_pairs={{0,2},{1,3},{2,0},{3,1},{4,6},{5,7},{6,4},{7,5},{8,10},{9,11},{10,... | collective-permute-start | bytes 3145736 | tf_op jit(solution)/shard_map/ppermute | solution.py:926
  279.8 5.5 %collective-permute-start.25 = (bf16[512,1024]{1,0:T(8,128)(2,1)S(1)}, bf16[512,1024]{1,0:T(8,128)(2,1)S(1)}, u32[]{:S(2)}, u32[]{:S(2)}) collective-permute-start(bf16[512,1024]{1,0:T(8,128)(2,1)S(1)} %get-tuple-element.168), channel_id=1, source_target_pairs={{0,1},{1,0},{2,3},{3,2},{4,5},{5,4},{6,7},{7,6},{8,9},{9,8},{10,11... | collective-permute-start | bytes 3145736 | tf_op jit(solution)/shard_map/ppermute | solution.py:908
  279.9 20.5 %collective-permute-start.17 = (bf16[512,1024]{1,0:T(8,128)(2,1)S(1)}, bf16[512,1024]{1,0:T(8,128)(2,1)S(1)}, u32[]{:S(2)}, u32[]{:S(2)}) collective-permute-start(bf16[512,1024]{1,0:T(8,128)(2,1)S(1)} %copy-done.35), channel_id=1, source_target_pairs={{0,1},{1,0},{2,3},{3,2},{4,5},{5,4},{6,7},{7,6},{8,9},{9,8},{10,11... | collective-permute-start | bytes 3145736 | tf_op jit(solution)/shard_map/ppermute | solution.py:908
  280.4 22.5 %collective-permute-start.30 = (bf16[512,1024]{1,0:T(8,128)(2,1)S(1)}, bf16[512,1024]{1,0:T(8,128)(2,1)S(1)}, u32[]{:S(2)}, u32[]{:S(2)}) collective-permute-start(bf16[512,1024]{1,0:T(8,128)(2,1)S(1)} %shard_map.401.refs_10_.refs_3_), channel_id=1, source_target_pairs={{0,1},{1,0},{2,3},{3,2},{4,5},{5,4},{6,7},{7,6},{8,9},{9,8},{10,11... | collective-permute-start | bytes 3145736 | tf_op jit(solution)/shard_map/ppermute | solution.py:908
  281.7 8.8 %collective-permute-start.27 = (f32[8,4096]{1,0:T(8,128)S(1)}, f32[8,4096]{1,0:T(8,128)S(1)}, u32[]{:S(2)}, u32[]{:S(2)}) collective-permute-start(f32[8,4096]{1,0:T(8,128)S(1)} %pad_maximum_fusion.4.refs_0_), channel_id=1, source_target_pairs={{0,4},{4,0},{8,12},{12,8},{16,20},{20,16},{24,28},{28,24},{1,5},{5... | collective-permute-start | bytes 393224 | tf_op jit(solution)/shard_map/ppermute | solution.py:900
  285.5 31.4 %collective-permute-start.31 = (bf16[512,1024]{1,0:T(8,128)(2,1)S(1)}, bf16[512,1024]{1,0:T(8,128)(2,1)S(1)}, u32[]{:S(2)}, u32[]{:S(2)}) collective-permute-start(bf16[512,1024]{1,0:T(8,128)(2,1)S(1)} %shard_map.407.refs_2_.refs_6_), channel_id=1, source_target_pairs={{0,2},{1,3},{2,0},{3,1},{4,6},{5,7},{6,4},{7,5},{8,10},{9,11},{10,... | collective-permute-start | bytes 3145736 | tf_op jit(solution)/shard_map/ppermute | solution.py:926
  290.5 8.3 %collective-permute-start.28 = (f32[8,4096]{1,0:T(8,128)S(1)}, f32[8,4096]{1,0:T(8,128)S(1)}, u32[]{:S(2)}, u32[]{:S(2)}) collective-permute-start(f32[8,4096]{1,0:T(8,128)S(1)} %shard_map.411.refs_7_.refs_0_), channel_id=1, source_target_pairs={{0,8},{4,12},{8,0},{12,4},{16,24},{20,28},{24,16},{28,20},{1,9},{5... | collective-permute-start | bytes 393224 | tf_op jit(solution)/shard_map/ppermute | solution.py:900
  298.8 16.5 %copy-start.2 = (f32[1024,1024]{1,0:T(8,128)}, f32[1024,1024]{1,0:T(8,128)S(1)}, u32[]{:S(2)}) copy-start(f32[1024,1024]{1,0:T(8,128)S(1)} %get-tuple-element.182.refs_1_.refs_0_) | copy-start | bytes 12582916
  298.9 8.8 %collective-permute-start.29 = (f32[8,4096]{1,0:T(8,128)S(1)}, f32[8,4096]{1,0:T(8,128)S(1)}, u32[]{:S(2)}, u32[]{:S(2)}) collective-permute-start(f32[8,4096]{1,0:T(8,128)S(1)} %shard_map.413.refs_4_.refs_0_), channel_id=1, source_target_pairs={{0,16},{4,20},{8,24},{12,28},{16,0},{20,4},{24,8},{28,12},{1,17},{... | collective-permute-start | bytes 393224 | tf_op jit(solution)/shard_map/ppermute | solution.py:900
  300.4 21.2 %collective-permute-start.33 = (bf16[512,1024]{1,0:T(8,128)(2,1)}, bf16[512,1024]{1,0:T(8,128)(2,1)}, u32[]{:S(2)}, u32[]{:S(2)}) collective-permute-start(bf16[512,1024]{1,0:T(8,128)(2,1)} %get-tuple-element.172.refs_2_.refs_3_), channel_id=1, source_target_pairs={{0,1},{1,0},{2,3},{3,2},{4,5},{5,4},{6,7},{7,6},{8,9},{9,8},{10,11... | collective-permute-start | bytes 3145736 | tf_op jit(solution)/shard_map/ppermute | solution.py:908
  300.5 11.2 %slice-start = ((s8[6291456]{0:T(1024)(128)(4,1)}), s8[4194304]{0:T(1024)(128)(4,1)S(1)}, s32[]{:S(2)}) async-start(s8[6291456]{0:T(1024)(128)(4,1)} %bitcast.65), calls=%async_computation.1 | async-start | bytes 8388608
  301.6 31.8 %collective-permute-start.26 = (bf16[512,1024]{1,0:T(8,128)(2,1)}, bf16[512,1024]{1,0:T(8,128)(2,1)}, u32[]{:S(2)}, u32[]{:S(2)}) collective-permute-start(bf16[512,1024]{1,0:T(8,128)(2,1)} %shard_map.408.refs_2_), channel_id=1, source_target_pairs={{0,2},{1,3},{2,0},{3,1},{4,6},{5,7},{6,4},{7,5},{8,10},{9,11},{10,... | collective-permute-start | bytes 3145736 | tf_op jit(solution)/shard_map/ppermute | solution.py:926
  320.2 18.2 %collective-permute-start.35 = (bf16[512,1024]{1,0:T(8,128)(2,1)}, bf16[512,1024]{1,0:T(8,128)(2,1)}, u32[]{:S(2)}, u32[]{:S(2)}) collective-permute-start(bf16[512,1024]{1,0:T(8,128)(2,1)} %get-tuple-element.193.refs_3_), channel_id=1, source_target_pairs={{0,1},{1,0},{2,3},{3,2},{4,5},{5,4},{6,7},{7,6},{8,9},{9,8},{10,11... | collective-permute-start | bytes 3145736 | tf_op jit(solution)/shard_map/ppermute | solution.py:908
  320.3 6.8 %collective-permute-start.32 = (f32[8,4128]{1,0:T(8,128)S(1)}, f32[8,4128]{1,0:T(8,128)S(1)}, u32[]{:S(2)}, u32[]{:S(2)}) collective-permute-start(f32[8,4128]{1,0:T(8,128)S(1)} %constant_dynamic-update-slice_fusion.refs_0_), channel_id=1, source_target_pairs={{0,4},{4,0},{8,12},{12,8},{16,20},{20,16},{24,28},{28,24},{1,5},{5... | collective-permute-start | bytes 396296 | tf_op jit(solution)/shard_map/ppermute | solution.py:900
  327.2 9.4 %collective-permute-start.36 = (f32[8,4128]{1,0:T(8,128)S(1)}, f32[8,4128]{1,0:T(8,128)S(1)}, u32[]{:S(2)}, u32[]{:S(2)}) collective-permute-start(f32[8,4128]{1,0:T(8,128)S(1)} %shard_map.422.refs_4_.refs_0_), channel_id=1, source_target_pairs={{0,8},{4,12},{8,0},{12,4},{16,24},{20,28},{24,16},{28,20},{1,9},{5... | collective-permute-start | bytes 396296 | tf_op jit(solution)/shard_map/ppermute | solution.py:900
  327.9 10.5 %copy-start.56 = (f32[8,1024]{1,0:T(8,128)S(1)}, f32[8,1024]{1,0:T(8,128)}, u32[]{:S(2)}) copy-start(f32[8,1024]{1,0:T(8,128)} %copy-done.55) | copy-start | bytes 98308
  336.6 8.7 %collective-permute-start.37 = (f32[8,4128]{1,0:T(8,128)S(1)}, f32[8,4128]{1,0:T(8,128)S(1)}, u32[]{:S(2)}, u32[]{:S(2)}) collective-permute-start(f32[8,4128]{1,0:T(8,128)S(1)} %shard_map.425.refs_5_.refs_0_), channel_id=1, source_target_pairs={{0,16},{4,20},{8,24},{12,28},{16,0},{20,4},{24,8},{28,12},{1,17},{... | collective-permute-start | bytes 396296 | tf_op jit(solution)/shard_map/ppermute | solution.py:900
  338.4 24.9 %collective-permute-start.34 = (bf16[512,1024]{1,0:T(8,128)(2,1)}, bf16[512,1024]{1,0:T(8,128)(2,1)}, u32[]{:S(2)}, u32[]{:S(2)}) collective-permute-start(bf16[512,1024]{1,0:T(8,128)(2,1)} %shard_map.423.refs_3_.refs_2_), channel_id=1, source_target_pairs={{0,1},{1,0},{2,3},{3,2},{4,5},{5,4},{6,7},{7,6},{8,9},{9,8},{10,11... | collective-permute-start | bytes 3145736 | tf_op jit(solution)/shard_map/ppermute | solution.py:908
  345.3 12.9 %copy-start.43 = (f32[128,1536]{1,0:T(8,128)S(1)}, f32[128,1536]{1,0:T(8,128)}, u32[]{:S(2)}) copy-start(f32[128,1536]{1,0:T(8,128)} %refs_4_.6) | copy-start | bytes 2359300
  346.0 10.6 %collective-permute-start.38 = (f32[8,288]{1,0:T(8,128)S(1)}, f32[8,288]{1,0:T(8,128)S(1)}, u32[]{:S(2)}, u32[]{:S(2)}) collective-permute-start(f32[8,288]{1,0:T(8,128)S(1)} %slice.78.refs_0_), channel_id=1, source_target_pairs={{0,1},{1,0},{2,3},{3,2},{4,5},{5,4},{6,7},{7,6},{8,9},{9,8},{10,11... | collective-permute-start | bytes 27656 | tf_op jit(solution)/shard_map/ppermute | solution.py:900
  346.0 12.2 %slice-start.2 = ((s8[6291456]{0:T(1024)(128)(4,1)}), s8[4194304]{0:T(1024)(128)(4,1)S(1)}, s32[]{:S(2)}) async-start(s8[6291456]{0:T(1024)(128)(4,1)} %bitcast.67), calls=%async_computation.3 | async-start | bytes 8388608
  356.6 5.9 %collective-permute-start.39 = (f32[8,288]{1,0:T(8,128)S(1)}, f32[8,288]{1,0:T(8,128)S(1)}, u32[]{:S(2)}, u32[]{:S(2)}) collective-permute-start(f32[8,288]{1,0:T(8,128)S(1)} %shard_map.432.refs_0_), channel_id=1, source_target_pairs={{0,2},{1,3},{2,0},{3,1},{4,6},{5,7},{6,4},{7,5},{8,10},{9,11},{10,... | collective-permute-start | bytes 27656 | tf_op jit(solution)/shard_map/ppermute | solution.py:900
  (69 other events, 302.4 us)
Sparse Core Ops, SparseCore 0:
  51.1 80.1 all-gather.1
